TPU v7x, 512 devices: a whole 4x4x16 slice. The times are simulated.
512 devices in a mesh: rows: 64 (over z, x), inner: 8 (over y, core).
Axes of the slice: x: 4, y: 4, z: 16, core: 2. Of those that a mesh axis runs over, the one named last changes fastest.
Arguments:
- blocks: bfloat16 [64, 16, 256, 256], P('rows'), may hold values from -0.375 to 0.375
- columns: int32 [64, 16], replicated, may hold values from -1 to 63, as said below
Outputs:
- purified: float32 [64, 16, 256, 256], P('rows', None, 'inner')
Inputs may be any that keep to these rules, and one draw needn't show every extreme that they name: Each entry of row i that is not -1 is (i + d) mod 64 for an offset d with -16 <= 2 * d < 16; the entries of a row are distinct and stand before its -1 entries; every row lists its diagonal block; some row lists 16 columns.
All inputs are finite; a program needn't handle non-finite values.
Results may differ from a plain program's by a relative error of at most 0.0055.
Values may be sent and summed in bfloat16 or wider, within the bound.
No kernel may reach another device: no remote copies, remote signals or barrier semaphores. Data moves between devices by JAX's collectives and lax.ppermute only.
A program may use at most 128 MiB of HBM per device.

v0:
```python
import jax
import jax.numpy as jnp
from jax import lax
from jax.sharding import PartitionSpec as P


def from_behind(value, axis, steps):
    count = lax.axis_size(axis)
    pairs = [(source, (source + steps) % count) for source in range(count)]
    return lax.ppermute(value, axis, pairs)


def in_blocks(shard, dim, devices):
    shape = shard.shape
    parts = shard.reshape(*shape[:dim], devices, shape[dim] // devices, *shape[dim + 1 :])
    return jnp.moveaxis(parts, dim, 0)


def sum_at_owner(shard, axis, dim):
    devices = lax.axis_size(axis)
    parts = lax.all_to_all(in_blocks(shard, dim, devices), axis, 0, 0, tiled=True)
    return jnp.sum(parts.astype(jnp.float32), axis=0)


def live_table(columns):
    nrows, band_width = columns.shape
    half_band = band_width // 2
    row_ids = jnp.arange(nrows, dtype=jnp.int32)
    target = (
        row_ids[:, None] + jnp.arange(band_width, dtype=jnp.int32)[None, :] - half_band
    ) % nrows
    return jnp.any(columns[:, None, :] == target[:, :, None], axis=2)


def slot_shift(piece, delta):
    band_width = piece.shape[1]
    if delta >= 0:
        return jnp.concatenate([piece[:, delta:], jnp.zeros_like(piece[:, :delta])], axis=1)
    return jnp.concatenate(
        [jnp.zeros_like(piece[:, :-delta]), piece[:, : band_width + delta]], axis=1
    )


def fetch_band(row_slab, below, above, block_rows, second):
    band_width = row_slab.shape[1]
    pieces = []
    for offset in range(-below, above + 1):
        if offset == 0:
            pieces.append(row_slab)
            continue
        trimmed = (abs(offset) - 1) * block_rows + 1
        if offset > 0:
            outgoing = row_slab[:, : band_width - trimmed]
        else:
            outgoing = row_slab[:, trimmed:]
        if second:
            incoming = from_behind(outgoing, "rows", -offset)
        else:
            incoming = from_behind(outgoing, "rows", -offset)
        filler = jnp.zeros_like(row_slab[:, :trimmed])
        if offset > 0:
            pieces.append(jnp.concatenate([incoming, filler], axis=1))
        else:
            pieces.append(jnp.concatenate([filler, incoming], axis=1))
    return jnp.concatenate(pieces, axis=0)


def merge_groups(totals):
    return totals[0]


def dense_terms(left, window, window_base, groups):
    block_rows, band_width, block_size, inner_width = left.shape
    out_width = window.shape[3]
    half_band = band_width // 2
    group_width = inner_width // groups
    stacked = jnp.stack(
        [
            slot_shift(
                window[window_base + offset : window_base + offset + block_rows], half_band - offset
            )
            for offset in range(band_width)
        ],
        axis=1,
    )
    left_groups = left.reshape(block_rows, band_width, block_size, groups, group_width)
    right_groups = stacked.reshape(
        block_rows, band_width, band_width, groups, group_width, out_width
    )
    totals = jnp.einsum(
        "ramcq,rascqn->crsmn", left_groups, right_groups, preferred_element_type=jnp.float32
    )
    return merge_groups(totals)


def band_terms(left, window, window_base, groups):
    return dense_terms(left, window, window_base, groups)


def per_device(blocks, columns):
    block_rows, band_width, block_size, _ = blocks.shape
    half_band = band_width // 2
    inner_count = lax.axis_size("inner")
    slab_width = block_size // inner_count
    inner_index = lax.axis_index("inner")
    row_owner = lax.axis_index("rows")
    live_own = lax.dynamic_slice_in_dim(live_table(columns), row_owner * block_rows, block_rows, 0)
    live_slots = live_own[:, :, None, None]
    masked = jnp.where(live_slots, blocks, jnp.zeros_like(blocks))
    below = -(-half_band // block_rows)
    above = -(-(half_band - 1) // block_rows)
    window_base = below * block_rows - half_band
    left = lax.dynamic_slice_in_dim(masked, inner_index * slab_width, slab_width, 3)
    row_slab = lax.dynamic_slice_in_dim(masked, inner_index * slab_width, slab_width, 2)
    window = fetch_band(row_slab, below, above, block_rows, False)
    square_terms = band_terms(left, window, window_base, 1)
    square = sum_at_owner(square_terms.astype(jnp.bfloat16), "inner", 2)
    square = jnp.where(live_slots, square, jnp.float32(0.0)).astype(jnp.bfloat16)
    second_window = fetch_band(square, below, above, block_rows, True)
    cube_terms = band_terms(left, second_window, window_base, 1)
    cubed = sum_at_owner(cube_terms.astype(jnp.bfloat16), "inner", 2)
    cubed = jnp.where(live_slots, cubed, jnp.float32(0.0))
    return 3.0 * square.astype(jnp.float32) - 2.0 * cubed


def solution(mesh):
    in_specs = (P("rows", None, None, None), P())
    out_specs = P("rows", None, "inner", None)
    return jax.shard_map(
        per_device, mesh=mesh, in_specs=in_specs, out_specs=out_specs, check_vma=False
    )
```

profile of v0, /device:TPU:1, one launch (start us, length us, event | category | flops | bytes accessed | tf_op | source)
XLA Modules:
  0.0 234.3 jit_solution(15636510658044663967)
XLA Ops:
  0.0 0.7 compare_reduce_fusion
  0.8 0.2 dynamic-slice_reduce_fusion
  0.9 1.8 broadcast_select_fusion
  2.8 0.8 constant_dynamic-slice_fusion
  3.5 6.6 %collective-permute-start.1 = (bf16[1,9,32,256]{3,2,1,0:T(8,128)(2,1)}, bf16[1,9,32,256]{3,2,1,0:T(8,128)(2,1)}, u32[]{:S(2)}, u32[]{:S(2)}) collective-permute-start(bf16[1,9,32,256]{3,2,1,0:T(8,128)(2,1)} %get-tuple-element.6), channel_id=1, source_target_pairs={{0,56},{8,64},{16,72},{24,80},{32,88},{40,96},{48,104},{56,112},{6... | collective-permute-start | bytes 442376 | tf_op jit(solution)/shard_map/ppermute | solution.py:10
  10.1 0.7 constant_dynamic-slice_fusion.14
  10.7 4.9 %collective-permute-start = (bf16[1,8,32,256]{3,2,1,0:T(8,128)(2,1)}, bf16[1,8,32,256]{3,2,1,0:T(8,128)(2,1)}, u32[]{:S(2)}, u32[]{:S(2)}) collective-permute-start(bf16[1,8,32,256]{3,2,1,0:T(8,128)(2,1)} %constant_dynamic-slice_fusion.14), channel_id=1, source_target_pairs={{0,64},{8,72},{16,80},{24,88},{32,96},{40,104},{48,112},{56,120},{... | collective-permute-start | bytes 393224 | tf_op jit(solution)/shard_map/ppermute | solution.py:10
  15.6 0.8 constant_dynamic-slice_fusion.1
  16.4 6.3 %collective-permute-start.2 = (bf16[1,10,32,256]{3,2,1,0:T(8,128)(2,1)}, bf16[1,10,32,256]{3,2,1,0:T(8,128)(2,1)}, u32[]{:S(2)}, u32[]{:S(2)}) collective-permute-start(bf16[1,10,32,256]{3,2,1,0:T(8,128)(2,1)} %get-tuple-element.8), channel_id=1, source_target_pairs={{0,48},{8,56},{16,64},{24,72},{32,80},{40,88},{48,96},{56,104},{64... | collective-permute-start | bytes 491528 | tf_op jit(solution)/shard_map/ppermute | solution.py:10
  22.7 0.8 constant_dynamic-slice_fusion.2
  23.5 3.9 %collective-permute-start.3 = (bf16[1,11,32,256]{3,2,1,0:T(8,128)(2,1)}, bf16[1,11,32,256]{3,2,1,0:T(8,128)(2,1)}, u32[]{:S(2)}, u32[]{:S(2)}) collective-permute-start(bf16[1,11,32,256]{3,2,1,0:T(8,128)(2,1)} %get-tuple-element.10), channel_id=1, source_target_pairs={{0,40},{8,48},{16,56},{24,64},{32,72},{40,80},{48,88},{56,96},{64,... | collective-permute-start | bytes 540680 | tf_op jit(solution)/shard_map/ppermute | solution.py:10
  27.4 0.7 constant_dynamic-slice_fusion.3
  28.1 3.5 %collective-permute-start.4 = (bf16[1,12,32,256]{3,2,1,0:T(8,128)(2,1)}, bf16[1,12,32,256]{3,2,1,0:T(8,128)(2,1)S(1)}, u32[]{:S(2)}, u32[]{:S(2)}) collective-permute-start(bf16[1,12,32,256]{3,2,1,0:T(8,128)(2,1)} %get-tuple-element.12), channel_id=1, source_target_pairs={{0,32},{8,40},{16,48},{24,56},{32,64},{40,72},{48,80},{56,88},{64,... | collective-permute-start | bytes 589832 | tf_op jit(solution)/shard_map/ppermute | solution.py:10
  31.8 0.0 collective-permute-done
  31.8 6.7 %collective-permute-start.5 = (bf16[1,13,32,256]{3,2,1,0:T(8,128)(2,1)S(1)}, bf16[1,13,32,256]{3,2,1,0:T(8,128)(2,1)S(1)}, u32[]{:S(2)}, u32[]{:S(2)}) collective-permute-start(bf16[1,13,32,256]{3,2,1,0:T(8,128)(2,1)S(1)} %get-tuple-element.14), channel_id=1, source_target_pairs={{0,24},{8,32},{16,40},{24,48},{32,56},{40,64},{48,72},{56,80},{64,... | collective-permute-start | bytes 638984 | tf_op jit(solution)/shard_map/ppermute | solution.py:10
  38.5 0.9 bitcast_dynamic-update-slice_fusion.27
  39.4 3.1 %collective-permute-start.6 = (bf16[1,14,32,256]{3,2,1,0:T(8,128)(2,1)S(1)}, bf16[1,14,32,256]{3,2,1,0:T(8,128)(2,1)S(1)}, u32[]{:S(2)}, u32[]{:S(2)}) collective-permute-start(bf16[1,14,32,256]{3,2,1,0:T(8,128)(2,1)S(1)} %get-tuple-element.16), channel_id=1, source_target_pairs={{0,16},{8,24},{16,32},{24,40},{32,48},{40,56},{48,64},{56,72},{64,... | collective-permute-start | bytes 688136 | tf_op jit(solution)/shard_map/ppermute | solution.py:10
  42.6 0.9 bitcast_dynamic-update-slice_fusion.26
  43.5 1.9 collective-permute-start.7
  45.5 0.9 bitcast_dynamic-update-slice_fusion.25
  46.4 0.0 collective-permute-done.3
  46.4 6.7 %collective-permute-start.8 = (bf16[1,15,32,256]{3,2,1,0:T(8,128)(2,1)S(1)}, bf16[1,15,32,256]{3,2,1,0:T(8,128)(2,1)S(1)}, u32[]{:S(2)}, u32[]{:S(2)}) collective-permute-start(bf16[1,15,32,256]{3,2,1,0:T(8,128)(2,1)S(1)} %get-tuple-element.17), channel_id=1, source_target_pairs={{0,504},{8,0},{16,8},{24,16},{32,24},{40,32},{48,40},{56,48},{64,5... | collective-permute-start | bytes 737288 | tf_op jit(solution)/shard_map/ppermute | solution.py:10
  53.1 0.9 bitcast_dynamic-update-slice_fusion.24
  54.1 2.4 %collective-permute-start.9 = (bf16[1,14,32,256]{3,2,1,0:T(8,128)(2,1)S(1)}, bf16[1,14,32,256]{3,2,1,0:T(8,128)(2,1)S(1)}, u32[]{:S(2)}, u32[]{:S(2)}) collective-permute-start(bf16[1,14,32,256]{3,2,1,0:T(8,128)(2,1)S(1)} %get-tuple-element.15), channel_id=1, source_target_pairs={{0,496},{8,504},{16,0},{24,8},{32,16},{40,24},{48,32},{56,40},{64,... | collective-permute-start | bytes 688136 | tf_op jit(solution)/shard_map/ppermute | solution.py:10
  56.5 0.0 collective-permute-done.5
  56.5 1.9 collective-permute-start.10
  58.5 0.0 collective-permute-done.6
  58.5 1.9 collective-permute-start.11
  60.5 6.0 %collective-permute-done.7 = bf16[1,15,32,256]{3,2,1,0:T(8,128)(2,1)S(1)} collective-permute-done((bf16[1,15,32,256]{3,2,1,0:T(8,128)(2,1)S(1)}, bf16[1,15,32,256]{3,2,1,0:T(8,128)(2,1)S(1)}, u32[]{:S(2)}, u32[]{:S(2)}) %collective-permute-start.7) | collective-permute-done | bytes 245792 | tf_op jit(solution)/shard_map/ppermute | solution.py:10
  66.4 2.2 collective-permute-start.12
  68.7 3.2 %collective-permute-start.13 = (bf16[1,10,32,256]{3,2,1,0:T(8,128)(2,1)S(1)}, bf16[1,10,32,256]{3,2,1,0:T(8,128)(2,1)S(1)}, u32[]{:S(2)}, u32[]{:S(2)}) collective-permute-start(bf16[1,10,32,256]{3,2,1,0:T(8,128)(2,1)S(1)} %copy-done), channel_id=1, source_target_pairs={{0,464},{8,472},{16,480},{24,488},{32,496},{40,504},{48,0},{56,8},... | collective-permute-start | bytes 491528 | tf_op jit(solution)/shard_map/ppermute | solution.py:10
  71.9 6.8 %collective-permute-start.14 = (bf16[1,9,32,256]{3,2,1,0:T(8,128)(2,1)S(1)}, bf16[1,9,32,256]{3,2,1,0:T(8,128)(2,1)S(1)}, u32[]{:S(2)}, u32[]{:S(2)}) collective-permute-start(bf16[1,9,32,256]{3,2,1,0:T(8,128)(2,1)S(1)} %copy-done.1), channel_id=1, source_target_pairs={{0,456},{8,464},{16,472},{24,480},{32,488},{40,496},{48,504},{56,0... | collective-permute-start | bytes 442376 | tf_op jit(solution)/shard_map/ppermute | solution.py:10
  78.9 9.7 %collective-permute-done.13 = bf16[1,10,32,256]{3,2,1,0:T(8,128)(2,1)S(1)} collective-permute-done((bf16[1,10,32,256]{3,2,1,0:T(8,128)(2,1)S(1)}, bf16[1,10,32,256]{3,2,1,0:T(8,128)(2,1)S(1)}, u32[]{:S(2)}, u32[]{:S(2)}) %collective-permute-start.13) | collective-permute-done | bytes 163872 | tf_op jit(solution)/shard_map/ppermute | solution.py:10
  88.6 3.1 %collective-permute-done.14 = bf16[1,9,32,256]{3,2,1,0:T(8,128)(2,1)S(1)} collective-permute-done((bf16[1,9,32,256]{3,2,1,0:T(8,128)(2,1)S(1)}, bf16[1,9,32,256]{3,2,1,0:T(8,128)(2,1)S(1)}, u32[]{:S(2)}, u32[]{:S(2)}) %collective-permute-start.14) | collective-permute-done | bytes 147488 | tf_op jit(solution)/shard_map/ppermute | solution.py:10
  91.8 1.9 bitcast_convert_fusion.1
  93.7 0.2 copy.136
  94.0 33.8 %all_to_all.10 = bf16[8,1,16,32,256]{4,3,2,1,0:T(8,128)(2,1)S(1)} all-to-all(bf16[8,1,16,32,256]{4,3,2,1,0:T(8,128)(2,1)S(1)} %bitcast.182), channel_id=1, replica_groups=mesh['rows'=64,'inner'=8] {'inner'}, dimensions={0} | all-to-all | bytes 4194304 | tf_op jit(solution)/shard_map/all_to_all | solution.py:21
  127.7 0.4 convert_reduce_fusion.1
  128.1 0.1 fusion.15
  128.5 1.9 collective-permute-start.15
  130.4 1.9 collective-permute-start.16
  132.4 1.9 collective-permute-start.17
  134.3 7.7 %collective-permute-start.18 = (bf16[1,11,32,256]{3,2,1,0:T(8,128)(2,1)S(1)}, bf16[1,11,32,256]{3,2,1,0:T(8,128)(2,1)S(1)}, u32[]{:S(2)}, u32[]{:S(2)}) collective-permute-start(bf16[1,11,32,256]{3,2,1,0:T(8,128)(2,1)S(1)} %get-tuple-element.24), channel_id=1, source_target_pairs={{0,40},{8,48},{16,56},{24,64},{32,72},{40,80},{48,88},{56,96},{64,... | collective-permute-start | bytes 540680 | tf_op jit(solution)/shard_map/ppermute | solution.py:10
  142.0 3.5 %collective-permute-start.19 = (bf16[1,12,32,256]{3,2,1,0:T(8,128)(2,1)S(1)}, bf16[1,12,32,256]{3,2,1,0:T(8,128)(2,1)S(1)}, u32[]{:S(2)}, u32[]{:S(2)}) collective-permute-start(bf16[1,12,32,256]{3,2,1,0:T(8,128)(2,1)S(1)} %get-tuple-element.26), channel_id=1, source_target_pairs={{0,32},{8,40},{16,48},{24,56},{32,64},{40,72},{48,80},{56,88},{64,... | collective-permute-start | bytes 589832 | tf_op jit(solution)/shard_map/ppermute | solution.py:10
  145.5 4.3 %collective-permute-start.20 = (bf16[1,13,32,256]{3,2,1,0:T(8,128)(2,1)S(1)}, bf16[1,13,32,256]{3,2,1,0:T(8,128)(2,1)S(1)}, u32[]{:S(2)}, u32[]{:S(2)}) collective-permute-start(bf16[1,13,32,256]{3,2,1,0:T(8,128)(2,1)S(1)} %get-tuple-element.28), channel_id=1, source_target_pairs={{0,24},{8,32},{16,40},{24,48},{32,56},{40,64},{48,72},{56,80},{64,... | collective-permute-start | bytes 638984 | tf_op jit(solution)/shard_map/ppermute | solution.py:10
  149.9 1.9 collective-permute-start.21
  151.8 2.5 %collective-permute-start.22 = (bf16[1,15,32,256]{3,2,1,0:T(8,128)(2,1)S(1)}, bf16[1,15,32,256]{3,2,1,0:T(8,128)(2,1)S(1)}, u32[]{:S(2)}, u32[]{:S(2)}) collective-permute-start(bf16[1,15,32,256]{3,2,1,0:T(8,128)(2,1)S(1)} %get-tuple-element.32), channel_id=1, source_target_pairs={{0,8},{8,16},{16,24},{24,32},{32,40},{40,48},{48,56},{56,64},{64,7... | collective-permute-start | bytes 737288 | tf_op jit(solution)/shard_map/ppermute | solution.py:10
  154.4 6.1 %collective-permute-start.23 = (bf16[1,15,32,256]{3,2,1,0:T(8,128)(2,1)S(1)}, bf16[1,15,32,256]{3,2,1,0:T(8,128)(2,1)S(1)}, u32[]{:S(2)}, u32[]{:S(2)}) collective-permute-start(bf16[1,15,32,256]{3,2,1,0:T(8,128)(2,1)S(1)} %get-tuple-element.31), channel_id=1, source_target_pairs={{0,504},{8,0},{16,8},{24,16},{32,24},{40,32},{48,40},{56,48},{64,5... | collective-permute-start | bytes 737288 | tf_op jit(solution)/shard_map/ppermute | solution.py:10
  160.5 3.7 %collective-permute-start.24 = (bf16[1,14,32,256]{3,2,1,0:T(8,128)(2,1)S(1)}, bf16[1,14,32,256]{3,2,1,0:T(8,128)(2,1)S(1)}, u32[]{:S(2)}, u32[]{:S(2)}) collective-permute-start(bf16[1,14,32,256]{3,2,1,0:T(8,128)(2,1)S(1)} %get-tuple-element.29), channel_id=1, source_target_pairs={{0,496},{8,504},{16,0},{24,8},{32,16},{40,24},{48,32},{56,40},{64,... | collective-permute-start | bytes 688136 | tf_op jit(solution)/shard_map/ppermute | solution.py:10
  164.2 4.7 %collective-permute-start.25 = (bf16[1,13,32,256]{3,2,1,0:T(8,128)(2,1)S(1)}, bf16[1,13,32,256]{3,2,1,0:T(8,128)(2,1)S(1)}, u32[]{:S(2)}, u32[]{:S(2)}) collective-permute-start(bf16[1,13,32,256]{3,2,1,0:T(8,128)(2,1)S(1)} %get-tuple-element.27), channel_id=1, source_target_pairs={{0,488},{8,496},{16,504},{24,0},{32,8},{40,16},{48,24},{56,32},{64... | collective-permute-start | bytes 638984 | tf_op jit(solution)/shard_map/ppermute | solution.py:10
  168.9 2.4 %collective-permute-start.26 = (bf16[1,12,32,256]{3,2,1,0:T(8,128)(2,1)S(1)}, bf16[1,12,32,256]{3,2,1,0:T(8,128)(2,1)S(1)}, u32[]{:S(2)}, u32[]{:S(2)}) collective-permute-start(bf16[1,12,32,256]{3,2,1,0:T(8,128)(2,1)S(1)} %get-tuple-element.25), channel_id=1, source_target_pairs={{0,480},{8,488},{16,496},{24,504},{32,0},{40,8},{48,16},{56,24},{6... | collective-permute-start | bytes 589832 | tf_op jit(solution)/shard_map/ppermute | solution.py:10
  171.4 6.0 %collective-permute-done.22 = bf16[1,15,32,256]{3,2,1,0:T(8,128)(2,1)S(1)} collective-permute-done((bf16[1,15,32,256]{3,2,1,0:T(8,128)(2,1)S(1)}, bf16[1,15,32,256]{3,2,1,0:T(8,128)(2,1)S(1)}, u32[]{:S(2)}, u32[]{:S(2)}) %collective-permute-start.22) | collective-permute-done | bytes 245792 | tf_op jit(solution)/shard_map/ppermute | solution.py:10
  177.4 1.9 collective-permute-start.27
  179.3 0.1 fusion.17
  179.5 3.7 %collective-permute-start.28 = (bf16[1,10,32,256]{3,2,1,0:T(8,128)(2,1)S(1)}, bf16[1,10,32,256]{3,2,1,0:T(8,128)(2,1)S(1)}, u32[]{:S(2)}, u32[]{:S(2)}) collective-permute-start(bf16[1,10,32,256]{3,2,1,0:T(8,128)(2,1)S(1)} %get-tuple-element.21), channel_id=1, source_target_pairs={{0,464},{8,472},{16,480},{24,488},{32,496},{40,504},{48,0},{56,8},... | collective-permute-start | bytes 491528 | tf_op jit(solution)/shard_map/ppermute | solution.py:10
  183.2 2.8 %collective-permute-start.29 = (bf16[1,9,32,256]{3,2,1,0:T(8,128)(2,1)S(1)}, bf16[1,9,32,256]{3,2,1,0:T(8,128)(2,1)S(1)}, u32[]{:S(2)}, u32[]{:S(2)}) collective-permute-start(bf16[1,9,32,256]{3,2,1,0:T(8,128)(2,1)S(1)} %get-tuple-element.19), channel_id=1, source_target_pairs={{0,456},{8,464},{16,472},{24,480},{32,488},{40,496},{48,504},{56,0... | collective-permute-start | bytes 442376 | tf_op jit(solution)/shard_map/ppermute | solution.py:10
  186.1 4.6 %collective-permute-done.27 = bf16[1,11,32,256]{3,2,1,0:T(8,128)(2,1)S(1)} collective-permute-done((bf16[1,11,32,256]{3,2,1,0:T(8,128)(2,1)S(1)}, bf16[1,11,32,256]{3,2,1,0:T(8,128)(2,1)S(1)}, u32[]{:S(2)}, u32[]{:S(2)}) %collective-permute-start.27) | collective-permute-done | bytes 180256 | tf_op jit(solution)/shard_map/ppermute | solution.py:10
  190.8 6.5 %collective-permute-done.28 = bf16[1,10,32,256]{3,2,1,0:T(8,128)(2,1)S(1)} collective-permute-done((bf16[1,10,32,256]{3,2,1,0:T(8,128)(2,1)S(1)}, bf16[1,10,32,256]{3,2,1,0:T(8,128)(2,1)S(1)}, u32[]{:S(2)}, u32[]{:S(2)}) %collective-permute-start.28) | collective-permute-done | bytes 163872 | tf_op jit(solution)/shard_map/ppermute | solution.py:10
  197.2 3.1 %collective-permute-done.29 = bf16[1,9,32,256]{3,2,1,0:T(8,128)(2,1)S(1)} collective-permute-done((bf16[1,9,32,256]{3,2,1,0:T(8,128)(2,1)S(1)}, bf16[1,9,32,256]{3,2,1,0:T(8,128)(2,1)S(1)}, u32[]{:S(2)}, u32[]{:S(2)}) %collective-permute-start.29) | collective-permute-done | bytes 147488 | tf_op jit(solution)/shard_map/ppermute | solution.py:10
  200.4 1.9 bitcast_convert_fusion
  202.3 0.2 copy.135
  202.5 30.4 %all_to_all.11 = bf16[8,1,16,32,256]{4,3,2,1,0:T(8,128)(2,1)S(1)} all-to-all(bf16[8,1,16,32,256]{4,3,2,1,0:T(8,128)(2,1)S(1)} %bitcast.183), channel_id=1, replica_groups=mesh['rows'=64,'inner'=8] {'inner'}, dimensions={0} | all-to-all | bytes 4194304 | tf_op jit(solution)/shard_map/all_to_all | solution.py:21
  232.9 0.4 convert_reduce_fusion
  233.3 1.0 fusion.13
  (62 shorter events, 1.0 us)
Async XLA Ops:
  3.5 35.9 %collective-permute-start.1 = (bf16[1,9,32,256]{3,2,1,0:T(8,128)(2,1)}, bf16[1,9,32,256]{3,2,1,0:T(8,128)(2,1)}, u32[]{:S(2)}, u32[]{:S(2)}) collective-permute-start(bf16[1,9,32,256]{3,2,1,0:T(8,128)(2,1)} %get-tuple-element.6), channel_id=1, source_target_pairs={{0,56},{8,64},{16,72},{24,80},{32,88},{40,96},{48,104},{56,112},{6... | collective-permute-start | bytes 442376 | tf_op jit(solution)/shard_map/ppermute | solution.py:10
  10.7 21.1 %collective-permute-start = (bf16[1,8,32,256]{3,2,1,0:T(8,128)(2,1)}, bf16[1,8,32,256]{3,2,1,0:T(8,128)(2,1)}, u32[]{:S(2)}, u32[]{:S(2)}) collective-permute-start(bf16[1,8,32,256]{3,2,1,0:T(8,128)(2,1)} %constant_dynamic-slice_fusion.14), channel_id=1, source_target_pairs={{0,64},{8,72},{16,80},{24,88},{32,96},{40,104},{48,112},{56,120},{... | collective-permute-start | bytes 393224 | tf_op jit(solution)/shard_map/ppermute | solution.py:10
  16.4 27.1 %collective-permute-start.2 = (bf16[1,10,32,256]{3,2,1,0:T(8,128)(2,1)}, bf16[1,10,32,256]{3,2,1,0:T(8,128)(2,1)}, u32[]{:S(2)}, u32[]{:S(2)}) collective-permute-start(bf16[1,10,32,256]{3,2,1,0:T(8,128)(2,1)} %get-tuple-element.8), channel_id=1, source_target_pairs={{0,48},{8,56},{16,64},{24,72},{32,80},{40,88},{48,96},{56,104},{64... | collective-permute-start | bytes 491528 | tf_op jit(solution)/shard_map/ppermute | solution.py:10
  23.5 22.9 %collective-permute-start.3 = (bf16[1,11,32,256]{3,2,1,0:T(8,128)(2,1)}, bf16[1,11,32,256]{3,2,1,0:T(8,128)(2,1)}, u32[]{:S(2)}, u32[]{:S(2)}) collective-permute-start(bf16[1,11,32,256]{3,2,1,0:T(8,128)(2,1)} %get-tuple-element.10), channel_id=1, source_target_pairs={{0,40},{8,48},{16,56},{24,64},{32,72},{40,80},{48,88},{56,96},{64,... | collective-permute-start | bytes 540680 | tf_op jit(solution)/shard_map/ppermute | solution.py:10
  28.1 26.0 %collective-permute-start.4 = (bf16[1,12,32,256]{3,2,1,0:T(8,128)(2,1)}, bf16[1,12,32,256]{3,2,1,0:T(8,128)(2,1)S(1)}, u32[]{:S(2)}, u32[]{:S(2)}) collective-permute-start(bf16[1,12,32,256]{3,2,1,0:T(8,128)(2,1)} %get-tuple-element.12), channel_id=1, source_target_pairs={{0,32},{8,40},{16,48},{24,56},{32,64},{40,72},{48,80},{56,88},{64,... | collective-permute-start | bytes 589832 | tf_op jit(solution)/shard_map/ppermute | solution.py:10
  31.8 36.9 %copy-start = (bf16[1,10,32,256]{3,2,1,0:T(8,128)(2,1)S(1)}, bf16[1,10,32,256]{3,2,1,0:T(8,128)(2,1)}, u32[]{:S(2)}) copy-start(bf16[1,10,32,256]{3,2,1,0:T(8,128)(2,1)} %get-tuple-element.7) | copy-start | bytes 491524
  31.8 40.2 %copy-start.1 = (bf16[1,9,32,256]{3,2,1,0:T(8,128)(2,1)S(1)}, bf16[1,9,32,256]{3,2,1,0:T(8,128)(2,1)}, u32[]{:S(2)}) copy-start(bf16[1,9,32,256]{3,2,1,0:T(8,128)(2,1)} %get-tuple-element.5) | copy-start | bytes 442372
  31.8 24.7 %collective-permute-start.5 = (bf16[1,13,32,256]{3,2,1,0:T(8,128)(2,1)S(1)}, bf16[1,13,32,256]{3,2,1,0:T(8,128)(2,1)S(1)}, u32[]{:S(2)}, u32[]{:S(2)}) collective-permute-start(bf16[1,13,32,256]{3,2,1,0:T(8,128)(2,1)S(1)} %get-tuple-element.14), channel_id=1, source_target_pairs={{0,24},{8,32},{16,40},{24,48},{32,56},{40,64},{48,72},{56,80},{64,... | collective-permute-start | bytes 638984 | tf_op jit(solution)/shard_map/ppermute | solution.py:10
  39.4 19.1 %collective-permute-start.6 = (bf16[1,14,32,256]{3,2,1,0:T(8,128)(2,1)S(1)}, bf16[1,14,32,256]{3,2,1,0:T(8,128)(2,1)S(1)}, u32[]{:S(2)}, u32[]{:S(2)}) collective-permute-start(bf16[1,14,32,256]{3,2,1,0:T(8,128)(2,1)S(1)} %get-tuple-element.16), channel_id=1, source_target_pairs={{0,16},{8,24},{16,32},{24,40},{32,48},{40,56},{48,64},{56,72},{64,... | collective-permute-start | bytes 688136 | tf_op jit(solution)/shard_map/ppermute | solution.py:10
  43.5 22.9 %collective-permute-start.7 = (bf16[1,15,32,256]{3,2,1,0:T(8,128)(2,1)S(1)}, bf16[1,15,32,256]{3,2,1,0:T(8,128)(2,1)S(1)}, u32[]{:S(2)}, u32[]{:S(2)}) collective-permute-start(bf16[1,15,32,256]{3,2,1,0:T(8,128)(2,1)S(1)} %get-tuple-element.18), channel_id=1, source_target_pairs={{0,8},{8,16},{16,24},{24,32},{32,40},{40,48},{48,56},{56,64},{64,7... | collective-permute-start | bytes 737288 | tf_op jit(solution)/shard_map/ppermute | solution.py:10
  46.4 22.3 %collective-permute-start.8 = (bf16[1,15,32,256]{3,2,1,0:T(8,128)(2,1)S(1)}, bf16[1,15,32,256]{3,2,1,0:T(8,128)(2,1)S(1)}, u32[]{:S(2)}, u32[]{:S(2)}) collective-permute-start(bf16[1,15,32,256]{3,2,1,0:T(8,128)(2,1)S(1)} %get-tuple-element.17), channel_id=1, source_target_pairs={{0,504},{8,0},{16,8},{24,16},{32,24},{40,32},{48,40},{56,48},{64,5... | collective-permute-start | bytes 737288 | tf_op jit(solution)/shard_map/ppermute | solution.py:10
  54.1 17.8 %collective-permute-start.9 = (bf16[1,14,32,256]{3,2,1,0:T(8,128)(2,1)S(1)}, bf16[1,14,32,256]{3,2,1,0:T(8,128)(2,1)S(1)}, u32[]{:S(2)}, u32[]{:S(2)}) collective-permute-start(bf16[1,14,32,256]{3,2,1,0:T(8,128)(2,1)S(1)} %get-tuple-element.15), channel_id=1, source_target_pairs={{0,496},{8,504},{16,0},{24,8},{32,16},{40,24},{48,32},{56,40},{64,... | collective-permute-start | bytes 688136 | tf_op jit(solution)/shard_map/ppermute | solution.py:10
  56.5 22.2 %collective-permute-start.10 = (bf16[1,13,32,256]{3,2,1,0:T(8,128)(2,1)S(1)}, bf16[1,13,32,256]{3,2,1,0:T(8,128)(2,1)S(1)}, u32[]{:S(2)}, u32[]{:S(2)}) collective-permute-start(bf16[1,13,32,256]{3,2,1,0:T(8,128)(2,1)S(1)} %get-tuple-element.13), channel_id=1, source_target_pairs={{0,488},{8,496},{16,504},{24,0},{32,8},{40,16},{48,24},{56,32},{64... | collective-permute-start | bytes 638984 | tf_op jit(solution)/shard_map/ppermute | solution.py:10
  58.5 20.3 %collective-permute-start.11 = (bf16[1,12,32,256]{3,2,1,0:T(8,128)(2,1)S(1)}, bf16[1,12,32,256]{3,2,1,0:T(8,128)(2,1)S(1)}, u32[]{:S(2)}, u32[]{:S(2)}) collective-permute-start(bf16[1,12,32,256]{3,2,1,0:T(8,128)(2,1)S(1)} %get-tuple-element.11), channel_id=1, source_target_pairs={{0,480},{8,488},{16,496},{24,504},{32,0},{40,8},{48,16},{56,24},{6... | collective-permute-start | bytes 589832 | tf_op jit(solution)/shard_map/ppermute | solution.py:10
  66.4 12.4 %collective-permute-start.12 = (bf16[1,11,32,256]{3,2,1,0:T(8,128)(2,1)}, bf16[1,11,32,256]{3,2,1,0:T(8,128)(2,1)S(1)}, u32[]{:S(2)}, u32[]{:S(2)}) collective-permute-start(bf16[1,11,32,256]{3,2,1,0:T(8,128)(2,1)} %get-tuple-element.9), channel_id=1, source_target_pairs={{0,472},{8,480},{16,488},{24,496},{32,504},{40,0},{48,8},{56,16},{... | collective-permute-start | bytes 540680 | tf_op jit(solution)/shard_map/ppermute | solution.py:10
  68.7 19.9 %collective-permute-start.13 = (bf16[1,10,32,256]{3,2,1,0:T(8,128)(2,1)S(1)}, bf16[1,10,32,256]{3,2,1,0:T(8,128)(2,1)S(1)}, u32[]{:S(2)}, u32[]{:S(2)}) collective-permute-start(bf16[1,10,32,256]{3,2,1,0:T(8,128)(2,1)S(1)} %copy-done), channel_id=1, source_target_pairs={{0,464},{8,472},{16,480},{24,488},{32,496},{40,504},{48,0},{56,8},... | collective-permute-start | bytes 491528 | tf_op jit(solution)/shard_map/ppermute | solution.py:10
  71.9 19.8 %collective-permute-start.14 = (bf16[1,9,32,256]{3,2,1,0:T(8,128)(2,1)S(1)}, bf16[1,9,32,256]{3,2,1,0:T(8,128)(2,1)S(1)}, u32[]{:S(2)}, u32[]{:S(2)}) collective-permute-start(bf16[1,9,32,256]{3,2,1,0:T(8,128)(2,1)S(1)} %copy-done.1), channel_id=1, source_target_pairs={{0,456},{8,464},{16,472},{24,480},{32,488},{40,496},{48,504},{56,0... | collective-permute-start | bytes 442376 | tf_op jit(solution)/shard_map/ppermute | solution.py:10
  128.5 17.0 %collective-permute-start.15 = (bf16[1,8,32,256]{3,2,1,0:T(8,128)(2,1)S(1)}, bf16[1,8,32,256]{3,2,1,0:T(8,128)(2,1)S(1)}, u32[]{:S(2)}, u32[]{:S(2)}) collective-permute-start(bf16[1,8,32,256]{3,2,1,0:T(8,128)(2,1)S(1)} %slice.120), channel_id=1, source_target_pairs={{0,64},{8,72},{16,80},{24,88},{32,96},{40,104},{48,112},{56,120},{... | collective-permute-start | bytes 393224 | tf_op jit(solution)/shard_map/ppermute | solution.py:10
  130.4 19.4 %collective-permute-start.16 = (bf16[1,9,32,256]{3,2,1,0:T(8,128)(2,1)S(1)}, bf16[1,9,32,256]{3,2,1,0:T(8,128)(2,1)S(1)}, u32[]{:S(2)}, u32[]{:S(2)}) collective-permute-start(bf16[1,9,32,256]{3,2,1,0:T(8,128)(2,1)S(1)} %get-tuple-element.20), channel_id=1, source_target_pairs={{0,56},{8,64},{16,72},{24,80},{32,88},{40,96},{48,104},{56,112},{6... | collective-permute-start | bytes 442376 | tf_op jit(solution)/shard_map/ppermute | solution.py:10
  132.4 19.5 %collective-permute-start.17 = (bf16[1,10,32,256]{3,2,1,0:T(8,128)(2,1)S(1)}, bf16[1,10,32,256]{3,2,1,0:T(8,128)(2,1)S(1)}, u32[]{:S(2)}, u32[]{:S(2)}) collective-permute-start(bf16[1,10,32,256]{3,2,1,0:T(8,128)(2,1)S(1)} %get-tuple-element.22), channel_id=1, source_target_pairs={{0,48},{8,56},{16,64},{24,72},{32,80},{40,88},{48,96},{56,104},{64... | collective-permute-start | bytes 491528 | tf_op jit(solution)/shard_map/ppermute | solution.py:10
  134.3 20.1 %collective-permute-start.18 = (bf16[1,11,32,256]{3,2,1,0:T(8,128)(2,1)S(1)}, bf16[1,11,32,256]{3,2,1,0:T(8,128)(2,1)S(1)}, u32[]{:S(2)}, u32[]{:S(2)}) collective-permute-start(bf16[1,11,32,256]{3,2,1,0:T(8,128)(2,1)S(1)} %get-tuple-element.24), channel_id=1, source_target_pairs={{0,40},{8,48},{16,56},{24,64},{32,72},{40,80},{48,88},{56,96},{64,... | collective-permute-start | bytes 540680 | tf_op jit(solution)/shard_map/ppermute | solution.py:10
  142.0 18.5 %collective-permute-start.19 = (bf16[1,12,32,256]{3,2,1,0:T(8,128)(2,1)S(1)}, bf16[1,12,32,256]{3,2,1,0:T(8,128)(2,1)S(1)}, u32[]{:S(2)}, u32[]{:S(2)}) collective-permute-start(bf16[1,12,32,256]{3,2,1,0:T(8,128)(2,1)S(1)} %get-tuple-element.26), channel_id=1, source_target_pairs={{0,32},{8,40},{16,48},{24,56},{32,64},{40,72},{48,80},{56,88},{64,... | collective-permute-start | bytes 589832 | tf_op jit(solution)/shard_map/ppermute | solution.py:10
  145.5 18.7 %collective-permute-start.20 = (bf16[1,13,32,256]{3,2,1,0:T(8,128)(2,1)S(1)}, bf16[1,13,32,256]{3,2,1,0:T(8,128)(2,1)S(1)}, u32[]{:S(2)}, u32[]{:S(2)}) collective-permute-start(bf16[1,13,32,256]{3,2,1,0:T(8,128)(2,1)S(1)} %get-tuple-element.28), channel_id=1, source_target_pairs={{0,24},{8,32},{16,40},{24,48},{32,56},{40,64},{48,72},{56,80},{64,... | collective-permute-start | bytes 638984 | tf_op jit(solution)/shard_map/ppermute | solution.py:10
  149.9 19.1 %collective-permute-start.21 = (bf16[1,14,32,256]{3,2,1,0:T(8,128)(2,1)S(1)}, bf16[1,14,32,256]{3,2,1,0:T(8,128)(2,1)S(1)}, u32[]{:S(2)}, u32[]{:S(2)}) collective-permute-start(bf16[1,14,32,256]{3,2,1,0:T(8,128)(2,1)S(1)} %get-tuple-element.30), channel_id=1, source_target_pairs={{0,16},{8,24},{16,32},{24,40},{32,48},{40,56},{48,64},{56,72},{64,... | collective-permute-start | bytes 688136 | tf_op jit(solution)/shard_map/ppermute | solution.py:10
  151.8 25.6 %collective-permute-start.22 = (bf16[1,15,32,256]{3,2,1,0:T(8,128)(2,1)S(1)}, bf16[1,15,32,256]{3,2,1,0:T(8,128)(2,1)S(1)}, u32[]{:S(2)}, u32[]{:S(2)}) collective-permute-start(bf16[1,15,32,256]{3,2,1,0:T(8,128)(2,1)S(1)} %get-tuple-element.32), channel_id=1, source_target_pairs={{0,8},{8,16},{16,24},{24,32},{32,40},{40,48},{48,56},{56,64},{64,7... | collective-permute-start | bytes 737288 | tf_op jit(solution)/shard_map/ppermute | solution.py:10
  154.4 25.1 %collective-permute-start.23 = (bf16[1,15,32,256]{3,2,1,0:T(8,128)(2,1)S(1)}, bf16[1,15,32,256]{3,2,1,0:T(8,128)(2,1)S(1)}, u32[]{:S(2)}, u32[]{:S(2)}) collective-permute-start(bf16[1,15,32,256]{3,2,1,0:T(8,128)(2,1)S(1)} %get-tuple-element.31), channel_id=1, source_target_pairs={{0,504},{8,0},{16,8},{24,16},{32,24},{40,32},{48,40},{56,48},{64,5... | collective-permute-start | bytes 737288 | tf_op jit(solution)/shard_map/ppermute | solution.py:10
  160.5 22.7 %collective-permute-start.24 = (bf16[1,14,32,256]{3,2,1,0:T(8,128)(2,1)S(1)}, bf16[1,14,32,256]{3,2,1,0:T(8,128)(2,1)S(1)}, u32[]{:S(2)}, u32[]{:S(2)}) collective-permute-start(bf16[1,14,32,256]{3,2,1,0:T(8,128)(2,1)S(1)} %get-tuple-element.29), channel_id=1, source_target_pairs={{0,496},{8,504},{16,0},{24,8},{32,16},{40,24},{48,32},{56,40},{64,... | collective-permute-start | bytes 688136 | tf_op jit(solution)/shard_map/ppermute | solution.py:10
  164.2 21.8 %collective-permute-start.25 = (bf16[1,13,32,256]{3,2,1,0:T(8,128)(2,1)S(1)}, bf16[1,13,32,256]{3,2,1,0:T(8,128)(2,1)S(1)}, u32[]{:S(2)}, u32[]{:S(2)}) collective-permute-start(bf16[1,13,32,256]{3,2,1,0:T(8,128)(2,1)S(1)} %get-tuple-element.27), channel_id=1, source_target_pairs={{0,488},{8,496},{16,504},{24,0},{32,8},{40,16},{48,24},{56,32},{64... | collective-permute-start | bytes 638984 | tf_op jit(solution)/shard_map/ppermute | solution.py:10
  168.9 17.2 %collective-permute-start.26 = (bf16[1,12,32,256]{3,2,1,0:T(8,128)(2,1)S(1)}, bf16[1,12,32,256]{3,2,1,0:T(8,128)(2,1)S(1)}, u32[]{:S(2)}, u32[]{:S(2)}) collective-permute-start(bf16[1,12,32,256]{3,2,1,0:T(8,128)(2,1)S(1)} %get-tuple-element.25), channel_id=1, source_target_pairs={{0,480},{8,488},{16,496},{24,504},{32,0},{40,8},{48,16},{56,24},{6... | collective-permute-start | bytes 589832 | tf_op jit(solution)/shard_map/ppermute | solution.py:10
  177.4 13.3 %collective-permute-start.27 = (bf16[1,11,32,256]{3,2,1,0:T(8,128)(2,1)S(1)}, bf16[1,11,32,256]{3,2,1,0:T(8,128)(2,1)S(1)}, u32[]{:S(2)}, u32[]{:S(2)}) collective-permute-start(bf16[1,11,32,256]{3,2,1,0:T(8,128)(2,1)S(1)} %get-tuple-element.23), channel_id=1, source_target_pairs={{0,472},{8,480},{16,488},{24,496},{32,504},{40,0},{48,8},{56,16},{... | collective-permute-start | bytes 540680 | tf_op jit(solution)/shard_map/ppermute | solution.py:10
  179.5 17.8 %collective-permute-start.28 = (bf16[1,10,32,256]{3,2,1,0:T(8,128)(2,1)S(1)}, bf16[1,10,32,256]{3,2,1,0:T(8,128)(2,1)S(1)}, u32[]{:S(2)}, u32[]{:S(2)}) collective-permute-start(bf16[1,10,32,256]{3,2,1,0:T(8,128)(2,1)S(1)} %get-tuple-element.21), channel_id=1, source_target_pairs={{0,464},{8,472},{16,480},{24,488},{32,496},{40,504},{48,0},{56,8},... | collective-permute-start | bytes 491528 | tf_op jit(solution)/shard_map/ppermute | solution.py:10
  183.2 17.2 %collective-permute-start.29 = (bf16[1,9,32,256]{3,2,1,0:T(8,128)(2,1)S(1)}, bf16[1,9,32,256]{3,2,1,0:T(8,128)(2,1)S(1)}, u32[]{:S(2)}, u32[]{:S(2)}) collective-permute-start(bf16[1,9,32,256]{3,2,1,0:T(8,128)(2,1)S(1)} %get-tuple-element.19), channel_id=1, source_target_pairs={{0,456},{8,464},{16,472},{24,480},{32,488},{40,496},{48,504},{56,0... | collective-permute-start | bytes 442376 | tf_op jit(solution)/shard_map/ppermute | solution.py:10
where the time goes:
time: 238 us; the launch traced here: 234 us
  starting transfers between devices  113 us (47%)
  blocking collectives  64.2 us (27%)
  waiting for transfers between devices  39.1 us (16%)
  local copies, waits for them, and re-layouts  8.93 us (4%)
  other arithmetic  4.46 us (2%)
  matrix products  3.82 us (2%)
    ppermute x30, starting transfers between devices, from_behind(): return lax.ppermute(value, axis, pairs)  113 us
    all_to_all x2, blocking collectives, sum_at_owner(): lax.all_to_all(in_blocks(shard, dim, devices), axis, 0, 0, tiled=True)  64.2 us
    ppermute x30, waiting for transfers between devices, from_behind(): return lax.ppermute(value, axis, pairs)  39.1 us
  transfers between devices with their start and end apart: 30, of which 7 were waited for; matrix products, arithmetic and copies ran while one was open for 3% of the time, Pallas kernels for 0%

commit v1 on v0

v1 whole, which is shorter than its diff:
```python
import functools

import jax
import jax.numpy as jnp
from jax import lax
from jax.experimental import pallas as pl
from jax.experimental.pallas import tpu as pltpu
from jax.sharding import Mesh
from jax.sharding import PartitionSpec as P

BS = 256
BAND = 16
NB = 64
NZ, NX, NY, NC = 16, 4, 4, 2
SLAB = 32
ROWS = BAND * SLAB
BF = jnp.bfloat16
F32 = jnp.float32


def shift(value, axis, steps):
    count = lax.axis_size(axis)
    return lax.ppermute(value, axis, [(s, (s + steps) % count) for s in range(count)])


def band_kernel(last, place, own, up1, up2, down1, down2, left0, left_a, left_b, out, padded):
    x, c = place[0], place[1]
    edge = 8 * SLAB
    for dz in range(5):
        padded[dz, :edge, :] = jnp.zeros((edge, BS), BF)
        padded[dz, 3 * edge :, :] = jnp.zeros((edge, BS), BF)
    padded[2, edge : edge + ROWS, :] = own[...]
    padded[3, edge : edge + 15 * SLAB, :] = up1[...]
    padded[4, edge : edge + 11 * SLAB, :] = up2[...]
    padded[1, edge + SLAB : edge + ROWS, :] = down1[...]
    padded[0, edge + 5 * SLAB : edge + ROWS, :] = down2[...]
    contract = (((1,), (1,)), ((), ()))
    for e in range(4):
        wrapped = jnp.where(x < e, 1, 0)
        total = None
        for q in range(4):
            if e == 0:
                block = left0[q]
                turn = q
            else:
                block = left_a[e - 1, q] if q < 2 else left_b[e - 1, q - 2]
                turn = 2 * (c if q < 2 else 1 - c) + q % 2
            start = (16 - e - 4 * turn) * SLAB
            if e:
                start = pl.multiple_of(start, SLAB)
            rows = padded[turn + wrapped, pl.ds(start, ROWS), :]
            term = lax.dot_general(rows, block, contract, preferred_element_type=F32)
            total = term if total is None else total + term
        if last and e == 0:
            total = total - 1.5 * own[...].astype(F32)
        target = lax.rem(x - e + 4, 4)
        if not last:
            out[target] = total.astype(BF)
            continue
        for h in range(2):
            lane = lax.broadcasted_iota(jnp.int32, (128, 128), 1) // SLAB
            for g in range(4):
                packed = None
                for sh in range(4):
                    piece = total[sh * 128 : sh * 128 + 128, h * 128 : h * 128 + 128]
                    if sh != g:
                        piece = pltpu.roll(piece, ((sh - g) % 4) * SLAB, 1)
                    packed = piece if packed is None else jnp.where(lane == sh, piece, packed)
                out[target * 8 + h * 4 + g] = packed.astype(BF)


def band_terms(place, window, left, last):
    shape = (32, 128, 128) if last else (4, ROWS, BS)
    vmem = pl.BlockSpec(memory_space=pltpu.VMEM)
    return pl.pallas_call(
        functools.partial(band_kernel, last),
        out_shape=jax.ShapeDtypeStruct(shape, BF),
        in_specs=[pl.BlockSpec(memory_space=pltpu.SMEM)] + [vmem] * 8,
        out_specs=vmem,
        scratch_shapes=[pltpu.VMEM((5, 4 * 8 * SLAB, BS), BF)],
        compiler_params=pltpu.CompilerParams(vmem_limit_bytes=40 * 2**20),
        cost_estimate=pl.CostEstimate(
            flops=2 * 16 * ROWS * BS * BS, bytes_accessed=6 * 2**20, transcendentals=0
        ),
        name="cube_terms" if last else "square_terms",
    )(place, *window, *left)


def finish_kernel(parts, out):
    total = parts[0].astype(F32)
    for x in range(1, 4):
        total = total + parts[x].astype(F32)
    total = -2.0 * total
    for lo in range(4):
        tile = total[:, lo * SLAB : lo * SLAB + SLAB, :].reshape(BS, 128)
        flat = tile.T
        for hi in range(4):
            out[hi * 4 + lo] = flat[hi * SLAB : hi * SLAB + SLAB, :]


def finish(parts):
    vmem = pl.BlockSpec(memory_space=pltpu.VMEM)
    return pl.pallas_call(
        finish_kernel,
        out_shape=jax.ShapeDtypeStruct((BAND, SLAB, BS), F32),
        in_specs=[vmem],
        out_specs=vmem,
        compiler_params=pltpu.CompilerParams(vmem_limit_bytes=40 * 2**20),
        name="finish",
    )(parts)


def band_window(own):
    up1 = shift(own[: 15 * SLAB], "z", -1)
    down1 = shift(own[SLAB:], "z", 1)
    up2 = shift(own[: 11 * SLAB], "z", -2)
    down2 = shift(own[5 * SLAB :], "z", 2)
    return own, up1, up2, down1, down2


def per_device(blocks, columns):
    z, x, y, c = (lax.axis_index(name) for name in ("z", "x", "y", "core"))
    row = z * NX + x
    listed = lax.dynamic_slice_in_dim(columns, row, 1, 0)
    target = (row + jnp.arange(BAND, dtype=jnp.int32) - BAND // 2) % NB
    live = jnp.any(listed == target[:, None], axis=1)[:, None, None]
    place = jnp.stack([x, c]).astype(jnp.int32)

    masked = jnp.where(live, blocks[0], jnp.zeros_like(blocks[0]))
    slab = y * NC + c
    pick = (jnp.arange(BS)[None, :] == slab * SLAB + jnp.arange(SLAB)[:, None]).astype(BF)
    own = jnp.einsum("pn,skn->spk", pick, masked, preferred_element_type=F32)
    own = own.astype(BF).reshape(ROWS, BS)

    quarters = masked.reshape(4, 4, BS, BS)
    half = lax.dynamic_slice_in_dim(quarters, 2 * c, 2, 0)
    left_a = jnp.stack([shift(half[:, e], "x", e) for e in (1, 2, 3)])
    left_b = shift(left_a, "core", 1)
    left = (quarters[:, 0], left_a, left_b)

    terms = band_terms(place, band_window(own), left, False)
    parts = lax.all_to_all(terms, "x", 0, 0, tiled=True)
    square = jnp.sum(parts.astype(F32), axis=0).reshape(BAND, SLAB, BS)
    square = jnp.where(live, square, 0.0).astype(BF).reshape(ROWS, BS)

    terms = band_terms(place, band_window(square), left, True)
    parts = lax.all_to_all(terms, ("x", "y", "core"), 0, 0, tiled=True)
    result = finish(parts.reshape(4, 8, 128, 128))
    return jnp.where(live, result, 0.0)[None]


def solution(mesh):
    grid = Mesh(mesh.devices.reshape(NZ, NX, NY, NC), ("z", "x", "y", "core"))
    return jax.shard_map(
        per_device,
        mesh=grid,
        in_specs=(P(("z", "x"), None, None, None), P()),
        out_specs=P(("z", "x"), None, ("y", "core"), None),
        check_vma=False,
    )
```

time: 238 us -> 132 us (0.55); the launches traced: 234 us -> 131 us
  starting transfers between devices: 113 us -> 53.7 us
  blocking collectives: 64.2 us -> 25.1 us
  local copies, waits for them, and re-layouts: 8.93 us -> 2.53 us
  Pallas kernels: 0 us -> 5.48 us
    ppermute x30 -> x12, starting transfers between devices: 113 us -> 50.1 us  [shift(): lax.ppermute(value, axis, [(s, (s + steps) % count) for s in range(count)])]
    all_to_all x2 -> x1, blocking collectives: 64.2 us -> 25.1 us  [per_device(): parts = lax.all_to_all(terms, ('x', 'y', 'core'), 0, 0, tiled=True)]
    ppermute x30 -> x12, waiting for transfers between devices: 39.1 us -> 24 us  [shift(): lax.ppermute(value, axis, [(s, (s + steps) % count) for s in range(count)])]
    all_to_all x0 -> x1, waiting for transfers between devices: none -> 13.3 us  [per_device(): parts = lax.all_to_all(terms, 'x', 0, 0, tiled=True)]
    pallas_call x0 -> x3, Pallas kernels: none -> 5.48 us  [the longest x2 5.28 us: band_terms(): pl.pallas_call(functools.partial(band_kernel, last), out_shape=jax.ShapeD...]
    slice x16 -> x4, local copies, waits for them, and re-layouts: 4.06 us -> 0.15 us  [the longest x2 0.09 us: band_window(): down1 = shift(own[SLAB:], 'z', 1)]
    all_to_all x0 -> x1, starting transfers between devices: none -> 3.51 us  [per_device(): parts = lax.all_to_all(terms, 'x', 0, 0, tiled=True)]
    unnamed x33 -> x4, local copies, waits for them, and re-layouts: 4.21 us -> 0.7 us
  transfers between devices with their start and end apart: 30 -> 13, of which waited for: 7 -> 7; matrix products, arithmetic and copies ran while one was open for 3% -> 3% of each run, Pallas kernels for 0% -> 0%
where the time goes in v1:
time: 132 us; the launch traced here: 131 us
  starting transfers between devices  53.7 us (41%)
  waiting for transfers between devices  37.3 us (28%)
  blocking collectives  25.1 us (19%)
  Pallas kernels  5.48 us (4%)
  other arithmetic  4.4 us (3%)
  local copies, waits for them, and re-layouts  2.53 us (2%)
  matrix products  2.37 us (2%)
    ppermute x12, starting transfers between devices, shift(): lax.ppermute(value, axis, [(s, (s + steps) % count) for s in range(count)])  50.1 us
    all_to_all x1, blocking collectives, per_device(): parts = lax.all_to_all(terms, ('x', 'y', 'core'), 0, 0, tiled=True)  25.1 us
    ppermute x12, waiting for transfers between devices, shift(): lax.ppermute(value, axis, [(s, (s + steps) % count) for s in range(count)])  24 us
    all_to_all x1, waiting for transfers between devices, per_device(): parts = lax.all_to_all(terms, 'x', 0, 0, tiled=True)  13.3 us
    pallas_call x2, Pallas kernels, band_terms(): pl.pallas_call(functools.partial(band_kernel, last), out_shape=jax.ShapeD...  5.28 us
    all_to_all x1, starting transfers between devices, per_device(): parts = lax.all_to_all(terms, 'x', 0, 0, tiled=True)  3.51 us
  transfers between devices with their start and end apart: 13, of which 7 were waited for; matrix products, arithmetic and copies ran while one was open for 3% of the time, Pallas kernels for 0%

profile of v1, /device:TPU:1, one launch (start us, length us, event | category | flops | bytes accessed | tf_op | source)
XLA Modules:
  0.0 131.0 jit_solution(8373914121214102761)
XLA Ops:
  0.0 0.0 copy-start
  0.0 0.7 copy-done
  0.7 0.2 dynamic-slice_reduce_fusion
  0.9 0.2 compare_reduce_fusion
  1.1 0.1 broadcast_in_dim.54
  1.2 0.1 copy.6
  1.3 1.8 %copy_select_fusion = bf16[4,4,256,256]{3,2,0,1:T(8,128)(2,1)S(1)} fusion(bf16[4,4,256,256]{3,2,1,0:T(8,128)(2,1)} %bitcast.42, pred[4,4]{0,1:T(4,128)(4,1)S(1)} %copy.6), kind=kLoop, calls=%fused_computation.2 | loop fusion | flops 1048576 | bytes 4194320 | tf_op jit(solution)/shard_map/jit(_where)/select_n | solution.py:129
  3.1 0.0 copy-start.1
  3.1 0.1 dynamic-slice_bitcast_fusion.2
  3.2 5.2 %collective-permute-start.6 = (bf16[2,256,256]{2,1,0:T(8,128)(2,1)S(1)}, bf16[2,256,256]{2,1,0:T(8,128)(2,1)S(1)}, u32[]{:S(2)}, u32[]{:S(2)}) collective-permute-start(bf16[2,256,256]{2,1,0:T(8,128)(2,1)S(1)} %get-tuple-element.7), channel_id=1, source_target_pairs={{0,24},{8,0},{16,8},{24,16},{1,25},{9,1},{17,9},{25,17},{2,26},{10... | collective-permute-start | bytes 786440 | tf_op jit(solution)/shard_map/ppermute | solution.py:23
  8.4 2.4 %collective-permute-start.5 = (bf16[2,256,256]{2,1,0:T(8,128)(2,1)S(1)}, bf16[2,256,256]{2,1,0:T(8,128)(2,1)S(1)}, u32[]{:S(2)}, u32[]{:S(2)}) collective-permute-start(bf16[2,256,256]{2,1,0:T(8,128)(2,1)S(1)} %get-tuple-element.6), channel_id=1, source_target_pairs={{0,16},{8,24},{16,0},{24,8},{1,17},{9,25},{17,1},{25,9},{2,18},{10... | collective-permute-start | bytes 786440 | tf_op jit(solution)/shard_map/ppermute | solution.py:23
  10.8 2.5 %collective-permute-start.4 = (bf16[2,256,256]{2,1,0:T(8,128)(2,1)S(1)}, bf16[2,256,256]{2,1,0:T(8,128)(2,1)}, u32[]{:S(2)}, u32[]{:S(2)}) collective-permute-start(bf16[2,256,256]{2,1,0:T(8,128)(2,1)S(1)} %get-tuple-element.5), channel_id=1, source_target_pairs={{0,8},{8,16},{16,24},{24,0},{1,9},{9,17},{17,25},{25,1},{2,10},{10... | collective-permute-start | bytes 786440 | tf_op jit(solution)/shard_map/ppermute | solution.py:23
  13.4 2.4 %fusion.2 = bf16[16,256,32]{1,2,0:T(8,128)(2,1)S(1)} fusion(bf16[1,16,256,256]{3,2,1,0:T(8,128)(2,1)} %param.2, pred[16]{0:T(512)(128)(4,1)S(1)} %compare_reduce_fusion, s32[32]{0:T(128)S(1)} %iota_add_fusion), kind=kOutput, calls=%fused_computation.5 | convolution fusion | flops 68296704 | bytes 2359440 | tf_op jit(solution)/shard_map/pn,skn->spk/dot_general | solution.py:132
  15.7 0.0 copy-done.1
  15.8 0.0 collective-permute-done.6
  15.8 1.3 %collective-permute-done.5 = bf16[2,256,256]{2,1,0:T(8,128)(2,1)S(1)} collective-permute-done((bf16[2,256,256]{2,1,0:T(8,128)(2,1)S(1)}, bf16[2,256,256]{2,1,0:T(8,128)(2,1)S(1)}, u32[]{:S(2)}, u32[]{:S(2)}) %collective-permute-start.5) | collective-permute-done | bytes 262176 | tf_op jit(solution)/shard_map/ppermute | solution.py:23
  17.1 4.5 %collective-permute-done.4 = bf16[2,256,256]{2,1,0:T(8,128)(2,1)} collective-permute-done((bf16[2,256,256]{2,1,0:T(8,128)(2,1)S(1)}, bf16[2,256,256]{2,1,0:T(8,128)(2,1)}, u32[]{:S(2)}, u32[]{:S(2)}) %collective-permute-start.4) | collective-permute-done | bytes 262176 | tf_op jit(solution)/shard_map/ppermute | solution.py:23
  21.6 1.0 pad_maximum_fusion.left_a
  22.7 6.5 %collective-permute-start.7 = (bf16[3,2,256,256]{3,2,1,0:T(8,128)(2,1)S(1)}, bf16[3,2,256,256]{3,2,1,0:T(8,128)(2,1)S(1)}, u32[]{:S(2)}, u32[]{:S(2)}) collective-permute-start(bf16[3,2,256,256]{3,2,1,0:T(8,128)(2,1)S(1)} %pad_maximum_fusion.left_a), channel_id=1, source_target_pairs={{0,1},{1,0},{2,3},{3,2},{4,5},{5,4},{6,7},{7,6},{8,9},{9,8},{10,11... | collective-permute-start | bytes 2359304 | tf_op jit(solution)/shard_map/ppermute | solution.py:23
  29.2 11.1 %collective-permute-start = (bf16[480,256]{1,0:T(8,128)(2,1)S(1)}, bf16[480,256]{1,0:T(8,128)(2,1)S(1)}, u32[]{:S(2)}, u32[]{:S(2)}) collective-permute-start(bf16[480,256]{1,0:T(8,128)(2,1)S(1)} %bitcast.47), channel_id=1, source_target_pairs={{0,480},{32,0},{64,32},{96,64},{128,96},{160,128},{192,160},{224,1... | collective-permute-start | bytes 737288 | tf_op jit(solution)/shard_map/ppermute | solution.py:23
  40.4 3.1 %collective-permute-start.1 = (bf16[352,256]{1,0:T(8,128)(2,1)S(1)}, bf16[352,256]{1,0:T(8,128)(2,1)S(1)}, u32[]{:S(2)}, u32[]{:S(2)}) collective-permute-start(bf16[352,256]{1,0:T(8,128)(2,1)S(1)} %bitcast.50), channel_id=1, source_target_pairs={{0,448},{32,480},{64,0},{96,32},{128,64},{160,96},{192,128},{224,1... | collective-permute-start | bytes 540680 | tf_op jit(solution)/shard_map/ppermute | solution.py:23
  43.5 2.6 %collective-permute-start.2 = (bf16[480,256]{1,0:T(8,128)(2,1)S(1)}, bf16[480,256]{1,0:T(8,128)(2,1)S(1)}, u32[]{:S(2)}, u32[]{:S(2)}) collective-permute-start(bf16[480,256]{1,0:T(8,128)(2,1)S(1)} %bitcast.45), channel_id=1, source_target_pairs={{0,32},{32,64},{64,96},{96,128},{128,160},{160,192},{192,224},{224... | collective-permute-start | bytes 737288 | tf_op jit(solution)/shard_map/ppermute | solution.py:23
  46.1 2.4 %collective-permute-start.3 = (bf16[352,256]{1,0:T(8,128)(2,1)S(1)}, bf16[352,256]{1,0:T(8,128)(2,1)S(1)}, u32[]{:S(2)}, u32[]{:S(2)}) collective-permute-start(bf16[352,256]{1,0:T(8,128)(2,1)S(1)} %bitcast.49), channel_id=1, source_target_pairs={{0,64},{32,96},{64,128},{96,160},{128,192},{160,224},{192,256},{22... | collective-permute-start | bytes 540680 | tf_op jit(solution)/shard_map/ppermute | solution.py:23
  48.5 1.1 slice_bitcast_fusion.left0
  49.6 0.1 pad_add_fusion.place
  49.7 3.6 %collective-permute-done.1.up2 = bf16[352,256]{1,0:T(8,128)(2,1)S(1)} collective-permute-done((bf16[352,256]{1,0:T(8,128)(2,1)S(1)}, bf16[352,256]{1,0:T(8,128)(2,1)S(1)}, u32[]{:S(2)}, u32[]{:S(2)}) %collective-permute-start.1) | collective-permute-done | bytes 180256 | tf_op jit(solution)/shard_map/ppermute | solution.py:23
  53.3 5.1 %collective-permute-done.3.down2 = bf16[352,256]{1,0:T(8,128)(2,1)S(1)} collective-permute-done((bf16[352,256]{1,0:T(8,128)(2,1)S(1)}, bf16[352,256]{1,0:T(8,128)(2,1)S(1)}, u32[]{:S(2)}, u32[]{:S(2)}) %collective-permute-start.3) | collective-permute-done | bytes 180256 | tf_op jit(solution)/shard_map/ppermute | solution.py:23
  58.4 0.0 collective-permute-done.up1
  58.4 0.0 collective-permute-done.2.down1
  58.4 0.0 collective-permute-done.7.left_b
  58.4 2.9 %square_terms.1 = bf16[4,512,256]{2,1,0:T(8,128)(2,1)} custom-call(s32[2]{0:T(128)S(1)} %pad_add_fusion.place, bf16[512,256]{1,0:T(8,128)(2,1)S(1)} %bitcast.39, bf16[480,256]{1,0:T(8,128)(2,1)S(1)} %collective-permute-done.up1, bf16[352,256]{1,0:T(8,128)(2,1)S(1)} %collective-permute-done.1.up2, bf16[480,256]{1,0:T(8,128)(2,1)S(1)} %collective-permute-done.2.down1, ...), custom_call_target="tpu_custom_call" | custom-call | flops 1073741824 | bytes 6291456 | tf_op jit(solution)/shard_map/square_terms/pallas_call | solution.py:75
  61.3 3.5 %all-to-all-start = ((bf16[4,512,256]{2,1,0:T(8,128)(2,1)}), bf16[4,512,256]{2,1,0:T(8,128)(2,1)S(1)}, u32[]{:S(2)}, u32[]{:S(2)}) async-start(bf16[4,512,256]{2,1,0:T(8,128)(2,1)} %square_terms.1), calls=%async_computation | async-start | bytes 2097152 | tf_op jit(solution)/shard_map/all_to_all | solution.py:142
  64.8 0.1 broadcast_in_dim.49
  64.9 0.1 broadcast_in_dim.50
  65.0 13.3 %all-to-all-done = bf16[4,512,256]{2,1,0:T(8,128)(2,1)S(1)} async-done(((bf16[4,512,256]{2,1,0:T(8,128)(2,1)}), bf16[4,512,256]{2,1,0:T(8,128)(2,1)S(1)}, u32[]{:S(2)}, u32[]{:S(2)}) %all-to-all-start) | async-done | bytes 1048608 | tf_op jit(solution)/shard_map/all_to_all | solution.py:142
  78.3 0.1 convert_reduce_fusion
  78.4 0.1 select_convert_fusion
  78.6 6.1 %collective-permute-start.8 = (bf16[480,256]{1,0:T(8,128)(2,1)S(1)}, bf16[480,256]{1,0:T(8,128)(2,1)S(1)}, u32[]{:S(2)}, u32[]{:S(2)}) collective-permute-start(bf16[480,256]{1,0:T(8,128)(2,1)S(1)} %bitcast.48), channel_id=1, source_target_pairs={{0,480},{32,0},{64,32},{96,64},{128,96},{160,128},{192,160},{224,1... | collective-permute-start | bytes 737288 | tf_op jit(solution)/shard_map/ppermute | solution.py:23
  84.7 1.9 %collective-permute-start.10 = (bf16[480,256]{1,0:T(8,128)(2,1)S(1)}, bf16[480,256]{1,0:T(8,128)(2,1)S(1)}, u32[]{:S(2)}, u32[]{:S(2)}) collective-permute-start(bf16[480,256]{1,0:T(8,128)(2,1)S(1)} %bitcast.46), channel_id=1, source_target_pairs={{0,32},{32,64},{64,96},{96,128},{128,160},{160,192},{192,224},{224... | collective-permute-start | bytes 737288 | tf_op jit(solution)/shard_map/ppermute | solution.py:23
  86.7 4.0 %collective-permute-start.9 = (bf16[352,256]{1,0:T(8,128)(2,1)S(1)}, bf16[352,256]{1,0:T(8,128)(2,1)S(1)}, u32[]{:S(2)}, u32[]{:S(2)}) collective-permute-start(bf16[352,256]{1,0:T(8,128)(2,1)S(1)} %bitcast.52), channel_id=1, source_target_pairs={{0,448},{32,480},{64,0},{96,32},{128,64},{160,96},{192,128},{224,1... | collective-permute-start | bytes 540680 | tf_op jit(solution)/shard_map/ppermute | solution.py:23
  90.7 2.2 %collective-permute-start.11 = (bf16[352,256]{1,0:T(8,128)(2,1)S(1)}, bf16[352,256]{1,0:T(8,128)(2,1)S(1)}, u32[]{:S(2)}, u32[]{:S(2)}) collective-permute-start(bf16[352,256]{1,0:T(8,128)(2,1)S(1)} %bitcast.51), channel_id=1, source_target_pairs={{0,64},{32,96},{64,128},{96,160},{128,192},{160,224},{192,256},{22... | collective-permute-start | bytes 540680 | tf_op jit(solution)/shard_map/ppermute | solution.py:23
  92.9 0.1 select_convert_fusion.1.own
  93.0 2.8 %collective-permute-done.9.up2 = bf16[352,256]{1,0:T(8,128)(2,1)S(1)} collective-permute-done((bf16[352,256]{1,0:T(8,128)(2,1)S(1)}, bf16[352,256]{1,0:T(8,128)(2,1)S(1)}, u32[]{:S(2)}, u32[]{:S(2)}) %collective-permute-start.9) | collective-permute-done | bytes 180256 | tf_op jit(solution)/shard_map/ppermute | solution.py:23
  95.8 6.6 %collective-permute-done.11.down2 = bf16[352,256]{1,0:T(8,128)(2,1)S(1)} collective-permute-done((bf16[352,256]{1,0:T(8,128)(2,1)S(1)}, bf16[352,256]{1,0:T(8,128)(2,1)S(1)}, u32[]{:S(2)}, u32[]{:S(2)}) %collective-permute-start.11) | collective-permute-done | bytes 180256 | tf_op jit(solution)/shard_map/ppermute | solution.py:23
  102.4 0.0 collective-permute-done.8.up1
  102.4 0.0 collective-permute-done.10.down1
  102.4 2.4 %cube_terms.1 = bf16[32,128,128]{2,1,0:T(8,128)(2,1)S(1)} custom-call(s32[2]{0:T(128)S(1)} %pad_add_fusion.place, bf16[512,256]{1,0:T(8,128)(2,1)S(1)} %select_convert_fusion.1.own, bf16[480,256]{1,0:T(8,128)(2,1)S(1)} %collective-permute-done.8.up1, bf16[352,256]{1,0:T(8,128)(2,1)S(1)} %collective-permute-done.9.up2, ...), custom_call_target="tpu_custom_call" | custom-call | flops 1073741824 | bytes 6291456 | tf_op jit(solution)/shard_map/cube_terms/pallas_call | solution.py:75
  104.8 25.1 %all_to_all.10 = bf16[32,128,128]{2,1,0:T(8,128)(2,1)S(1)} all-to-all(bf16[32,128,128]{2,1,0:T(8,128)(2,1)S(1)} %cube_terms.1), channel_id=1, replica_groups=mesh['z'=16,'x'=4,'y'=4,'core'=2] {'x','y','core'}, dimensions={0} | all-to-all | bytes 2097152 | tf_op jit(solution)/shard_map/all_to_all | solution.py:147
  129.9 0.2 finish.1
  130.1 0.9 select_bitcast_fusion
  (6 shorter events, 0.2 us)
Async XLA Ops:
  0.0 0.7 copy-start
  3.1 12.7 %copy-start.1 = (bf16[4,4,256,256]{3,2,0,1:T(8,128)(2,1)}, bf16[4,4,256,256]{3,2,0,1:T(8,128)(2,1)S(1)}, u32[]{:S(2)}) copy-start(bf16[4,4,256,256]{3,2,0,1:T(8,128)(2,1)S(1)} %copy_select_fusion) | copy-start | bytes 6291460
  3.2 12.6 %collective-permute-start.6 = (bf16[2,256,256]{2,1,0:T(8,128)(2,1)S(1)}, bf16[2,256,256]{2,1,0:T(8,128)(2,1)S(1)}, u32[]{:S(2)}, u32[]{:S(2)}) collective-permute-start(bf16[2,256,256]{2,1,0:T(8,128)(2,1)S(1)} %get-tuple-element.7), channel_id=1, source_target_pairs={{0,24},{8,0},{16,8},{24,16},{1,25},{9,1},{17,9},{25,17},{2,26},{10... | collective-permute-start | bytes 786440 | tf_op jit(solution)/shard_map/ppermute | solution.py:23
  8.4 8.7 %collective-permute-start.5 = (bf16[2,256,256]{2,1,0:T(8,128)(2,1)S(1)}, bf16[2,256,256]{2,1,0:T(8,128)(2,1)S(1)}, u32[]{:S(2)}, u32[]{:S(2)}) collective-permute-start(bf16[2,256,256]{2,1,0:T(8,128)(2,1)S(1)} %get-tuple-element.6), channel_id=1, source_target_pairs={{0,16},{8,24},{16,0},{24,8},{1,17},{9,25},{17,1},{25,9},{2,18},{10... | collective-permute-start | bytes 786440 | tf_op jit(solution)/shard_map/ppermute | solution.py:23
  10.8 10.8 %collective-permute-start.4 = (bf16[2,256,256]{2,1,0:T(8,128)(2,1)S(1)}, bf16[2,256,256]{2,1,0:T(8,128)(2,1)}, u32[]{:S(2)}, u32[]{:S(2)}) collective-permute-start(bf16[2,256,256]{2,1,0:T(8,128)(2,1)S(1)} %get-tuple-element.5), channel_id=1, source_target_pairs={{0,8},{8,16},{16,24},{24,0},{1,9},{9,17},{17,25},{25,1},{2,10},{10... | collective-permute-start | bytes 786440 | tf_op jit(solution)/shard_map/ppermute | solution.py:23
  22.7 35.8 %collective-permute-start.7 = (bf16[3,2,256,256]{3,2,1,0:T(8,128)(2,1)S(1)}, bf16[3,2,256,256]{3,2,1,0:T(8,128)(2,1)S(1)}, u32[]{:S(2)}, u32[]{:S(2)}) collective-permute-start(bf16[3,2,256,256]{3,2,1,0:T(8,128)(2,1)S(1)} %pad_maximum_fusion.left_a), channel_id=1, source_target_pairs={{0,1},{1,0},{2,3},{3,2},{4,5},{5,4},{6,7},{7,6},{8,9},{9,8},{10,11... | collective-permute-start | bytes 2359304 | tf_op jit(solution)/shard_map/ppermute | solution.py:23
  29.2 29.2 %collective-permute-start = (bf16[480,256]{1,0:T(8,128)(2,1)S(1)}, bf16[480,256]{1,0:T(8,128)(2,1)S(1)}, u32[]{:S(2)}, u32[]{:S(2)}) collective-permute-start(bf16[480,256]{1,0:T(8,128)(2,1)S(1)} %bitcast.47), channel_id=1, source_target_pairs={{0,480},{32,0},{64,32},{96,64},{128,96},{160,128},{192,160},{224,1... | collective-permute-start | bytes 737288 | tf_op jit(solution)/shard_map/ppermute | solution.py:23
  40.4 12.9 %collective-permute-start.1 = (bf16[352,256]{1,0:T(8,128)(2,1)S(1)}, bf16[352,256]{1,0:T(8,128)(2,1)S(1)}, u32[]{:S(2)}, u32[]{:S(2)}) collective-permute-start(bf16[352,256]{1,0:T(8,128)(2,1)S(1)} %bitcast.50), channel_id=1, source_target_pairs={{0,448},{32,480},{64,0},{96,32},{128,64},{160,96},{192,128},{224,1... | collective-permute-start | bytes 540680 | tf_op jit(solution)/shard_map/ppermute | solution.py:23
  43.5 14.9 %collective-permute-start.2 = (bf16[480,256]{1,0:T(8,128)(2,1)S(1)}, bf16[480,256]{1,0:T(8,128)(2,1)S(1)}, u32[]{:S(2)}, u32[]{:S(2)}) collective-permute-start(bf16[480,256]{1,0:T(8,128)(2,1)S(1)} %bitcast.45), channel_id=1, source_target_pairs={{0,32},{32,64},{64,96},{96,128},{128,160},{160,192},{192,224},{224... | collective-permute-start | bytes 737288 | tf_op jit(solution)/shard_map/ppermute | solution.py:23
  46.1 12.3 %collective-permute-start.3 = (bf16[352,256]{1,0:T(8,128)(2,1)S(1)}, bf16[352,256]{1,0:T(8,128)(2,1)S(1)}, u32[]{:S(2)}, u32[]{:S(2)}) collective-permute-start(bf16[352,256]{1,0:T(8,128)(2,1)S(1)} %bitcast.49), channel_id=1, source_target_pairs={{0,64},{32,96},{64,128},{96,160},{128,192},{160,224},{192,256},{22... | collective-permute-start | bytes 540680 | tf_op jit(solution)/shard_map/ppermute | solution.py:23
  61.3 17.0 %all-to-all-start = ((bf16[4,512,256]{2,1,0:T(8,128)(2,1)}), bf16[4,512,256]{2,1,0:T(8,128)(2,1)S(1)}, u32[]{:S(2)}, u32[]{:S(2)}) async-start(bf16[4,512,256]{2,1,0:T(8,128)(2,1)} %square_terms.1), calls=%async_computation | async-start | bytes 2097152 | tf_op jit(solution)/shard_map/all_to_all | solution.py:142
  78.6 23.8 %collective-permute-start.8 = (bf16[480,256]{1,0:T(8,128)(2,1)S(1)}, bf16[480,256]{1,0:T(8,128)(2,1)S(1)}, u32[]{:S(2)}, u32[]{:S(2)}) collective-permute-start(bf16[480,256]{1,0:T(8,128)(2,1)S(1)} %bitcast.48), channel_id=1, source_target_pairs={{0,480},{32,0},{64,32},{96,64},{128,96},{160,128},{192,160},{224,1... | collective-permute-start | bytes 737288 | tf_op jit(solution)/shard_map/ppermute | solution.py:23
  84.7 17.7 %collective-permute-start.10 = (bf16[480,256]{1,0:T(8,128)(2,1)S(1)}, bf16[480,256]{1,0:T(8,128)(2,1)S(1)}, u32[]{:S(2)}, u32[]{:S(2)}) collective-permute-start(bf16[480,256]{1,0:T(8,128)(2,1)S(1)} %bitcast.46), channel_id=1, source_target_pairs={{0,32},{32,64},{64,96},{96,128},{128,160},{160,192},{192,224},{224... | collective-permute-start | bytes 737288 | tf_op jit(solution)/shard_map/ppermute | solution.py:23
  86.7 9.1 %collective-permute-start.9 = (bf16[352,256]{1,0:T(8,128)(2,1)S(1)}, bf16[352,256]{1,0:T(8,128)(2,1)S(1)}, u32[]{:S(2)}, u32[]{:S(2)}) collective-permute-start(bf16[352,256]{1,0:T(8,128)(2,1)S(1)} %bitcast.52), channel_id=1, source_target_pairs={{0,448},{32,480},{64,0},{96,32},{128,64},{160,96},{192,128},{224,1... | collective-permute-start | bytes 540680 | tf_op jit(solution)/shard_map/ppermute | solution.py:23
  90.7 11.7 %collective-permute-start.11 = (bf16[352,256]{1,0:T(8,128)(2,1)S(1)}, bf16[352,256]{1,0:T(8,128)(2,1)S(1)}, u32[]{:S(2)}, u32[]{:S(2)}) collective-permute-start(bf16[352,256]{1,0:T(8,128)(2,1)S(1)} %bitcast.51), channel_id=1, source_target_pairs={{0,64},{32,96},{64,128},{96,160},{128,192},{160,224},{192,256},{22... | collective-permute-start | bytes 540680 | tf_op jit(solution)/shard_map/ppermute | solution.py:23

commit v2 on v1

--- a/solution.py
+++ b/solution.py
@@ -23,7 +23,7 @@
     return lax.ppermute(value, axis, [(s, (s + steps) % count) for s in range(count)])
 
 
-def band_kernel(last, place, own, up1, up2, down1, down2, left0, left_a, left_b, out, padded):
+def band_kernel(last, place, own, up1, up2, down1, down2, left_a, left_b, out, padded):
     x, c = place[0], place[1]
     edge = 8 * SLAB
     for dz in range(5):
@@ -37,23 +37,17 @@
     contract = (((1,), (1,)), ((), ()))
     for e in range(4):
         wrapped = jnp.where(x < e, 1, 0)
+        target = lax.rem(x - e + 4, 4)
         total = None
         for q in range(4):
-            if e == 0:
-                block = left0[q]
-                turn = q
-            else:
-                block = left_a[e - 1, q] if q < 2 else left_b[e - 1, q - 2]
-                turn = 2 * (c if q < 2 else 1 - c) + q % 2
-            start = (16 - e - 4 * turn) * SLAB
-            if e:
-                start = pl.multiple_of(start, SLAB)
+            block = left_a[target, q] if q < 2 else left_b[target, q - 2]
+            turn = 2 * (c if q < 2 else 1 - c) + q % 2
+            start = pl.multiple_of((16 - e - 4 * turn) * SLAB, SLAB)
             rows = padded[turn + wrapped, pl.ds(start, ROWS), :]
             term = lax.dot_general(rows, block, contract, preferred_element_type=F32)
             total = term if total is None else total + term
         if last and e == 0:
             total = total - 1.5 * own[...].astype(F32)
-        target = lax.rem(x - e + 4, 4)
         if not last:
             out[target] = total.astype(BF)
             continue
@@ -75,7 +69,7 @@
     return pl.pallas_call(
         functools.partial(band_kernel, last),
         out_shape=jax.ShapeDtypeStruct(shape, BF),
-        in_specs=[pl.BlockSpec(memory_space=pltpu.SMEM)] + [vmem] * 8,
+        in_specs=[pl.BlockSpec(memory_space=pltpu.SMEM)] + [vmem] * 7,
         out_specs=vmem,
         scratch_shapes=[pltpu.VMEM((5, 4 * 8 * SLAB, BS), BF)],
         compiler_params=pltpu.CompilerParams(vmem_limit_bytes=40 * 2**20),
@@ -86,7 +80,7 @@
     )(place, *window, *left)
 
 
-def finish_kernel(parts, out):
+def finish_kernel(live, parts, out):
     total = parts[0].astype(F32)
     for x in range(1, 4):
         total = total + parts[x].astype(F32)
@@ -95,19 +89,63 @@
         tile = total[:, lo * SLAB : lo * SLAB + SLAB, :].reshape(BS, 128)
         flat = tile.T
         for hi in range(4):
-            out[hi * 4 + lo] = flat[hi * SLAB : hi * SLAB + SLAB, :]
+            slot = hi * 4 + lo
+            piece = flat[hi * SLAB : hi * SLAB + SLAB, :]
+            out[slot] = jnp.where(live[slot] > 0, piece, 0.0)
 
 
-def finish(parts):
+def finish(live, parts):
     vmem = pl.BlockSpec(memory_space=pltpu.VMEM)
     return pl.pallas_call(
         finish_kernel,
         out_shape=jax.ShapeDtypeStruct((BAND, SLAB, BS), F32),
-        in_specs=[vmem],
+        in_specs=[pl.BlockSpec(memory_space=pltpu.SMEM), vmem],
         out_specs=vmem,
         compiler_params=pltpu.CompilerParams(vmem_limit_bytes=40 * 2**20),
         name="finish",
-    )(parts)
+    )(live, parts)
+
+
+def prepare_kernel(place, live, blocks, own, sent):
+    step = pl.program_id(0)
+    x, c, slab = place[0], place[1], place[2]
+    base = pl.multiple_of((slab // 4) * 128, 128)
+    column = lax.broadcasted_iota(jnp.int32, (SLAB, 128), 1)
+    pick = column == lax.rem(slab, 4) * SLAB + lax.broadcasted_iota(jnp.int32, (SLAB, 128), 0)
+    for e in range(4):
+        chosen = jnp.where(pick & (live[4 * step + e] > 0), 1.0, 0.0).astype(BF)
+        part = lax.dot_general(
+            chosen,
+            blocks[e, :, pl.ds(base, 128)],
+            (((1,), (1,)), ((), ())),
+            preferred_element_type=F32,
+        )
+        own[e * SLAB : e * SLAB + SLAB, :] = part.astype(BF)
+
+    @pl.when(step // 2 == c)
+    def _():
+        for e in range(4):
+            kept = jnp.where(live[4 * step + e] > 0, blocks[e], jnp.zeros((BS, BS), BF))
+            sent[lax.rem(x + e, 4), lax.rem(step, 2)] = kept
+
+
+def prepare(place, live, blocks):
+    smem = pl.BlockSpec(memory_space=pltpu.SMEM)
+    return pl.pallas_call(
+        prepare_kernel,
+        grid=(4,),
+        out_shape=(
+            jax.ShapeDtypeStruct((ROWS, BS), BF),
+            jax.ShapeDtypeStruct((4, 2, BS, BS), BF),
+        ),
+        in_specs=[smem, smem, pl.BlockSpec((4, BS, BS), lambda q: (q, 0, 0))],
+        out_specs=(
+            pl.BlockSpec((4 * SLAB, BS), lambda q: (q, 0)),
+            pl.BlockSpec((4, 2, BS, BS), lambda q: (0, 0, 0, 0)),
+        ),
+        compiler_params=pltpu.CompilerParams(vmem_limit_bytes=40 * 2**20),
+        name="prepare",
+    )(place, live, blocks)
 
 
 def band_window(own):
@@ -123,30 +161,28 @@
     row = z * NX + x
     listed = lax.dynamic_slice_in_dim(columns, row, 1, 0)
     target = (row + jnp.arange(BAND, dtype=jnp.int32) - BAND // 2) % NB
-    live = jnp.any(listed == target[:, None], axis=1)[:, None, None]
-    place = jnp.stack([x, c]).astype(jnp.int32)
+    live = jnp.any(listed == target[:, None], axis=1)
+    live_flags = live.astype(jnp.int32)
+    live = live[:, None, None]
+    place = jnp.stack([x, c, y * NC + c]).astype(jnp.int32)
 
-    masked = jnp.where(live, blocks[0], jnp.zeros_like(blocks[0]))
-    slab = y * NC + c
-    pick = (jnp.arange(BS)[None, :] == slab * SLAB + jnp.arange(SLAB)[:, None]).astype(BF)
-    own = jnp.einsum("pn,skn->spk", pick, masked, preferred_element_type=F32)
-    own = own.astype(BF).reshape(ROWS, BS)
+    own, sent = prepare(place, live_flags, blocks[0])
+    left_a = lax.all_to_all(sent, "x", 0, 0, tiled=True)
+    window = band_window(own)
+    first = tuple(window[k] for k in (1, 2, 3, 4))
+    left_a, first = lax.optimization_barrier((left_a, first))
+    window = tuple(dict(zip((1, 2, 3, 4), first)).get(k, part) for k, part in enumerate(window))
+    left_b = shift(left_a, "core", 1)
+    left = (left_a, left_b)
 
-    quarters = masked.reshape(4, 4, BS, BS)
-    half = lax.dynamic_slice_in_dim(quarters, 2 * c, 2, 0)
-    left_a = jnp.stack([shift(half[:, e], "x", e) for e in (1, 2, 3)])
-    left_b = shift(left_a, "core", 1)
-    left = (quarters[:, 0], left_a, left_b)
-
-    terms = band_terms(place, band_window(own), left, False)
+    terms = band_terms(place, window, left, False)
     parts = lax.all_to_all(terms, "x", 0, 0, tiled=True)
     square = jnp.sum(parts.astype(F32), axis=0).reshape(BAND, SLAB, BS)
     square = jnp.where(live, square, 0.0).astype(BF).reshape(ROWS, BS)
 
     terms = band_terms(place, band_window(square), left, True)
     parts = lax.all_to_all(terms, ("x", "y", "core"), 0, 0, tiled=True)
-    result = finish(parts.reshape(4, 8, 128, 128))
-    return jnp.where(live, result, 0.0)[None]
+    return finish(live_flags, parts.reshape(4, 8, 128, 128))[None]
 
 
 def solution(mesh):

time: 132 us -> 120 us (0.909)
  waiting for transfers between devices: 37.3 us -> 29.9 us
  starting transfers between devices: 53.7 us -> 48.3 us
  Pallas kernels: 5.48 us -> 9.35 us
  other arithmetic: 4.4 us -> 1.89 us
  matrix products: 2.37 us -> 0 us
  blocking collectives: 25.1 us -> 27.1 us
    ppermute x12 -> x9, starting transfers between devices: 50.1 us -> 35.4 us  [shift(): lax.ppermute(value, axis, [(s, (s + steps) % count) for s in range(count)])]
    ppermute x12 -> x9, waiting for transfers between devices: 24 us -> 15.4 us  [shift(): lax.ppermute(value, axis, [(s, (s + steps) % count) for s in range(count)])]
    all_to_all x0 -> x1, starting transfers between devices: none -> 4.84 us  [per_device(): left_a = lax.all_to_all(sent, 'x', 0, 0, tiled=True)]
    all_to_all x1, starting transfers between devices: 3.51 us -> 8.02 us  [per_device(): parts = lax.all_to_all(terms, 'x', 0, 0, tiled=True)]
    pallas_call x0 -> x1, Pallas kernels: none -> 2.53 us  [prepare(): pl.pallas_call(prepare_kernel, grid=(4,), out_shape=(jax.ShapeDtypeStruct...]
    dot_general x1 -> x0, matrix products: 2.37 us -> none  [per_device(): own = jnp.einsum('pn,skn->spk', pick, masked, preferred_element_type=F32)]
    all_to_all x1, blocking collectives: 25.1 us -> 27.1 us  [per_device(): parts = lax.all_to_all(terms, ('x', 'y', 'core'), 0, 0, tiled=True)]
    select_n x1 -> x0, other arithmetic: 1.8 us -> none  [per_device(): masked = jnp.where(live, blocks[0], jnp.zeros_like(blocks[0]))]
  transfers between devices with their start and end apart: 13 -> 11, of which waited for: 7 -> 6; matrix products, arithmetic and copies ran while one was open for 3% -> 0% of each run, Pallas kernels for 0% -> 0%
where the time goes in v2:
time: 120 us; the launch traced here: 119 us
  starting transfers between devices  48.3 us (40%)
  waiting for transfers between devices  29.9 us (25%)
  blocking collectives  27.1 us (23%)
  Pallas kernels  9.35 us (8%)
  local copies, waits for them, and re-layouts  2.75 us (2%)
  other arithmetic  1.89 us (2%)
    ppermute x9, starting transfers between devices, shift(): lax.ppermute(value, axis, [(s, (s + steps) % count) for s in range(count)])  35.4 us
    all_to_all x1, blocking collectives, per_device(): parts = lax.all_to_all(terms, ('x', 'y', 'core'), 0, 0, tiled=True)  27.1 us
    ppermute x9, waiting for transfers between devices, shift(): lax.ppermute(value, axis, [(s, (s + steps) % count) for s in range(count)])  15.4 us
    all_to_all x1, waiting for transfers between devices, per_device(): parts = lax.all_to_all(terms, 'x', 0, 0, tiled=True)  14.5 us
    all_to_all x1, starting transfers between devices, per_device(): parts = lax.all_to_all(terms, 'x', 0, 0, tiled=True)  8.02 us
    pallas_call x2, Pallas kernels, band_terms(): pl.pallas_call(functools.partial(band_kernel, last), out_shape=jax.ShapeD...  5.27 us
    all_to_all x1, starting transfers between devices, per_device(): left_a = lax.all_to_all(sent, 'x', 0, 0, tiled=True)  4.84 us
    pallas_call x1, Pallas kernels, prepare(): pl.pallas_call(prepare_kernel, grid=(4,), out_shape=(jax.ShapeDtypeStruct...  2.53 us
  transfers between devices with their start and end apart: 11, of which 6 were waited for; matrix products, arithmetic and copies ran while one was open for 0% of the time, Pallas kernels for 0%

profile of v2, /device:TPU:1, one launch (start us, length us, event | category | flops | bytes accessed | tf_op | source)
XLA Modules:
  0.0 119.5 jit_solution(7589839823021400897)
XLA Ops:
  0.0 0.0 copy-start
  0.0 0.7 copy-done
  0.7 0.2 dynamic-slice_reduce_fusion
  0.9 0.2 compare_reduce_fusion
  1.1 0.1 pad_add_fusion.place
  1.2 0.0 copy-start.1
  1.2 1.6 %copy-done.1 = bf16[1,16,256,256]{3,2,1,0:T(8,128)(2,1)S(1)} copy-done((bf16[1,16,256,256]{3,2,1,0:T(8,128)(2,1)S(1)}, bf16[1,16,256,256]{3,2,1,0:T(8,128)(2,1)}, u32[]{:S(2)}) %copy-start.1) | copy-done | bytes 2097176
  2.8 2.5 %prepare.1 = (bf16[512,256]{1,0:T(8,128)(2,1)S(1)}, bf16[4,2,256,256]{3,2,1,0:T(8,128)(2,1)}) custom-call(s32[3]{0:T(128)S(1)} %pad_add_fusion.place, s32[16]{0:T(128)S(1)} %convert_element_type.12.live, bf16[16,256,256]{2,1,0:T(8,128)(2,1)S(1)} %bitcast.12), custom_call_target="tpu_custom_call" | custom-call | tf_op jit(solution)/shard_map/prepare/pallas_call | solution.py:134
  5.3 4.8 %all-to-all-start = ((bf16[4,2,256,256]{3,2,1,0:T(8,128)(2,1)}), bf16[4,2,256,256]{3,2,1,0:T(8,128)(2,1)S(1)}, u32[]{:S(2)}, u32[]{:S(2)}) async-start(bf16[4,2,256,256]{3,2,1,0:T(8,128)(2,1)} %get-tuple-element.13), calls=%async_computation | async-start | bytes 2097152 | tf_op jit(solution)/shard_map/all_to_all | solution.py:170
  10.2 11.1 %collective-permute-start = (bf16[480,256]{1,0:T(8,128)(2,1)S(1)}, bf16[480,256]{1,0:T(8,128)(2,1)S(1)}, u32[]{:S(2)}, u32[]{:S(2)}) collective-permute-start(bf16[480,256]{1,0:T(8,128)(2,1)S(1)} %get-tuple-element.26), channel_id=1, source_target_pairs={{0,480},{32,0},{64,32},{96,64},{128,96},{160,128},{192,160},{224,1... | collective-permute-start | bytes 737288 | tf_op jit(solution)/shard_map/ppermute | solution.py:23
  21.3 1.9 %collective-permute-start.2 = (bf16[480,256]{1,0:T(8,128)(2,1)S(1)}, bf16[480,256]{1,0:T(8,128)(2,1)S(1)}, u32[]{:S(2)}, u32[]{:S(2)}) collective-permute-start(bf16[480,256]{1,0:T(8,128)(2,1)S(1)} %get-tuple-element.25), channel_id=1, source_target_pairs={{0,32},{32,64},{64,96},{96,128},{128,160},{160,192},{192,224},{224... | collective-permute-start | bytes 737288 | tf_op jit(solution)/shard_map/ppermute | solution.py:23
  23.3 3.8 %collective-permute-start.1 = (bf16[352,256]{1,0:T(8,128)(2,1)S(1)}, bf16[352,256]{1,0:T(8,128)(2,1)S(1)}, u32[]{:S(2)}, u32[]{:S(2)}) collective-permute-start(bf16[352,256]{1,0:T(8,128)(2,1)S(1)} %get-tuple-element.24), channel_id=1, source_target_pairs={{0,448},{32,480},{64,0},{96,32},{128,64},{160,96},{192,128},{224,1... | collective-permute-start | bytes 540680 | tf_op jit(solution)/shard_map/ppermute | solution.py:23
  27.1 2.4 %collective-permute-start.3 = (bf16[352,256]{1,0:T(8,128)(2,1)S(1)}, bf16[352,256]{1,0:T(8,128)(2,1)S(1)}, u32[]{:S(2)}, u32[]{:S(2)}) collective-permute-start(bf16[352,256]{1,0:T(8,128)(2,1)S(1)} %get-tuple-element.23), channel_id=1, source_target_pairs={{0,64},{32,96},{64,128},{96,160},{128,192},{160,224},{192,256},{22... | collective-permute-start | bytes 540680 | tf_op jit(solution)/shard_map/ppermute | solution.py:23
  29.5 2.9 %collective-permute-done.1.up2 = bf16[352,256]{1,0:T(8,128)(2,1)S(1)} collective-permute-done((bf16[352,256]{1,0:T(8,128)(2,1)S(1)}, bf16[352,256]{1,0:T(8,128)(2,1)S(1)}, u32[]{:S(2)}, u32[]{:S(2)}) %collective-permute-start.1) | collective-permute-done | bytes 180256 | tf_op jit(solution)/shard_map/ppermute | solution.py:23
  32.4 3.2 %collective-permute-done.3.down2 = bf16[352,256]{1,0:T(8,128)(2,1)S(1)} collective-permute-done((bf16[352,256]{1,0:T(8,128)(2,1)S(1)}, bf16[352,256]{1,0:T(8,128)(2,1)S(1)}, u32[]{:S(2)}, u32[]{:S(2)}) %collective-permute-start.3) | collective-permute-done | bytes 180256 | tf_op jit(solution)/shard_map/ppermute | solution.py:23
  35.5 0.0 collective-permute-done.up1
  35.6 0.0 collective-permute-done.2.down1
  35.6 0.0 all-to-all-done.left_a
  35.6 4.8 %collective-permute-start.4 = (bf16[4,2,256,256]{3,2,1,0:T(8,128)(2,1)S(1)}, bf16[4,2,256,256]{3,2,1,0:T(8,128)(2,1)S(1)}, u32[]{:S(2)}, u32[]{:S(2)}) collective-permute-start(bf16[4,2,256,256]{3,2,1,0:T(8,128)(2,1)S(1)} %all-to-all-done.left_a), channel_id=1, source_target_pairs={{0,1},{1,0},{2,3},{3,2},{4,5},{5,4},{6,7},{7,6},{8,9},{9,8},{10,11... | collective-permute-start | bytes 3145736 | tf_op jit(solution)/shard_map/ppermute | solution.py:23
  40.3 2.3 %collective-permute-done.4.left_b = bf16[4,2,256,256]{3,2,1,0:T(8,128)(2,1)S(1)} collective-permute-done((bf16[4,2,256,256]{3,2,1,0:T(8,128)(2,1)S(1)}, bf16[4,2,256,256]{3,2,1,0:T(8,128)(2,1)S(1)}, u32[]{:S(2)}, u32[]{:S(2)}) %collective-permute-start.4) | collective-permute-done | bytes 1048608 | tf_op jit(solution)/shard_map/ppermute | solution.py:23
  42.6 2.9 %square_terms.1 = bf16[4,512,256]{2,1,0:T(8,128)(2,1)} custom-call(s32[3]{0:T(128)S(1)} %pad_add_fusion.place, bf16[512,256]{1,0:T(8,128)(2,1)S(1)} %get-tuple-element.12.own, bf16[480,256]{1,0:T(8,128)(2,1)S(1)} %collective-permute-done.up1, bf16[352,256]{1,0:T(8,128)(2,1)S(1)} %collective-permute-done.1.up2, ...), custom_call_target="tpu_custom_call" | custom-call | flops 1073741824 | bytes 6291456 | tf_op jit(solution)/shard_map/square_terms/pallas_call | solution.py:69
  45.5 8.0 %all-to-all-start.1 = ((bf16[4,512,256]{2,1,0:T(8,128)(2,1)}), bf16[4,512,256]{2,1,0:T(8,128)(2,1)}, u32[]{:S(2)}, u32[]{:S(2)}) async-start(bf16[4,512,256]{2,1,0:T(8,128)(2,1)} %square_terms.1), calls=%async_computation.1 | async-start | bytes 2097152 | tf_op jit(solution)/shard_map/all_to_all | solution.py:179
  53.5 0.1 broadcast_in_dim.25
  53.6 0.1 broadcast_in_dim.26
  53.7 14.5 %all-to-all-done.1 = bf16[4,512,256]{2,1,0:T(8,128)(2,1)} async-done(((bf16[4,512,256]{2,1,0:T(8,128)(2,1)}), bf16[4,512,256]{2,1,0:T(8,128)(2,1)}, u32[]{:S(2)}, u32[]{:S(2)}) %all-to-all-start.1) | async-done | bytes 1048608 | tf_op jit(solution)/shard_map/all_to_all | solution.py:179
  68.2 1.4 %convert_reduce_fusion = bf16[512,256]{1,0:T(8,128)(2,1)S(1)} fusion(bf16[4,512,256]{2,1,0:T(8,128)(2,1)} %all-to-all-done.1), kind=kLoop, calls=%fused_computation | loop fusion | flops 917504 | bytes 1310720 | tf_op jit(solution)/shard_map/reduce_sum | solution.py:180
  69.5 0.1 select_convert_fusion
  69.7 2.2 %collective-permute-start.5 = (bf16[480,256]{1,0:T(8,128)(2,1)S(1)}, bf16[480,256]{1,0:T(8,128)(2,1)S(1)}, u32[]{:S(2)}, u32[]{:S(2)}) collective-permute-start(bf16[480,256]{1,0:T(8,128)(2,1)S(1)} %bitcast.15), channel_id=1, source_target_pairs={{0,480},{32,0},{64,32},{96,64},{128,96},{160,128},{192,160},{224,1... | collective-permute-start | bytes 737288 | tf_op jit(solution)/shard_map/ppermute | solution.py:23
  71.9 3.1 %collective-permute-start.7 = (bf16[480,256]{1,0:T(8,128)(2,1)S(1)}, bf16[480,256]{1,0:T(8,128)(2,1)S(1)}, u32[]{:S(2)}, u32[]{:S(2)}) collective-permute-start(bf16[480,256]{1,0:T(8,128)(2,1)S(1)} %bitcast.14), channel_id=1, source_target_pairs={{0,32},{32,64},{64,96},{96,128},{128,160},{160,192},{192,224},{224... | collective-permute-start | bytes 737288 | tf_op jit(solution)/shard_map/ppermute | solution.py:23
  75.0 3.7 %collective-permute-start.6 = (bf16[352,256]{1,0:T(8,128)(2,1)S(1)}, bf16[352,256]{1,0:T(8,128)(2,1)S(1)}, u32[]{:S(2)}, u32[]{:S(2)}) collective-permute-start(bf16[352,256]{1,0:T(8,128)(2,1)S(1)} %bitcast.17), channel_id=1, source_target_pairs={{0,448},{32,480},{64,0},{96,32},{128,64},{160,96},{192,128},{224,1... | collective-permute-start | bytes 540680 | tf_op jit(solution)/shard_map/ppermute | solution.py:23
  78.8 2.5 %collective-permute-start.8 = (bf16[352,256]{1,0:T(8,128)(2,1)S(1)}, bf16[352,256]{1,0:T(8,128)(2,1)S(1)}, u32[]{:S(2)}, u32[]{:S(2)}) collective-permute-start(bf16[352,256]{1,0:T(8,128)(2,1)S(1)} %bitcast.16), channel_id=1, source_target_pairs={{0,64},{32,96},{64,128},{96,160},{128,192},{160,224},{192,256},{22... | collective-permute-start | bytes 540680 | tf_op jit(solution)/shard_map/ppermute | solution.py:23
  81.2 0.1 select_convert_fusion.1.own
  81.4 3.0 %collective-permute-done.6.up2 = bf16[352,256]{1,0:T(8,128)(2,1)S(1)} collective-permute-done((bf16[352,256]{1,0:T(8,128)(2,1)S(1)}, bf16[352,256]{1,0:T(8,128)(2,1)S(1)}, u32[]{:S(2)}, u32[]{:S(2)}) %collective-permute-start.6) | collective-permute-done | bytes 180256 | tf_op jit(solution)/shard_map/ppermute | solution.py:23
  84.4 4.0 %collective-permute-done.8.down2 = bf16[352,256]{1,0:T(8,128)(2,1)S(1)} collective-permute-done((bf16[352,256]{1,0:T(8,128)(2,1)S(1)}, bf16[352,256]{1,0:T(8,128)(2,1)S(1)}, u32[]{:S(2)}, u32[]{:S(2)}) %collective-permute-start.8) | collective-permute-done | bytes 180256 | tf_op jit(solution)/shard_map/ppermute | solution.py:23
  88.4 0.0 collective-permute-done.5.up1
  88.4 0.0 collective-permute-done.7.down1
  88.4 2.3 %cube_terms.1 = bf16[32,128,128]{2,1,0:T(8,128)(2,1)S(1)} custom-call(s32[3]{0:T(128)S(1)} %pad_add_fusion.place, bf16[512,256]{1,0:T(8,128)(2,1)S(1)} %select_convert_fusion.1.own, bf16[480,256]{1,0:T(8,128)(2,1)S(1)} %collective-permute-done.5.up1, bf16[352,256]{1,0:T(8,128)(2,1)S(1)} %collective-permute-done.6.up2, ...), custom_call_target="tpu_custom_call" | custom-call | flops 1073741824 | bytes 6291456 | tf_op jit(solution)/shard_map/cube_terms/pallas_call | solution.py:69
  90.8 27.1 %all_to_all.15 = bf16[32,128,128]{2,1,0:T(8,128)(2,1)S(1)} all-to-all(bf16[32,128,128]{2,1,0:T(8,128)(2,1)S(1)} %cube_terms.1), channel_id=1, replica_groups=mesh['z'=16,'x'=4,'y'=4,'core'=2] {'x','y','core'}, dimensions={0} | all-to-all | bytes 2097152 | tf_op jit(solution)/shard_map/all_to_all | solution.py:184
  117.9 1.6 %finish.1 = f32[16,32,256]{2,1,0:T(8,128)} custom-call(s32[16]{0:T(128)S(1)} %convert_element_type.12.live, bf16[4,8,128,128]{3,2,1,0:T(8,128)(2,1)S(1)} %bitcast.11), custom_call_target="tpu_custom_call" | custom-call | tf_op jit(solution)/shard_map/finish/pallas_call | solution.py:99
  (6 shorter events, 0.2 us)
Async XLA Ops:
  0.0 0.7 copy-start
  1.2 1.6 %copy-start.1 = (bf16[1,16,256,256]{3,2,1,0:T(8,128)(2,1)S(1)}, bf16[1,16,256,256]{3,2,1,0:T(8,128)(2,1)}, u32[]{:S(2)}) copy-start(bf16[1,16,256,256]{3,2,1,0:T(8,128)(2,1)} %param.2) | copy-start | bytes 6291460
  5.3 30.3 %all-to-all-start = ((bf16[4,2,256,256]{3,2,1,0:T(8,128)(2,1)}), bf16[4,2,256,256]{3,2,1,0:T(8,128)(2,1)S(1)}, u32[]{:S(2)}, u32[]{:S(2)}) async-start(bf16[4,2,256,256]{3,2,1,0:T(8,128)(2,1)} %get-tuple-element.13), calls=%async_computation | async-start | bytes 2097152 | tf_op jit(solution)/shard_map/all_to_all | solution.py:170
  10.2 25.4 %collective-permute-start = (bf16[480,256]{1,0:T(8,128)(2,1)S(1)}, bf16[480,256]{1,0:T(8,128)(2,1)S(1)}, u32[]{:S(2)}, u32[]{:S(2)}) collective-permute-start(bf16[480,256]{1,0:T(8,128)(2,1)S(1)} %get-tuple-element.26), channel_id=1, source_target_pairs={{0,480},{32,0},{64,32},{96,64},{128,96},{160,128},{192,160},{224,1... | collective-permute-start | bytes 737288 | tf_op jit(solution)/shard_map/ppermute | solution.py:23
  21.3 14.3 %collective-permute-start.2 = (bf16[480,256]{1,0:T(8,128)(2,1)S(1)}, bf16[480,256]{1,0:T(8,128)(2,1)S(1)}, u32[]{:S(2)}, u32[]{:S(2)}) collective-permute-start(bf16[480,256]{1,0:T(8,128)(2,1)S(1)} %get-tuple-element.25), channel_id=1, source_target_pairs={{0,32},{32,64},{64,96},{96,128},{128,160},{160,192},{192,224},{224... | collective-permute-start | bytes 737288 | tf_op jit(solution)/shard_map/ppermute | solution.py:23
  23.3 9.1 %collective-permute-start.1 = (bf16[352,256]{1,0:T(8,128)(2,1)S(1)}, bf16[352,256]{1,0:T(8,128)(2,1)S(1)}, u32[]{:S(2)}, u32[]{:S(2)}) collective-permute-start(bf16[352,256]{1,0:T(8,128)(2,1)S(1)} %get-tuple-element.24), channel_id=1, source_target_pairs={{0,448},{32,480},{64,0},{96,32},{128,64},{160,96},{192,128},{224,1... | collective-permute-start | bytes 540680 | tf_op jit(solution)/shard_map/ppermute | solution.py:23
  27.1 8.5 %collective-permute-start.3 = (bf16[352,256]{1,0:T(8,128)(2,1)S(1)}, bf16[352,256]{1,0:T(8,128)(2,1)S(1)}, u32[]{:S(2)}, u32[]{:S(2)}) collective-permute-start(bf16[352,256]{1,0:T(8,128)(2,1)S(1)} %get-tuple-element.23), channel_id=1, source_target_pairs={{0,64},{32,96},{64,128},{96,160},{128,192},{160,224},{192,256},{22... | collective-permute-start | bytes 540680 | tf_op jit(solution)/shard_map/ppermute | solution.py:23
  35.6 7.0 %collective-permute-start.4 = (bf16[4,2,256,256]{3,2,1,0:T(8,128)(2,1)S(1)}, bf16[4,2,256,256]{3,2,1,0:T(8,128)(2,1)S(1)}, u32[]{:S(2)}, u32[]{:S(2)}) collective-permute-start(bf16[4,2,256,256]{3,2,1,0:T(8,128)(2,1)S(1)} %all-to-all-done.left_a), channel_id=1, source_target_pairs={{0,1},{1,0},{2,3},{3,2},{4,5},{5,4},{6,7},{7,6},{8,9},{9,8},{10,11... | collective-permute-start | bytes 3145736 | tf_op jit(solution)/shard_map/ppermute | solution.py:23
  45.5 22.7 %all-to-all-start.1 = ((bf16[4,512,256]{2,1,0:T(8,128)(2,1)}), bf16[4,512,256]{2,1,0:T(8,128)(2,1)}, u32[]{:S(2)}, u32[]{:S(2)}) async-start(bf16[4,512,256]{2,1,0:T(8,128)(2,1)} %square_terms.1), calls=%async_computation.1 | async-start | bytes 2097152 | tf_op jit(solution)/shard_map/all_to_all | solution.py:179
  69.7 18.7 %collective-permute-start.5 = (bf16[480,256]{1,0:T(8,128)(2,1)S(1)}, bf16[480,256]{1,0:T(8,128)(2,1)S(1)}, u32[]{:S(2)}, u32[]{:S(2)}) collective-permute-start(bf16[480,256]{1,0:T(8,128)(2,1)S(1)} %bitcast.15), channel_id=1, source_target_pairs={{0,480},{32,0},{64,32},{96,64},{128,96},{160,128},{192,160},{224,1... | collective-permute-start | bytes 737288 | tf_op jit(solution)/shard_map/ppermute | solution.py:23
  71.9 16.5 %collective-permute-start.7 = (bf16[480,256]{1,0:T(8,128)(2,1)S(1)}, bf16[480,256]{1,0:T(8,128)(2,1)S(1)}, u32[]{:S(2)}, u32[]{:S(2)}) collective-permute-start(bf16[480,256]{1,0:T(8,128)(2,1)S(1)} %bitcast.14), channel_id=1, source_target_pairs={{0,32},{32,64},{64,96},{96,128},{128,160},{160,192},{192,224},{224... | collective-permute-start | bytes 737288 | tf_op jit(solution)/shard_map/ppermute | solution.py:23
  75.0 9.4 %collective-permute-start.6 = (bf16[352,256]{1,0:T(8,128)(2,1)S(1)}, bf16[352,256]{1,0:T(8,128)(2,1)S(1)}, u32[]{:S(2)}, u32[]{:S(2)}) collective-permute-start(bf16[352,256]{1,0:T(8,128)(2,1)S(1)} %bitcast.17), channel_id=1, source_target_pairs={{0,448},{32,480},{64,0},{96,32},{128,64},{160,96},{192,128},{224,1... | collective-permute-start | bytes 540680 | tf_op jit(solution)/shard_map/ppermute | solution.py:23
  78.8 9.7 %collective-permute-start.8 = (bf16[352,256]{1,0:T(8,128)(2,1)S(1)}, bf16[352,256]{1,0:T(8,128)(2,1)S(1)}, u32[]{:S(2)}, u32[]{:S(2)}) collective-permute-start(bf16[352,256]{1,0:T(8,128)(2,1)S(1)} %bitcast.16), channel_id=1, source_target_pairs={{0,64},{32,96},{64,128},{96,160},{128,192},{160,224},{192,256},{22... | collective-permute-start | bytes 540680 | tf_op jit(solution)/shard_map/ppermute | solution.py:23

commit v3 on v1

v3 whole, which is shorter than its diff:
```python
import functools

import jax
import jax.numpy as jnp
from jax import lax
from jax.experimental import pallas as pl
from jax.experimental.pallas import tpu as pltpu
from jax.sharding import Mesh
from jax.sharding import PartitionSpec as P

BS = 256
BAND = 16
NB = 64
NZ, NX, NY, NC = 16, 4, 4, 2
SLAB = 32
ROWS = BAND * SLAB
BF = jnp.bfloat16
F32 = jnp.float32
MINE = NX + 2


READ = ((0, 15), (0, 11), (1, 16), (5, 16))
HOPS = (-1, -2, 1, 2)
OUTGOING = tuple(jax.ShapeDtypeStruct(((hi - lo) * SLAB, BS), BF) for lo, hi in READ)


def shift(value, axis, steps):
    count = lax.axis_size(axis)
    return lax.ppermute(value, axis, [(s, (s + steps) % count) for s in range(count)])


def band_kernel(last, flags, own, up1, up2, down1, down2, left, out, padded):
    x = lax.axis_index("x")
    edge = 8 * SLAB
    for dz in range(5):
        padded[dz, :edge, :] = jnp.zeros((edge, BS), BF)
        padded[dz, 3 * edge :, :] = jnp.zeros((edge, BS), BF)
    padded[5] = jnp.zeros((4 * edge, BS), BF)
    for dz, part, (lo, hi) in zip(
        (2, 3, 4, 1, 0), (own, up1, up2, down1, down2), ((0, BAND), *READ)
    ):
        if last:
            padded[dz, edge + lo * SLAB : edge + hi * SLAB, :] = part[...]
            continue
        for slot in range(lo, hi):
            piece = part[(slot - lo) * SLAB : (slot - lo + 1) * SLAB, :]
            piece = jnp.where(flags[4 + dz, slot] > 0, piece, jnp.zeros((SLAB, BS), BF))
            padded[dz, edge + slot * SLAB : edge + (slot + 1) * SLAB, :] = piece
    contract = (((1,), (1,)), ((), ()))
    for e in range(4):
        wrapped = jnp.where(x < e, 1, 0)
        target = lax.rem(x - e + 4, 4)
        total = None
        for q in range(4):
            start = (16 - e - 4 * q) * SLAB
            plane = jnp.where(flags[target, 4 * q + e] > 0, q + wrapped, 5)
            rows = padded[plane, start : start + ROWS, :]
            term = lax.dot_general(rows, left[target, q], contract, preferred_element_type=F32)
            total = term if total is None else total + term
        if last and e == 0:
            total = total - 1.5 * own[...].astype(F32)
        if not last:
            out[target] = total.astype(BF)
            continue
        for h in range(2):
            lane = lax.broadcasted_iota(jnp.int32, (128, 128), 1) // SLAB
            for g in range(4):
                packed = None
                for sh in range(4):
                    piece = total[sh * 128 : sh * 128 + 128, h * 128 : h * 128 + 128]
                    if sh != g:
                        piece = pltpu.roll(piece, ((sh - g) % 4) * SLAB, 1)
                    packed = piece if packed is None else jnp.where(lane == sh, piece, packed)
                out[target * 8 + h * 4 + g] = packed.astype(BF)


def band_terms(flags, window, left, last):
    shape = (32, 128, 128) if last else (4, ROWS, BS)
    vmem = pl.BlockSpec(memory_space=pltpu.VMEM)
    return pl.pallas_call(
        functools.partial(band_kernel, last),
        out_shape=jax.ShapeDtypeStruct(shape, BF),
        in_specs=[pl.BlockSpec(memory_space=pltpu.SMEM)] + [vmem] * 6,
        out_specs=vmem,
        scratch_shapes=[pltpu.VMEM((6, 4 * 8 * SLAB, BS), BF)],
        compiler_params=pltpu.CompilerParams(vmem_limit_bytes=40 * 2**20),
        cost_estimate=pl.CostEstimate(
            flops=2 * 16 * ROWS * BS * BS, bytes_accessed=6 * 2**20, transcendentals=0
        ),
        name="cube_terms" if last else "square_terms",
    )(flags, *window, left)


def finish_kernel(flags, parts, out):
    total = parts[0].astype(F32)
    for x in range(1, 4):
        total = total + parts[x].astype(F32)
    total = -2.0 * total
    for lo in range(4):
        tile = total[:, lo * SLAB : lo * SLAB + SLAB, :].reshape(BS, 128)
        flat = tile.T
        for hi in range(4):
            slot = hi * 4 + lo
            piece = flat[hi * SLAB : hi * SLAB + SLAB, :]
            out[slot] = jnp.where(flags[MINE, slot] > 0, piece, 0.0)


def finish(flags, parts):
    vmem = pl.BlockSpec(memory_space=pltpu.VMEM)
    return pl.pallas_call(
        finish_kernel,
        out_shape=jax.ShapeDtypeStruct((BAND, SLAB, BS), F32),
        in_specs=[pl.BlockSpec(memory_space=pltpu.SMEM), vmem],
        out_specs=vmem,
        compiler_params=pltpu.CompilerParams(vmem_limit_bytes=40 * 2**20),
        name="finish",
    )(flags, parts)


def band_window(own, outgoing):
    return (own, *(shift(part, "z", hop) for part, hop in zip(outgoing, HOPS)))


def store_slots(value, first, own, outgoing):
    count = value.shape[0] // SLAB
    own[first * SLAB : (first + count) * SLAB, :] = value
    for part, (lo, hi) in zip(outgoing, READ):
        begin, end = max(lo, first), min(hi, first + count)
        if begin < end:
            part[(begin - lo) * SLAB : (end - lo) * SLAB, :] = value[
                (begin - first) * SLAB : (end - first) * SLAB, :
            ]


def prepare_kernel(blocks, own, o1, o2, o3, o4, sent, held, move_sems, load_sems):
    x = lax.axis_index("x")
    slab = lax.axis_index("y") * NC + lax.axis_index("core")
    base = pl.multiple_of((slab // 4) * 128, 128)
    loads = [
        pltpu.make_async_copy(blocks.at[pl.ds(4 * q, 4)], held.at[q], load_sems.at[q])
        for q in range(4)
    ]
    for copy in loads:
        copy.start()
    moves = [
        pltpu.make_async_copy(
            held.at[q, e], sent.at[lax.rem(x + e, 4), q], move_sems.at[4 * q + e]
        )
        for q in range(4)
        for e in range(4)
    ]
    line = lax.broadcasted_iota(jnp.int32, (128, 128), 0) - lax.rem(slab, 4) * SLAB
    column = lax.broadcasted_iota(jnp.int32, (128, 128), 1)
    inside = (line >= 0) & (line < SLAB)
    picks = [
        jnp.where(inside & (column == line + e * SLAB), 1.0, 0.0).astype(BF) for e in range(4)
    ]
    for q in range(4):
        loads[q].wait()
        for e in range(4):
            moves[4 * q + e].start()
        total = None
        for e in range(4):
            part = jnp.dot(
                held[q, e, :, pl.ds(base, 128)], picks[e], preferred_element_type=F32
            )
            total = part if total is None else total + part
        store_slots(total.T.astype(BF), 4 * q, own, (o1, o2, o3, o4))
    for copy in moves:
        copy.wait()


def prepare(blocks):
    vmem = pl.BlockSpec(memory_space=pltpu.VMEM)
    anywhere = pl.BlockSpec(memory_space=pl.ANY)
    return pl.pallas_call(
        prepare_kernel,
        out_shape=(
            jax.ShapeDtypeStruct((ROWS, BS), BF),
            *OUTGOING,
            jax.ShapeDtypeStruct((4, 4, BS, BS), BF),
        ),
        in_specs=[anywhere],
        out_specs=(*(vmem,) * 5, anywhere),
        scratch_shapes=[
            pltpu.VMEM((4, 4, BS, BS), BF),
            pltpu.SemaphoreType.DMA((16,)),
            pltpu.SemaphoreType.DMA((4,)),
        ],
        compiler_params=pltpu.CompilerParams(vmem_limit_bytes=56 * 2**20),
        name="prepare",
    )(blocks)


def gather_kernel(flags, parts, own, o1, o2, o3, o4):
    for slot in range(BAND):
        piece = parts[0, slot * SLAB : slot * SLAB + SLAB, :].astype(F32)
        for x in range(1, 4):
            piece = piece + parts[x, slot * SLAB : slot * SLAB + SLAB, :].astype(F32)
        piece = jnp.where(flags[MINE, slot] > 0, piece, 0.0).astype(BF)
        store_slots(piece, slot, own, (o1, o2, o3, o4))


def gather_square(flags, parts):
    vmem = pl.BlockSpec(memory_space=pltpu.VMEM)
    return pl.pallas_call(
        gather_kernel,
        out_shape=(jax.ShapeDtypeStruct((ROWS, BS), BF), *OUTGOING),
        in_specs=[pl.BlockSpec(memory_space=pltpu.SMEM), vmem],
        out_specs=(vmem,) * 5,
        compiler_params=pltpu.CompilerParams(vmem_limit_bytes=40 * 2**20),
        name="gather_square",
    )(flags, parts)


def per_device(blocks, columns):
    own, *outgoing, sent = prepare(blocks[0])
    left = lax.all_to_all(sent, "x", 0, 0, tiled=True)
    own, *around = band_window(own, outgoing)
    left, around = lax.optimization_barrier((left, around))

    z, x = lax.axis_index("z"), lax.axis_index("x")
    rows = jnp.concatenate(
        [NX * z + jnp.arange(NX), NX * (z + jnp.arange(-2, 3)) + x]
    ).astype(jnp.int32) % NB
    listed = columns[rows]
    target = (rows[:, None] + jnp.arange(BAND, dtype=jnp.int32) - BAND // 2) % NB
    flags = jnp.any(listed[:, None, :] == target[:, :, None], axis=2).astype(jnp.int32)

    terms = band_terms(flags, (own, *around), left, False)
    parts = lax.all_to_all(terms, "x", 0, 0, tiled=True)
    own, *outgoing = gather_square(flags, parts)
    terms = band_terms(flags, band_window(own, outgoing), left, True)
    parts = lax.all_to_all(terms, ("x", "y", "core"), 0, 0, tiled=True)
    return finish(flags, parts.reshape(4, 8, 128, 128))[None]


def solution(mesh):
    grid = Mesh(mesh.devices.reshape(NZ, NX, NY, NC), ("z", "x", "y", "core"))
    return jax.shard_map(
        per_device,
        mesh=grid,
        in_specs=(P(("z", "x"), None, None, None), P()),
        out_specs=P(("z", "x"), None, ("y", "core"), None),
        check_vma=False,
    )
```

time: 132 us -> 112 us (0.85)
  waiting for transfers between devices: 37.3 us -> 11.4 us
  blocking collectives: 25.1 us -> 42.1 us
  starting transfers between devices: 53.7 us -> 45.2 us
  Pallas kernels: 5.48 us -> 11.1 us
  other arithmetic: 4.4 us -> 0.62 us
  matrix products: 2.37 us -> 0 us
  local copies, waits for them, and re-layouts: 2.53 us -> 0.66 us
    all_to_all x0 -> x1, blocking collectives: none -> 13.5 us  [per_device(): parts = lax.all_to_all(terms, 'x', 0, 0, tiled=True)]
    all_to_all x1, waiting for transfers between devices: 13.3 us -> 0.01 us  [per_device(): left = lax.all_to_all(sent, 'x', 0, 0, tiled=True)]
    ppermute x12 -> x8, waiting for transfers between devices: 24 us -> 11.4 us  [shift(): lax.ppermute(value, axis, [(s, (s + steps) % count) for s in range(count)])]
    ppermute x12 -> x8, starting transfers between devices: 50.1 us -> 40.2 us  [shift(): lax.ppermute(value, axis, [(s, (s + steps) % count) for s in range(count)])]
    pallas_call x0 -> x2, Pallas kernels: none -> 4.92 us  [the longest x1 4.1 us: prepare(): pl.pallas_call(prepare_kernel, out_shape=(jax.ShapeDtypeStruct((ROWS, BS)...]
    all_to_all x1, blocking collectives: 25.1 us -> 28.6 us  [per_device(): parts = lax.all_to_all(terms, ('x', 'y', 'core'), 0, 0, tiled=True)]
    dot_general x1 -> x0, matrix products: 2.37 us -> none  [per_device(): own = jnp.einsum('pn,skn->spk', pick, masked, preferred_element_type=F32)]
    select_n x2 -> x3, other arithmetic: 1.81 us -> 0.25 us  [the longest x1 0.08 us: per_device(): jnp.concatenate([NX * z + jnp.arange(NX), NX * (z + jnp.arange(-2, 3)) + x])]
  transfers between devices with their start and end apart: 13 -> 9, of which waited for: 7 -> 4; matrix products, arithmetic and copies ran while one was open for 3% -> 1% of each run, Pallas kernels for 0% -> 0%
where the time goes in v3:
time: 112 us; the launch traced here: 111 us
  starting transfers between devices  45.2 us (40%)
  blocking collectives  42.1 us (38%)
  waiting for transfers between devices  11.4 us (10%)
  Pallas kernels  11.1 us (10%)
    ppermute x8, starting transfers between devices, shift(): lax.ppermute(value, axis, [(s, (s + steps) % count) for s in range(count)])  40.2 us
    all_to_all x1, blocking collectives, per_device(): parts = lax.all_to_all(terms, ('x', 'y', 'core'), 0, 0, tiled=True)  28.6 us
    all_to_all x1, blocking collectives, per_device(): parts = lax.all_to_all(terms, 'x', 0, 0, tiled=True)  13.5 us
    ppermute x8, waiting for transfers between devices, shift(): lax.ppermute(value, axis, [(s, (s + steps) % count) for s in range(count)])  11.4 us
    all_to_all x1, starting transfers between devices, per_device(): left = lax.all_to_all(sent, 'x', 0, 0, tiled=True)  4.97 us
    pallas_call x2, Pallas kernels, band_terms(): pl.pallas_call(functools.partial(band_kernel, last), out_shape=jax.ShapeD...  4.51 us
    pallas_call x1, Pallas kernels, prepare(): pl.pallas_call(prepare_kernel, out_shape=(jax.ShapeDtypeStruct((ROWS, BS)...  4.1 us
  transfers between devices with their start and end apart: 9, of which 4 were waited for; matrix products, arithmetic and copies ran while one was open for 1% of the time, Pallas kernels for 0%

profile of v3, /device:TPU:1, one launch (start us, length us, event | category | flops | bytes accessed | tf_op | source)
XLA Modules:
  0.0 111.2 jit_solution(1926219232362214715)
XLA Ops:
  0.0 4.1 %prepare.1 = (bf16[512,256]{1,0:T(8,128)(2,1)}, bf16[480,256]{1,0:T(8,128)(2,1)}, bf16[352,256]{1,0:T(8,128)(2,1)}, bf16[480,256]{1,0:T(8,128)(2,1)}, bf16[352,2...) custom-call(bf16[16,256,256]{2,1,0:T(8,128)(2,1)} %bitcast.10), custom_call_target="tpu_custom_call" | custom-call | tf_op jit(solution)/shard_map/prepare/pallas_call | solution.py:176
  4.1 0.0 copy-start.2
  4.1 0.0 copy-start.1
  4.1 0.0 copy-start
  4.1 5.0 %all-to-all-start = ((bf16[4,4,256,256]{3,2,1,0:T(8,128)(2,1)}), bf16[4,4,256,256]{3,2,1,0:T(8,128)(2,1)S(1)}, u32[]{:S(2)}, u32[]{:S(2)}) async-start(bf16[4,4,256,256]{3,2,1,0:T(8,128)(2,1)} %get-tuple-element.22), calls=%async_computation | async-start | bytes 4194304 | tf_op jit(solution)/shard_map/all_to_all | solution.py:218
  9.1 11.1 %collective-permute-start = (bf16[480,256]{1,0:T(8,128)(2,1)}, bf16[480,256]{1,0:T(8,128)(2,1)S(1)}, u32[]{:S(2)}, u32[]{:S(2)}) collective-permute-start(bf16[480,256]{1,0:T(8,128)(2,1)} %get-tuple-element.23), channel_id=1, source_target_pairs={{0,480},{32,0},{64,32},{96,64},{128,96},{160,128},{192,160},{224,1... | collective-permute-start | bytes 737288 | tf_op jit(solution)/shard_map/ppermute | solution.py:29
  20.2 0.0 copy-done.2
  20.2 1.9 %collective-permute-start.2 = (bf16[480,256]{1,0:T(8,128)(2,1)S(1)}, bf16[480,256]{1,0:T(8,128)(2,1)S(1)}, u32[]{:S(2)}, u32[]{:S(2)}) collective-permute-start(bf16[480,256]{1,0:T(8,128)(2,1)S(1)} %copy-done.2), channel_id=1, source_target_pairs={{0,32},{32,64},{64,96},{96,128},{128,160},{160,192},{192,224},{224... | collective-permute-start | bytes 737288 | tf_op jit(solution)/shard_map/ppermute | solution.py:29
  22.2 3.8 %collective-permute-start.1 = (bf16[352,256]{1,0:T(8,128)(2,1)}, bf16[352,256]{1,0:T(8,128)(2,1)S(1)}, u32[]{:S(2)}, u32[]{:S(2)}) collective-permute-start(bf16[352,256]{1,0:T(8,128)(2,1)} %get-tuple-element.24), channel_id=1, source_target_pairs={{0,448},{32,480},{64,0},{96,32},{128,64},{160,96},{192,128},{224,1... | collective-permute-start | bytes 540680 | tf_op jit(solution)/shard_map/ppermute | solution.py:29
  26.0 2.4 %collective-permute-start.3 = (bf16[352,256]{1,0:T(8,128)(2,1)}, bf16[352,256]{1,0:T(8,128)(2,1)S(1)}, u32[]{:S(2)}, u32[]{:S(2)}) collective-permute-start(bf16[352,256]{1,0:T(8,128)(2,1)} %get-tuple-element.26), channel_id=1, source_target_pairs={{0,64},{32,96},{64,128},{96,160},{128,192},{160,224},{192,256},{22... | collective-permute-start | bytes 540680 | tf_op jit(solution)/shard_map/ppermute | solution.py:29
  28.4 0.1 and_select_fusion
  28.5 0.1 add_select_fusion
  28.6 0.1 fusion.3
  28.7 0.0 copy-done.1
  28.7 0.1 copy.4
  28.8 0.6 gather_fusion
  29.3 0.3 compare_reduce_fusion
  29.7 1.8 %collective-permute-done.1.up2 = bf16[352,256]{1,0:T(8,128)(2,1)S(1)} collective-permute-done((bf16[352,256]{1,0:T(8,128)(2,1)}, bf16[352,256]{1,0:T(8,128)(2,1)S(1)}, u32[]{:S(2)}, u32[]{:S(2)}) %collective-permute-start.1) | collective-permute-done | bytes 180256 | tf_op jit(solution)/shard_map/ppermute | solution.py:29
  31.5 3.4 %collective-permute-done.3.down2 = bf16[352,256]{1,0:T(8,128)(2,1)S(1)} collective-permute-done((bf16[352,256]{1,0:T(8,128)(2,1)}, bf16[352,256]{1,0:T(8,128)(2,1)S(1)}, u32[]{:S(2)}, u32[]{:S(2)}) %collective-permute-start.3) | collective-permute-done | bytes 180256 | tf_op jit(solution)/shard_map/ppermute | solution.py:29
  34.9 0.0 collective-permute-done.up1
  34.9 0.0 collective-permute-done.2.down1
  34.9 0.0 all-to-all-done.left
  34.9 0.0 copy-done
  35.0 2.1 %square_terms.1 = bf16[4,512,256]{2,1,0:T(8,128)(2,1)S(1)} custom-call(s32[9,16]{1,0:T(8,128)S(1)} %convert_element_type.3.flags, bf16[512,256]{1,0:T(8,128)(2,1)S(1)} %copy-done, bf16[480,256]{1,0:T(8,128)(2,1)S(1)} %collective-permute-done.up1, bf16[352,256]{1,0:T(8,128)(2,1)S(1)} %collective-permute-done.1.up2, ...), custom_call_target="tpu_custom_call" | custom-call | flops 1073741824 | bytes 6291456 | tf_op jit(solution)/shard_map/square_terms/pallas_call | solution.py:80
  37.0 13.5 %all_to_all.15.parts = bf16[4,512,256]{2,1,0:T(8,128)(2,1)S(1)} all-to-all(bf16[4,512,256]{2,1,0:T(8,128)(2,1)S(1)} %square_terms.1), channel_id=1, replica_groups=mesh['z'=16,'x'=4,'y'=4,'core'=2] {'x'}, dimensions={0} | all-to-all | bytes 2097152 | tf_op jit(solution)/shard_map/all_to_all | solution.py:231
  50.5 0.8 gather_square.1
  51.4 12.9 %collective-permute-start.4 = (bf16[480,256]{1,0:T(8,128)(2,1)S(1)}, bf16[480,256]{1,0:T(8,128)(2,1)S(1)}, u32[]{:S(2)}, u32[]{:S(2)}) collective-permute-start(bf16[480,256]{1,0:T(8,128)(2,1)S(1)} %get-tuple-element.33), channel_id=1, source_target_pairs={{0,480},{32,0},{64,32},{96,64},{128,96},{160,128},{192,160},{224,1... | collective-permute-start | bytes 737288 | tf_op jit(solution)/shard_map/ppermute | solution.py:29
  64.3 1.9 %collective-permute-start.6 = (bf16[480,256]{1,0:T(8,128)(2,1)S(1)}, bf16[480,256]{1,0:T(8,128)(2,1)S(1)}, u32[]{:S(2)}, u32[]{:S(2)}) collective-permute-start(bf16[480,256]{1,0:T(8,128)(2,1)S(1)} %get-tuple-element.35), channel_id=1, source_target_pairs={{0,32},{32,64},{64,96},{96,128},{128,160},{160,192},{192,224},{224... | collective-permute-start | bytes 737288 | tf_op jit(solution)/shard_map/ppermute | solution.py:29
  66.2 3.8 %collective-permute-start.5 = (bf16[352,256]{1,0:T(8,128)(2,1)S(1)}, bf16[352,256]{1,0:T(8,128)(2,1)S(1)}, u32[]{:S(2)}, u32[]{:S(2)}) collective-permute-start(bf16[352,256]{1,0:T(8,128)(2,1)S(1)} %get-tuple-element.34), channel_id=1, source_target_pairs={{0,448},{32,480},{64,0},{96,32},{128,64},{160,96},{192,128},{224,1... | collective-permute-start | bytes 540680 | tf_op jit(solution)/shard_map/ppermute | solution.py:29
  70.0 2.4 %collective-permute-start.7 = (bf16[352,256]{1,0:T(8,128)(2,1)S(1)}, bf16[352,256]{1,0:T(8,128)(2,1)S(1)}, u32[]{:S(2)}, u32[]{:S(2)}) collective-permute-start(bf16[352,256]{1,0:T(8,128)(2,1)S(1)} %get-tuple-element.36), channel_id=1, source_target_pairs={{0,64},{32,96},{64,128},{96,160},{128,192},{160,224},{192,256},{22... | collective-permute-start | bytes 540680 | tf_op jit(solution)/shard_map/ppermute | solution.py:29
  72.4 2.3 %collective-permute-done.5.up2 = bf16[352,256]{1,0:T(8,128)(2,1)S(1)} collective-permute-done((bf16[352,256]{1,0:T(8,128)(2,1)S(1)}, bf16[352,256]{1,0:T(8,128)(2,1)S(1)}, u32[]{:S(2)}, u32[]{:S(2)}) %collective-permute-start.5) | collective-permute-done | bytes 180256 | tf_op jit(solution)/shard_map/ppermute | solution.py:29
  74.7 3.8 %collective-permute-done.7.down2 = bf16[352,256]{1,0:T(8,128)(2,1)S(1)} collective-permute-done((bf16[352,256]{1,0:T(8,128)(2,1)S(1)}, bf16[352,256]{1,0:T(8,128)(2,1)S(1)}, u32[]{:S(2)}, u32[]{:S(2)}) %collective-permute-start.7) | collective-permute-done | bytes 180256 | tf_op jit(solution)/shard_map/ppermute | solution.py:29
  78.5 0.0 collective-permute-done.4.up1
  78.5 0.0 collective-permute-done.6.down1
  78.5 2.4 %cube_terms.1 = bf16[32,128,128]{2,1,0:T(8,128)(2,1)S(1)} custom-call(s32[9,16]{1,0:T(8,128)S(1)} %convert_element_type.3.flags, bf16[512,256]{1,0:T(8,128)(2,1)S(1)} %get-tuple-element.32.own, bf16[480,256]{1,0:T(8,128)(2,1)S(1)} %collective-permute-done.4.up1, bf16[352,256]{1,0:T(8,128)(2,1)S(1)} %collective-permute-done.5.up2, ...), custom_call_target="tpu_custom_call" | custom-call | flops 1073741824 | bytes 6291456 | tf_op jit(solution)/shard_map/cube_terms/pallas_call | solution.py:80
  80.9 28.6 %all_to_all.16 = bf16[32,128,128]{2,1,0:T(8,128)(2,1)S(1)} all-to-all(bf16[32,128,128]{2,1,0:T(8,128)(2,1)S(1)} %cube_terms.1), channel_id=1, replica_groups=mesh['z'=16,'x'=4,'y'=4,'core'=2] {'x','y','core'}, dimensions={0} | all-to-all | bytes 2097152 | tf_op jit(solution)/shard_map/all_to_all | solution.py:234
  109.5 1.7 %finish.1 = f32[16,32,256]{2,1,0:T(8,128)} custom-call(s32[9,16]{1,0:T(8,128)S(1)} %convert_element_type.3.flags, bf16[4,8,128,128]{3,2,1,0:T(8,128)(2,1)S(1)} %bitcast.9), custom_call_target="tpu_custom_call" | custom-call | tf_op jit(solution)/shard_map/finish/pallas_call | solution.py:110
  (6 shorter events, 0.0 us)
Async XLA Ops:
  4.1 16.1 %copy-start.2 = (bf16[480,256]{1,0:T(8,128)(2,1)S(1)}, bf16[480,256]{1,0:T(8,128)(2,1)}, u32[]{:S(2)}) copy-start(bf16[480,256]{1,0:T(8,128)(2,1)} %get-tuple-element.25) | copy-start | bytes 737284
  4.1 24.6 %copy-start.1 = (s32[64,16]{0,1:T(8,128)S(1)}, s32[64,16]{0,1:T(8,128)}, u32[]{:S(2)}) copy-start(s32[64,16]{0,1:T(8,128)} %param.3) | copy-start | bytes 12292
  4.1 30.8 %copy-start = (bf16[512,256]{1,0:T(8,128)(2,1)S(1)}, bf16[512,256]{1,0:T(8,128)(2,1)}, u32[]{:S(2)}) copy-start(bf16[512,256]{1,0:T(8,128)(2,1)} %get-tuple-element.21.own) | copy-start | bytes 786436
  4.1 30.8 %all-to-all-start = ((bf16[4,4,256,256]{3,2,1,0:T(8,128)(2,1)}), bf16[4,4,256,256]{3,2,1,0:T(8,128)(2,1)S(1)}, u32[]{:S(2)}, u32[]{:S(2)}) async-start(bf16[4,4,256,256]{3,2,1,0:T(8,128)(2,1)} %get-tuple-element.22), calls=%async_computation | async-start | bytes 4194304 | tf_op jit(solution)/shard_map/all_to_all | solution.py:218
  9.1 25.8 %collective-permute-start = (bf16[480,256]{1,0:T(8,128)(2,1)}, bf16[480,256]{1,0:T(8,128)(2,1)S(1)}, u32[]{:S(2)}, u32[]{:S(2)}) collective-permute-start(bf16[480,256]{1,0:T(8,128)(2,1)} %get-tuple-element.23), channel_id=1, source_target_pairs={{0,480},{32,0},{64,32},{96,64},{128,96},{160,128},{192,160},{224,1... | collective-permute-start | bytes 737288 | tf_op jit(solution)/shard_map/ppermute | solution.py:29
  20.2 14.7 %collective-permute-start.2 = (bf16[480,256]{1,0:T(8,128)(2,1)S(1)}, bf16[480,256]{1,0:T(8,128)(2,1)S(1)}, u32[]{:S(2)}, u32[]{:S(2)}) collective-permute-start(bf16[480,256]{1,0:T(8,128)(2,1)S(1)} %copy-done.2), channel_id=1, source_target_pairs={{0,32},{32,64},{64,96},{96,128},{128,160},{160,192},{192,224},{224... | collective-permute-start | bytes 737288 | tf_op jit(solution)/shard_map/ppermute | solution.py:29
  22.2 9.3 %collective-permute-start.1 = (bf16[352,256]{1,0:T(8,128)(2,1)}, bf16[352,256]{1,0:T(8,128)(2,1)S(1)}, u32[]{:S(2)}, u32[]{:S(2)}) collective-permute-start(bf16[352,256]{1,0:T(8,128)(2,1)} %get-tuple-element.24), channel_id=1, source_target_pairs={{0,448},{32,480},{64,0},{96,32},{128,64},{160,96},{192,128},{224,1... | collective-permute-start | bytes 540680 | tf_op jit(solution)/shard_map/ppermute | solution.py:29
  26.0 9.0 %collective-permute-start.3 = (bf16[352,256]{1,0:T(8,128)(2,1)}, bf16[352,256]{1,0:T(8,128)(2,1)S(1)}, u32[]{:S(2)}, u32[]{:S(2)}) collective-permute-start(bf16[352,256]{1,0:T(8,128)(2,1)} %get-tuple-element.26), channel_id=1, source_target_pairs={{0,64},{32,96},{64,128},{96,160},{128,192},{160,224},{192,256},{22... | collective-permute-start | bytes 540680 | tf_op jit(solution)/shard_map/ppermute | solution.py:29
  51.4 27.1 %collective-permute-start.4 = (bf16[480,256]{1,0:T(8,128)(2,1)S(1)}, bf16[480,256]{1,0:T(8,128)(2,1)S(1)}, u32[]{:S(2)}, u32[]{:S(2)}) collective-permute-start(bf16[480,256]{1,0:T(8,128)(2,1)S(1)} %get-tuple-element.33), channel_id=1, source_target_pairs={{0,480},{32,0},{64,32},{96,64},{128,96},{160,128},{192,160},{224,1... | collective-permute-start | bytes 737288 | tf_op jit(solution)/shard_map/ppermute | solution.py:29
  64.3 14.2 %collective-permute-start.6 = (bf16[480,256]{1,0:T(8,128)(2,1)S(1)}, bf16[480,256]{1,0:T(8,128)(2,1)S(1)}, u32[]{:S(2)}, u32[]{:S(2)}) collective-permute-start(bf16[480,256]{1,0:T(8,128)(2,1)S(1)} %get-tuple-element.35), channel_id=1, source_target_pairs={{0,32},{32,64},{64,96},{96,128},{128,160},{160,192},{192,224},{224... | collective-permute-start | bytes 737288 | tf_op jit(solution)/shard_map/ppermute | solution.py:29
  66.2 8.5 %collective-permute-start.5 = (bf16[352,256]{1,0:T(8,128)(2,1)S(1)}, bf16[352,256]{1,0:T(8,128)(2,1)S(1)}, u32[]{:S(2)}, u32[]{:S(2)}) collective-permute-start(bf16[352,256]{1,0:T(8,128)(2,1)S(1)} %get-tuple-element.34), channel_id=1, source_target_pairs={{0,448},{32,480},{64,0},{96,32},{128,64},{160,96},{192,128},{224,1... | collective-permute-start | bytes 540680 | tf_op jit(solution)/shard_map/ppermute | solution.py:29
  70.0 8.5 %collective-permute-start.7 = (bf16[352,256]{1,0:T(8,128)(2,1)S(1)}, bf16[352,256]{1,0:T(8,128)(2,1)S(1)}, u32[]{:S(2)}, u32[]{:S(2)}) collective-permute-start(bf16[352,256]{1,0:T(8,128)(2,1)S(1)} %get-tuple-element.36), channel_id=1, source_target_pairs={{0,64},{32,96},{64,128},{96,160},{128,192},{160,224},{192,256},{22... | collective-permute-start | bytes 540680 | tf_op jit(solution)/shard_map/ppermute | solution.py:29

commit v4 on v3

--- a/solution.py
+++ b/solution.py
@@ -19,9 +19,8 @@
 MINE = NX + 2
 
 
-READ = ((0, 15), (0, 11), (1, 16), (5, 16))
-HOPS = (-1, -2, 1, 2)
-OUTGOING = tuple(jax.ShapeDtypeStruct(((hi - lo) * SLAB, BS), BF) for lo, hi in READ)
+NEAR, FAR = 15, 11
+OUTGOING = (jax.ShapeDtypeStruct((NEAR * SLAB, BS), BF),) * 2
 
 
 def shift(value, axis, steps):
@@ -29,23 +28,31 @@
     return lax.ppermute(value, axis, [(s, (s + steps) % count) for s in range(count)])
 
 
-def band_kernel(last, flags, own, up1, up2, down1, down2, left, out, padded):
+def band_kernel(last, flags, own, near_a, near_b, far_a, far_b, left, out, padded):
     x = lax.axis_index("x")
+    even = 1 - lax.rem(lax.axis_index("z"), 2)
+    odd = 1 - even
     edge = 8 * SLAB
     for dz in range(5):
         padded[dz, :edge, :] = jnp.zeros((edge, BS), BF)
         padded[dz, 3 * edge :, :] = jnp.zeros((edge, BS), BF)
     padded[5] = jnp.zeros((4 * edge, BS), BF)
-    for dz, part, (lo, hi) in zip(
-        (2, 3, 4, 1, 0), (own, up1, up2, down1, down2), ((0, BAND), *READ)
+    for part, dz, lo, count in (
+        (own, 2, 0, BAND),
+        (near_a, 1 + 2 * even, odd, NEAR),
+        (near_b, 1 + 2 * odd, even, NEAR),
+        (far_a, 4 * even, 5 * odd, FAR),
+        (far_b, 4 * odd, 5 * even, FAR),
     ):
         if last:
-            padded[dz, edge + lo * SLAB : edge + hi * SLAB, :] = part[...]
+            begin = pl.multiple_of(edge + lo * SLAB, SLAB)
+            padded[dz, pl.ds(begin, count * SLAB), :] = part[...]
             continue
-        for slot in range(lo, hi):
-            piece = part[(slot - lo) * SLAB : (slot - lo + 1) * SLAB, :]
-            piece = jnp.where(flags[4 + dz, slot] > 0, piece, jnp.zeros((SLAB, BS), BF))
-            padded[dz, edge + slot * SLAB : edge + (slot + 1) * SLAB, :] = piece
+        for at in range(count):
+            piece = part[at * SLAB : (at + 1) * SLAB, :]
+            piece = jnp.where(flags[4 + dz, lo + at] > 0, piece, jnp.zeros((SLAB, BS), BF))
+            begin = pl.multiple_of(edge + (lo + at) * SLAB, SLAB)
+            padded[dz, pl.ds(begin, SLAB), :] = piece
     contract = (((1,), (1,)), ((), ()))
     for e in range(4):
         wrapped = jnp.where(x < e, 1, 0)
@@ -117,22 +124,26 @@
     )(flags, parts)
 
 
-def band_window(own, outgoing):
-    return (own, *(shift(part, "z", hop) for part, hop in zip(outgoing, HOPS)))
-
-
-def store_slots(value, first, own, outgoing):
-    count = value.shape[0] // SLAB
-    own[first * SLAB : (first + count) * SLAB, :] = value
-    for part, (lo, hi) in zip(outgoing, READ):
-        begin, end = max(lo, first), min(hi, first + count)
-        if begin < end:
-            part[(begin - lo) * SLAB : (end - lo) * SLAB, :] = value[
-                (begin - first) * SLAB : (end - first) * SLAB, :
-            ]
-
-
-def prepare_kernel(blocks, own, o1, o2, o3, o4, sent, held, move_sems, load_sems):
+def to_partner(value, kind):
+    return lax.ppermute(value, "z", [(z, (((z + kind) ^ 1) - kind) % NZ) for z in range(NZ)])
+
+
+def band_window(near_out):
+    near = [to_partner(part, kind) for kind, part in enumerate(near_out)]
+    odd = lax.axis_index("z") % 2
+    first = (NEAR - FAR) * SLAB
+    up = lax.dynamic_slice_in_dim(near[0], odd * first, FAR * SLAB, 0)
+    down = lax.dynamic_slice_in_dim(near[1], (1 - odd) * first, FAR * SLAB, 0)
+    return (*near, to_partner(down, 0), to_partner(up, 1))
+
+
+def store_outgoing(own, out_a, out_b):
+    even = 1 - lax.rem(lax.axis_index("z"), 2)
+    for part, lo in ((out_a, even), (out_b, 1 - even)):
+        part[...] = own[pl.ds(pl.multiple_of(lo * SLAB, SLAB), NEAR * SLAB), :]
+
+
+def prepare_kernel(blocks, own, out_a, out_b, sent, held, move_sems, load_sems):
     x = lax.axis_index("x")
     slab = lax.axis_index("y") * NC + lax.axis_index("core")
     base = pl.multiple_of((slab // 4) * 128, 128)
@@ -165,14 +176,15 @@
                 held[q, e, :, pl.ds(base, 128)], picks[e], preferred_element_type=F32
             )
             total = part if total is None else total + part
-        store_slots(total.T.astype(BF), 4 * q, own, (o1, o2, o3, o4))
+        own[q * 128 : q * 128 + 128, :] = total.T.astype(BF)
+    store_outgoing(own, out_a, out_b)
     for copy in moves:
         copy.wait()
 
 
 def prepare(blocks):
     vmem = pl.BlockSpec(memory_space=pltpu.VMEM)
-    anywhere = pl.BlockSpec(memory_space=pl.ANY)
+    hbm = pl.BlockSpec(memory_space=pltpu.HBM)
     return pl.pallas_call(
         prepare_kernel,
         out_shape=(
@@ -180,8 +192,8 @@
             *OUTGOING,
             jax.ShapeDtypeStruct((4, 4, BS, BS), BF),
         ),
-        in_specs=[anywhere],
-        out_specs=(*(vmem,) * 5, anywhere),
+        in_specs=[hbm],
+        out_specs=(vmem, vmem, vmem, hbm),
         scratch_shapes=[
             pltpu.VMEM((4, 4, BS, BS), BF),
             pltpu.SemaphoreType.DMA((16,)),
@@ -192,13 +204,14 @@
     )(blocks)
 
 
-def gather_kernel(flags, parts, own, o1, o2, o3, o4):
+def gather_kernel(flags, parts, own, out_a, out_b):
     for slot in range(BAND):
         piece = parts[0, slot * SLAB : slot * SLAB + SLAB, :].astype(F32)
         for x in range(1, 4):
             piece = piece + parts[x, slot * SLAB : slot * SLAB + SLAB, :].astype(F32)
         piece = jnp.where(flags[MINE, slot] > 0, piece, 0.0).astype(BF)
-        store_slots(piece, slot, own, (o1, o2, o3, o4))
+        own[slot * SLAB : slot * SLAB + SLAB, :] = piece
+    store_outgoing(own, out_a, out_b)
 
 
 def gather_square(flags, parts):
@@ -207,17 +220,18 @@
         gather_kernel,
         out_shape=(jax.ShapeDtypeStruct((ROWS, BS), BF), *OUTGOING),
         in_specs=[pl.BlockSpec(memory_space=pltpu.SMEM), vmem],
-        out_specs=(vmem,) * 5,
+        out_specs=(vmem,) * 3,
         compiler_params=pltpu.CompilerParams(vmem_limit_bytes=40 * 2**20),
         name="gather_square",
     )(flags, parts)
 
 
 def per_device(blocks, columns):
-    own, *outgoing, sent = prepare(blocks[0])
+    own, out_a, out_b, sent = prepare(blocks[0])
     left = lax.all_to_all(sent, "x", 0, 0, tiled=True)
-    own, *around = band_window(own, outgoing)
-    left, around = lax.optimization_barrier((left, around))
+    window = band_window((out_a, out_b))
+    left, window = lax.optimization_barrier((left, window))
+    window = (own, *window)
 
     z, x = lax.axis_index("z"), lax.axis_index("x")
     rows = jnp.concatenate(
@@ -227,10 +241,11 @@
     target = (rows[:, None] + jnp.arange(BAND, dtype=jnp.int32) - BAND // 2) % NB
     flags = jnp.any(listed[:, None, :] == target[:, :, None], axis=2).astype(jnp.int32)
 
-    terms = band_terms(flags, (own, *around), left, False)
+    terms = band_terms(flags, window, left, False)
     parts = lax.all_to_all(terms, "x", 0, 0, tiled=True)
-    own, *outgoing = gather_square(flags, parts)
-    terms = band_terms(flags, band_window(own, outgoing), left, True)
+    own, out_a, out_b = gather_square(flags, parts)
+    window = (own, *band_window((out_a, out_b)))
+    terms = band_terms(flags, window, left, True)
     parts = lax.all_to_all(terms, ("x", "y", "core"), 0, 0, tiled=True)
     return finish(flags, parts.reshape(4, 8, 128, 128))[None]
 

time: 112 us -> 112 us (level)
  starting transfers between devices: 45.2 us -> 39.2 us
  waiting for transfers between devices: 11.4 us -> 15 us
  blocking collectives: 42.1 us -> 44.1 us
    ppermute x8, starting transfers between devices: 40.2 us -> 34.2 us  [to_partner(): lax.ppermute(value, 'z', [(z, ((z + kind ^ 1) - kind) % NZ) for z in rang...]
    ppermute x8, waiting for transfers between devices: 11.4 us -> 15 us  [to_partner(): lax.ppermute(value, 'z', [(z, ((z + kind ^ 1) - kind) % NZ) for z in rang...]
    all_to_all x1, blocking collectives: 13.5 us -> 15.1 us  [per_device(): parts = lax.all_to_all(terms, 'x', 0, 0, tiled=True)]
  transfers between devices with their start and end apart: 9 -> 9, of which waited for: 4 -> 6; matrix products, arithmetic and copies ran while one was open for 1% -> 2% of each run, Pallas kernels for 0% -> 0%
where the time goes in v4:
time: 112 us
  blocking collectives  44.1 us (39%)
  starting transfers between devices  39.2 us (35%)
  waiting for transfers between devices  15 us (13%)
  Pallas kernels  11.2 us (10%)
  local copies, waits for them, and re-layouts  1.38 us (1%)
    ppermute x8, starting transfers between devices, to_partner(): lax.ppermute(value, 'z', [(z, ((z + kind ^ 1) - kind) % NZ) for z in rang...  34.2 us
    all_to_all x1, blocking collectives, per_device(): parts = lax.all_to_all(terms, ('x', 'y', 'core'), 0, 0, tiled=True)  29 us
    all_to_all x1, blocking collectives, per_device(): parts = lax.all_to_all(terms, 'x', 0, 0, tiled=True)  15.1 us
    ppermute x8, waiting for transfers between devices, to_partner(): lax.ppermute(value, 'z', [(z, ((z + kind ^ 1) - kind) % NZ) for z in rang...  15 us
    all_to_all x1, starting transfers between devices, per_device(): left = lax.all_to_all(sent, 'x', 0, 0, tiled=True)  4.98 us
    pallas_call x2, Pallas kernels, band_terms(): pl.pallas_call(functools.partial(band_kernel, last), out_shape=jax.ShapeD...  4.71 us
    pallas_call x1, Pallas kernels, prepare(): pl.pallas_call(prepare_kernel, out_shape=(jax.ShapeDtypeStruct((ROWS, BS)...  3.94 us
  transfers between devices with their start and end apart: 9, of which 6 were waited for; matrix products, arithmetic and copies ran while one was open for 2% of the time, Pallas kernels for 0%

profile of v4, /device:TPU:1, one launch (start us, length us, event | category | flops | bytes accessed | tf_op | source)
XLA Modules:
  0.0 111.7 jit_solution(11499668329704096285)
XLA Ops:
  0.0 3.9 %prepare.1 = (bf16[512,256]{1,0:T(8,128)(2,1)}, bf16[480,256]{1,0:T(8,128)(2,1)}, bf16[480,256]{1,0:T(8,128)(2,1)}, bf16[4,4,256,256]{3,2,1,0:T(8,128)(2,1)}) custom-call(bf16[16,256,256]{2,1,0:T(8,128)(2,1)} %bitcast.10), custom_call_target="tpu_custom_call" | custom-call | tf_op jit(solution)/shard_map/prepare/pallas_call | solution.py:188
  3.9 0.0 copy-start.2
  4.0 0.0 copy-start.1
  4.0 0.0 copy-start
  4.0 5.0 %all-to-all-start = ((bf16[4,4,256,256]{3,2,1,0:T(8,128)(2,1)}), bf16[4,4,256,256]{3,2,1,0:T(8,128)(2,1)S(1)}, u32[]{:S(2)}, u32[]{:S(2)}) async-start(bf16[4,4,256,256]{3,2,1,0:T(8,128)(2,1)} %get-tuple-element.18), calls=%async_computation | async-start | bytes 4194304 | tf_op jit(solution)/shard_map/all_to_all | solution.py:231
  9.0 3.5 %collective-permute-start = (bf16[480,256]{1,0:T(8,128)(2,1)}, bf16[480,256]{1,0:T(8,128)(2,1)S(1)}, u32[]{:S(2)}, u32[]{:S(2)}) collective-permute-start(bf16[480,256]{1,0:T(8,128)(2,1)} %get-tuple-element.19), channel_id=1, source_target_pairs={{0,32},{32,0},{64,96},{96,64},{128,160},{160,128},{192,224},{224,1... | collective-permute-start | bytes 737288 | tf_op jit(solution)/shard_map/ppermute | solution.py:128
  12.5 0.0 copy-done.2
  12.5 10.2 %collective-permute-start.1 = (bf16[480,256]{1,0:T(8,128)(2,1)S(1)}, bf16[480,256]{1,0:T(8,128)(2,1)S(1)}, u32[]{:S(2)}, u32[]{:S(2)}) collective-permute-start(bf16[480,256]{1,0:T(8,128)(2,1)S(1)} %copy-done.2), channel_id=1, source_target_pairs={{0,480},{32,64},{64,32},{96,128},{128,96},{160,192},{192,160},{224... | collective-permute-start | bytes 737288 | tf_op jit(solution)/shard_map/ppermute | solution.py:128
  22.8 0.1 and_select_fusion
  22.9 0.1 add_select_fusion
  23.0 0.0 copy-done.1
  23.0 0.1 copy.4
  23.1 0.1 fusion.3
  23.2 4.6 %collective-permute-done.1.near_b = bf16[480,256]{1,0:T(8,128)(2,1)S(1)} collective-permute-done((bf16[480,256]{1,0:T(8,128)(2,1)S(1)}, bf16[480,256]{1,0:T(8,128)(2,1)S(1)}, u32[]{:S(2)}, u32[]{:S(2)}) %collective-permute-start.1) | collective-permute-done | bytes 245792 | tf_op jit(solution)/shard_map/ppermute | solution.py:128
  27.8 1.9 %collective-permute-start.2 = (bf16[352,256]{1,0:T(8,128)(2,1)S(1)}, bf16[352,256]{1,0:T(8,128)(2,1)S(1)}, u32[]{:S(2)}, u32[]{:S(2)}) collective-permute-start(bf16[352,256]{1,0:T(8,128)(2,1)S(1)} %constant_dynamic-slice_fusion.3), channel_id=1, source_target_pairs={{0,32},{32,0},{64,96},{96,64},{128,160},{160,128},{192,224},{224,1... | collective-permute-start | bytes 540680 | tf_op jit(solution)/shard_map/ppermute | solution.py:128
  29.7 0.0 collective-permute-done.near_a
  29.7 0.7 constant_dynamic-slice_fusion.2
  30.4 4.3 %collective-permute-start.3 = (bf16[352,256]{1,0:T(8,128)(2,1)}, bf16[352,256]{1,0:T(8,128)(2,1)S(1)}, u32[]{:S(2)}, u32[]{:S(2)}) collective-permute-start(bf16[352,256]{1,0:T(8,128)(2,1)} %constant_dynamic-slice_fusion.2), channel_id=1, source_target_pairs={{0,480},{32,64},{64,32},{96,128},{128,96},{160,192},{192,160},{224... | collective-permute-start | bytes 540680 | tf_op jit(solution)/shard_map/ppermute | solution.py:128
  34.7 0.6 gather_fusion
  35.3 0.3 compare_reduce_fusion
  35.6 0.0 collective-permute-done.2.far_a
  35.6 2.5 %collective-permute-done.3.far_b = bf16[352,256]{1,0:T(8,128)(2,1)S(1)} collective-permute-done((bf16[352,256]{1,0:T(8,128)(2,1)}, bf16[352,256]{1,0:T(8,128)(2,1)S(1)}, u32[]{:S(2)}, u32[]{:S(2)}) %collective-permute-start.3) | collective-permute-done | bytes 180256 | tf_op jit(solution)/shard_map/ppermute | solution.py:128
  38.1 0.0 all-to-all-done.left
  38.1 0.0 copy-done
  38.1 2.2 %square_terms.1 = bf16[4,512,256]{2,1,0:T(8,128)(2,1)S(1)} custom-call(s32[9,16]{1,0:T(8,128)S(1)} %convert_element_type.3.flags, bf16[512,256]{1,0:T(8,128)(2,1)S(1)} %copy-done, bf16[480,256]{1,0:T(8,128)(2,1)S(1)} %collective-permute-done.near_a, bf16[480,256]{1,0:T(8,128)(2,1)S(1)} %collective-permute-done.1.near_b, ...), custom_call_target="tpu_custom_call" | custom-call | flops 1073741824 | bytes 6291456 | tf_op jit(solution)/shard_map/square_terms/pallas_call | solution.py:87
  40.3 15.1 %all_to_all.15.parts = bf16[4,512,256]{2,1,0:T(8,128)(2,1)S(1)} all-to-all(bf16[4,512,256]{2,1,0:T(8,128)(2,1)S(1)} %square_terms.1), channel_id=1, replica_groups=mesh['z'=16,'x'=4,'y'=4,'core'=2] {'x'}, dimensions={0} | all-to-all | bytes 2097152 | tf_op jit(solution)/shard_map/all_to_all | solution.py:245
  55.4 0.8 gather_square.1
  56.2 7.6 %collective-permute-start.5 = (bf16[480,256]{1,0:T(8,128)(2,1)S(1)}, bf16[480,256]{1,0:T(8,128)(2,1)S(1)}, u32[]{:S(2)}, u32[]{:S(2)}) collective-permute-start(bf16[480,256]{1,0:T(8,128)(2,1)S(1)} %get-tuple-element.28), channel_id=1, source_target_pairs={{0,480},{32,64},{64,32},{96,128},{128,96},{160,192},{192,160},{224... | collective-permute-start | bytes 737288 | tf_op jit(solution)/shard_map/ppermute | solution.py:128
  63.8 1.9 %collective-permute-start.4 = (bf16[480,256]{1,0:T(8,128)(2,1)S(1)}, bf16[480,256]{1,0:T(8,128)(2,1)S(1)}, u32[]{:S(2)}, u32[]{:S(2)}) collective-permute-start(bf16[480,256]{1,0:T(8,128)(2,1)S(1)} %get-tuple-element.27), channel_id=1, source_target_pairs={{0,32},{32,0},{64,96},{96,64},{128,160},{160,128},{192,224},{224,1... | collective-permute-start | bytes 737288 | tf_op jit(solution)/shard_map/ppermute | solution.py:128
  65.8 1.6 %collective-permute-done.5.near_b = bf16[480,256]{1,0:T(8,128)(2,1)S(1)} collective-permute-done((bf16[480,256]{1,0:T(8,128)(2,1)S(1)}, bf16[480,256]{1,0:T(8,128)(2,1)S(1)}, u32[]{:S(2)}, u32[]{:S(2)}) %collective-permute-start.5) | collective-permute-done | bytes 245792 | tf_op jit(solution)/shard_map/ppermute | solution.py:128
  67.4 1.9 %collective-permute-start.6 = (bf16[352,256]{1,0:T(8,128)(2,1)S(1)}, bf16[352,256]{1,0:T(8,128)(2,1)S(1)}, u32[]{:S(2)}, u32[]{:S(2)}) collective-permute-start(bf16[352,256]{1,0:T(8,128)(2,1)S(1)} %constant_dynamic-slice_fusion.1), channel_id=1, source_target_pairs={{0,32},{32,0},{64,96},{96,64},{128,160},{160,128},{192,224},{224,1... | collective-permute-start | bytes 540680 | tf_op jit(solution)/shard_map/ppermute | solution.py:128
  69.4 1.7 %collective-permute-done.4.near_a = bf16[480,256]{1,0:T(8,128)(2,1)S(1)} collective-permute-done((bf16[480,256]{1,0:T(8,128)(2,1)S(1)}, bf16[480,256]{1,0:T(8,128)(2,1)S(1)}, u32[]{:S(2)}, u32[]{:S(2)}) %collective-permute-start.4) | collective-permute-done | bytes 245792 | tf_op jit(solution)/shard_map/ppermute | solution.py:128
  71.1 2.9 %collective-permute-start.7 = (bf16[352,256]{1,0:T(8,128)(2,1)S(1)}, bf16[352,256]{1,0:T(8,128)(2,1)S(1)}, u32[]{:S(2)}, u32[]{:S(2)}) collective-permute-start(bf16[352,256]{1,0:T(8,128)(2,1)S(1)} %constant_dynamic-slice_fusion), channel_id=1, source_target_pairs={{0,480},{32,64},{64,32},{96,128},{128,96},{160,192},{192,160},{224... | collective-permute-start | bytes 540680 | tf_op jit(solution)/shard_map/ppermute | solution.py:128
  74.0 1.6 %collective-permute-done.6.far_a = bf16[352,256]{1,0:T(8,128)(2,1)S(1)} collective-permute-done((bf16[352,256]{1,0:T(8,128)(2,1)S(1)}, bf16[352,256]{1,0:T(8,128)(2,1)S(1)}, u32[]{:S(2)}, u32[]{:S(2)}) %collective-permute-start.6) | collective-permute-done | bytes 180256 | tf_op jit(solution)/shard_map/ppermute | solution.py:128
  75.6 3.0 %collective-permute-done.7.far_b = bf16[352,256]{1,0:T(8,128)(2,1)S(1)} collective-permute-done((bf16[352,256]{1,0:T(8,128)(2,1)S(1)}, bf16[352,256]{1,0:T(8,128)(2,1)S(1)}, u32[]{:S(2)}, u32[]{:S(2)}) %collective-permute-start.7) | collective-permute-done | bytes 180256 | tf_op jit(solution)/shard_map/ppermute | solution.py:128
  78.5 2.5 %cube_terms.1 = bf16[32,128,128]{2,1,0:T(8,128)(2,1)S(1)} custom-call(s32[9,16]{1,0:T(8,128)S(1)} %convert_element_type.3.flags, bf16[512,256]{1,0:T(8,128)(2,1)S(1)} %get-tuple-element.26.own, bf16[480,256]{1,0:T(8,128)(2,1)S(1)} %collective-permute-done.4.near_a, bf16[480,256]{1,0:T(8,128)(2,1)S(1)} %collective-permute-done.5.near_b, ...), custom_call_target="tpu_custom_call" | custom-call | flops 1073741824 | bytes 6291456 | tf_op jit(solution)/shard_map/cube_terms/pallas_call | solution.py:87
  81.0 29.0 %all_to_all.16 = bf16[32,128,128]{2,1,0:T(8,128)(2,1)S(1)} all-to-all(bf16[32,128,128]{2,1,0:T(8,128)(2,1)S(1)} %cube_terms.1), channel_id=1, replica_groups=mesh['z'=16,'x'=4,'y'=4,'core'=2] {'x','y','core'}, dimensions={0} | all-to-all | bytes 2097152 | tf_op jit(solution)/shard_map/all_to_all | solution.py:249
  110.0 1.7 %finish.1 = f32[16,32,256]{2,1,0:T(8,128)} custom-call(s32[9,16]{1,0:T(8,128)S(1)} %convert_element_type.3.flags, bf16[4,8,128,128]{3,2,1,0:T(8,128)(2,1)S(1)} %bitcast.9), custom_call_target="tpu_custom_call" | custom-call | tf_op jit(solution)/shard_map/finish/pallas_call | solution.py:117
  (9 shorter events, 0.1 us)
Async XLA Ops:
  3.9 8.6 %copy-start.2 = (bf16[480,256]{1,0:T(8,128)(2,1)S(1)}, bf16[480,256]{1,0:T(8,128)(2,1)}, u32[]{:S(2)}) copy-start(bf16[480,256]{1,0:T(8,128)(2,1)} %get-tuple-element.20) | copy-start | bytes 737284
  4.0 19.0 %copy-start.1 = (s32[64,16]{0,1:T(8,128)S(1)}, s32[64,16]{0,1:T(8,128)}, u32[]{:S(2)}) copy-start(s32[64,16]{0,1:T(8,128)} %param.3) | copy-start | bytes 12292
  4.0 34.1 %copy-start = (bf16[512,256]{1,0:T(8,128)(2,1)S(1)}, bf16[512,256]{1,0:T(8,128)(2,1)}, u32[]{:S(2)}) copy-start(bf16[512,256]{1,0:T(8,128)(2,1)} %get-tuple-element.17.own) | copy-start | bytes 786436
  4.0 34.1 %all-to-all-start = ((bf16[4,4,256,256]{3,2,1,0:T(8,128)(2,1)}), bf16[4,4,256,256]{3,2,1,0:T(8,128)(2,1)S(1)}, u32[]{:S(2)}, u32[]{:S(2)}) async-start(bf16[4,4,256,256]{3,2,1,0:T(8,128)(2,1)} %get-tuple-element.18), calls=%async_computation | async-start | bytes 4194304 | tf_op jit(solution)/shard_map/all_to_all | solution.py:231
  9.0 20.8 %collective-permute-start = (bf16[480,256]{1,0:T(8,128)(2,1)}, bf16[480,256]{1,0:T(8,128)(2,1)S(1)}, u32[]{:S(2)}, u32[]{:S(2)}) collective-permute-start(bf16[480,256]{1,0:T(8,128)(2,1)} %get-tuple-element.19), channel_id=1, source_target_pairs={{0,32},{32,0},{64,96},{96,64},{128,160},{160,128},{192,224},{224,1... | collective-permute-start | bytes 737288 | tf_op jit(solution)/shard_map/ppermute | solution.py:128
  12.5 15.2 %collective-permute-start.1 = (bf16[480,256]{1,0:T(8,128)(2,1)S(1)}, bf16[480,256]{1,0:T(8,128)(2,1)S(1)}, u32[]{:S(2)}, u32[]{:S(2)}) collective-permute-start(bf16[480,256]{1,0:T(8,128)(2,1)S(1)} %copy-done.2), channel_id=1, source_target_pairs={{0,480},{32,64},{64,32},{96,128},{128,96},{160,192},{192,160},{224... | collective-permute-start | bytes 737288 | tf_op jit(solution)/shard_map/ppermute | solution.py:128
  27.8 7.8 %collective-permute-start.2 = (bf16[352,256]{1,0:T(8,128)(2,1)S(1)}, bf16[352,256]{1,0:T(8,128)(2,1)S(1)}, u32[]{:S(2)}, u32[]{:S(2)}) collective-permute-start(bf16[352,256]{1,0:T(8,128)(2,1)S(1)} %constant_dynamic-slice_fusion.3), channel_id=1, source_target_pairs={{0,32},{32,0},{64,96},{96,64},{128,160},{160,128},{192,224},{224,1... | collective-permute-start | bytes 540680 | tf_op jit(solution)/shard_map/ppermute | solution.py:128
  30.4 7.6 %collective-permute-start.3 = (bf16[352,256]{1,0:T(8,128)(2,1)}, bf16[352,256]{1,0:T(8,128)(2,1)S(1)}, u32[]{:S(2)}, u32[]{:S(2)}) collective-permute-start(bf16[352,256]{1,0:T(8,128)(2,1)} %constant_dynamic-slice_fusion.2), channel_id=1, source_target_pairs={{0,480},{32,64},{64,32},{96,128},{128,96},{160,192},{192,160},{224... | collective-permute-start | bytes 540680 | tf_op jit(solution)/shard_map/ppermute | solution.py:128
  56.2 11.2 %collective-permute-start.5 = (bf16[480,256]{1,0:T(8,128)(2,1)S(1)}, bf16[480,256]{1,0:T(8,128)(2,1)S(1)}, u32[]{:S(2)}, u32[]{:S(2)}) collective-permute-start(bf16[480,256]{1,0:T(8,128)(2,1)S(1)} %get-tuple-element.28), channel_id=1, source_target_pairs={{0,480},{32,64},{64,32},{96,128},{128,96},{160,192},{192,160},{224... | collective-permute-start | bytes 737288 | tf_op jit(solution)/shard_map/ppermute | solution.py:128
  63.8 7.2 %collective-permute-start.4 = (bf16[480,256]{1,0:T(8,128)(2,1)S(1)}, bf16[480,256]{1,0:T(8,128)(2,1)S(1)}, u32[]{:S(2)}, u32[]{:S(2)}) collective-permute-start(bf16[480,256]{1,0:T(8,128)(2,1)S(1)} %get-tuple-element.27), channel_id=1, source_target_pairs={{0,32},{32,0},{64,96},{96,64},{128,160},{160,128},{192,224},{224,1... | collective-permute-start | bytes 737288 | tf_op jit(solution)/shard_map/ppermute | solution.py:128
  67.4 8.2 %collective-permute-start.6 = (bf16[352,256]{1,0:T(8,128)(2,1)S(1)}, bf16[352,256]{1,0:T(8,128)(2,1)S(1)}, u32[]{:S(2)}, u32[]{:S(2)}) collective-permute-start(bf16[352,256]{1,0:T(8,128)(2,1)S(1)} %constant_dynamic-slice_fusion.1), channel_id=1, source_target_pairs={{0,32},{32,0},{64,96},{96,64},{128,160},{160,128},{192,224},{224,1... | collective-permute-start | bytes 540680 | tf_op jit(solution)/shard_map/ppermute | solution.py:128
  71.1 7.4 %collective-permute-start.7 = (bf16[352,256]{1,0:T(8,128)(2,1)S(1)}, bf16[352,256]{1,0:T(8,128)(2,1)S(1)}, u32[]{:S(2)}, u32[]{:S(2)}) collective-permute-start(bf16[352,256]{1,0:T(8,128)(2,1)S(1)} %constant_dynamic-slice_fusion), channel_id=1, source_target_pairs={{0,480},{32,64},{64,32},{96,128},{128,96},{160,192},{192,160},{224... | collective-permute-start | bytes 540680 | tf_op jit(solution)/shard_map/ppermute | solution.py:128

commit v5 on v3

--- a/solution.py
+++ b/solution.py
@@ -50,13 +50,18 @@
     for e in range(4):
         wrapped = jnp.where(x < e, 1, 0)
         target = lax.rem(x - e + 4, 4)
-        total = None
+        rows, blocks = [], []
         for q in range(4):
             start = (16 - e - 4 * q) * SLAB
             plane = jnp.where(flags[target, 4 * q + e] > 0, q + wrapped, 5)
-            rows = padded[plane, start : start + ROWS, :]
-            term = lax.dot_general(rows, left[target, q], contract, preferred_element_type=F32)
-            total = term if total is None else total + term
+            rows.append(padded[plane, start : start + ROWS, :])
+            blocks.append(left[target, q])
+        total = lax.dot_general(
+            jnp.concatenate(rows, axis=1),
+            jnp.concatenate(blocks, axis=1),
+            contract,
+            preferred_element_type=F32,
+        )
         if last and e == 0:
             total = total - 1.5 * own[...].astype(F32)
         if not last:
@@ -91,30 +96,40 @@
     )(flags, *window, left)
 
 
-def finish_kernel(flags, parts, out):
-    total = parts[0].astype(F32)
-    for x in range(1, 4):
-        total = total + parts[x].astype(F32)
-    total = -2.0 * total
+def finish_kernel(flags, parts, out, ready, sems):
+    writes = []
     for lo in range(4):
-        tile = total[:, lo * SLAB : lo * SLAB + SLAB, :].reshape(BS, 128)
-        flat = tile.T
+        total = None
+        for x in range(4):
+            part = parts[x, :, lo * SLAB : lo * SLAB + SLAB, :].astype(F32)
+            total = part if total is None else total + part
+        flat = (-2.0 * total).reshape(BS, 128).T
         for hi in range(4):
-            slot = hi * 4 + lo
             piece = flat[hi * SLAB : hi * SLAB + SLAB, :]
-            out[slot] = jnp.where(flags[MINE, slot] > 0, piece, 0.0)
+            ready[lo, hi] = jnp.where(flags[MINE, hi * 4 + lo] > 0, piece, 0.0)
+        writes.append(pltpu.make_async_copy(ready.at[lo], out.at[:, lo], sems.at[lo]))
+        writes[-1].start()
+    for copy in writes:
+        copy.wait()
 
 
 def finish(flags, parts):
-    vmem = pl.BlockSpec(memory_space=pltpu.VMEM)
-    return pl.pallas_call(
+    result = pl.pallas_call(
         finish_kernel,
-        out_shape=jax.ShapeDtypeStruct((BAND, SLAB, BS), F32),
-        in_specs=[pl.BlockSpec(memory_space=pltpu.SMEM), vmem],
-        out_specs=vmem,
+        out_shape=jax.ShapeDtypeStruct((4, 4, SLAB, BS), F32),
+        in_specs=[
+            pl.BlockSpec(memory_space=pltpu.SMEM),
+            pl.BlockSpec(memory_space=pltpu.VMEM),
+        ],
+        out_specs=pl.BlockSpec(memory_space=pl.ANY),
+        scratch_shapes=[
+            pltpu.VMEM((4, 4, SLAB, BS), F32),
+            pltpu.SemaphoreType.DMA((4,)),
+        ],
         compiler_params=pltpu.CompilerParams(vmem_limit_bytes=40 * 2**20),
         name="finish",
     )(flags, parts)
+    return result.reshape(BAND, SLAB, BS)
 
 
 def band_window(own, outgoing):
@@ -132,7 +147,7 @@
             ]
 
 
-def prepare_kernel(blocks, own, o1, o2, o3, o4, sent, held, move_sems, load_sems):
+def prepare_kernel(blocks, own, o1, o2, o3, o4, sent, held, slab_t, move_sems, load_sems, out_sems):
     x = lax.axis_index("x")
     slab = lax.axis_index("y") * NC + lax.axis_index("core")
     base = pl.multiple_of((slab // 4) * 128, 128)
@@ -165,13 +180,25 @@
                 held[q, e, :, pl.ds(base, 128)], picks[e], preferred_element_type=F32
             )
             total = part if total is None else total + part
-        store_slots(total.T.astype(BF), 4 * q, own, (o1, o2, o3, o4))
+        slab_t[q * 128 : q * 128 + 128, :] = total.T.astype(BF)
+        for at, (part, (lo, hi)) in enumerate(
+            zip((own, o1, o2, o3, o4), ((0, BAND), *READ))
+        ):
+            begin, end = max(lo, 4 * q), min(hi, 4 * q + 4)
+            if begin < end:
+                size = (end - begin) * SLAB
+                copy = pltpu.make_async_copy(
+                    slab_t.at[pl.ds(begin * SLAB, size)],
+                    part.at[pl.ds((begin - lo) * SLAB, size)],
+                    out_sems.at[4 * at + q],
+                )
+                copy.start()
+                moves.append(copy)
     for copy in moves:
         copy.wait()
 
 
 def prepare(blocks):
-    vmem = pl.BlockSpec(memory_space=pltpu.VMEM)
     anywhere = pl.BlockSpec(memory_space=pl.ANY)
     return pl.pallas_call(
         prepare_kernel,
@@ -181,11 +208,13 @@
             jax.ShapeDtypeStruct((4, 4, BS, BS), BF),
         ),
         in_specs=[anywhere],
-        out_specs=(*(vmem,) * 5, anywhere),
+        out_specs=(anywhere,) * 6,
         scratch_shapes=[
             pltpu.VMEM((4, 4, BS, BS), BF),
+            pltpu.VMEM((ROWS, BS), BF),
             pltpu.SemaphoreType.DMA((16,)),
             pltpu.SemaphoreType.DMA((4,)),
+            pltpu.SemaphoreType.DMA((20,)),
         ],
         compiler_params=pltpu.CompilerParams(vmem_limit_bytes=56 * 2**20),
         name="prepare",

time: 112 us -> 111 us (level)
  no operation moved by 1% of the time
where the time goes in v5:
time: 111 us
  starting transfers between devices  45.2 us (41%)
  blocking collectives  42.1 us (38%)
  waiting for transfers between devices  11.4 us (10%)
  Pallas kernels  10.4 us (9%)
    ppermute x8, starting transfers between devices, shift(): lax.ppermute(value, axis, [(s, (s + steps) % count) for s in range(count)])  40.2 us
    all_to_all x1, blocking collectives, per_device(): parts = lax.all_to_all(terms, ('x', 'y', 'core'), 0, 0, tiled=True)  28.6 us
    all_to_all x1, blocking collectives, per_device(): parts = lax.all_to_all(terms, 'x', 0, 0, tiled=True)  13.5 us
    ppermute x8, waiting for transfers between devices, shift(): lax.ppermute(value, axis, [(s, (s + steps) % count) for s in range(count)])  11.4 us
    all_to_all x1, starting transfers between devices, per_device(): left = lax.all_to_all(sent, 'x', 0, 0, tiled=True)  4.99 us
    pallas_call x2, Pallas kernels, band_terms(): pl.pallas_call(functools.partial(band_kernel, last), out_shape=jax.ShapeD...  4.53 us
    pallas_call x1, Pallas kernels, prepare(): pl.pallas_call(prepare_kernel, out_shape=(jax.ShapeDtypeStruct((ROWS, BS)...  3.51 us
  transfers between devices with their start and end apart: 9, of which 4 were waited for; matrix products, arithmetic and copies ran while one was open for 1% of the time, Pallas kernels for 0%

profile of v5, /device:TPU:1, one launch (start us, length us, event | category | flops | bytes accessed | tf_op | source)
XLA Modules:
  0.0 110.5 jit_solution(12794928980976066781)
XLA Ops:
  0.0 3.5 %prepare.1 = (bf16[512,256]{1,0:T(8,128)(2,1)}, bf16[480,256]{1,0:T(8,128)(2,1)}, bf16[352,256]{1,0:T(8,128)(2,1)}, bf16[480,256]{1,0:T(8,128)(2,1)}, bf16[352,2...) custom-call(bf16[16,256,256]{2,1,0:T(8,128)(2,1)} %bitcast.10), custom_call_target="tpu_custom_call" | custom-call | tf_op jit(solution)/shard_map/prepare/pallas_call | solution.py:203
  3.5 0.0 copy-start.2
  3.5 0.0 copy-start.1
  3.5 0.0 copy-start
  3.5 5.0 %all-to-all-start = ((bf16[4,4,256,256]{3,2,1,0:T(8,128)(2,1)}), bf16[4,4,256,256]{3,2,1,0:T(8,128)(2,1)S(1)}, u32[]{:S(2)}, u32[]{:S(2)}) async-start(bf16[4,4,256,256]{3,2,1,0:T(8,128)(2,1)} %get-tuple-element.22), calls=%async_computation | async-start | bytes 4194304 | tf_op jit(solution)/shard_map/all_to_all | solution.py:247
  8.5 11.1 %collective-permute-start = (bf16[480,256]{1,0:T(8,128)(2,1)}, bf16[480,256]{1,0:T(8,128)(2,1)S(1)}, u32[]{:S(2)}, u32[]{:S(2)}) collective-permute-start(bf16[480,256]{1,0:T(8,128)(2,1)} %get-tuple-element.23), channel_id=1, source_target_pairs={{0,480},{32,0},{64,32},{96,64},{128,96},{160,128},{192,160},{224,1... | collective-permute-start | bytes 737288 | tf_op jit(solution)/shard_map/ppermute | solution.py:29
  19.7 0.0 copy-done.2
  19.7 1.9 %collective-permute-start.2 = (bf16[480,256]{1,0:T(8,128)(2,1)S(1)}, bf16[480,256]{1,0:T(8,128)(2,1)S(1)}, u32[]{:S(2)}, u32[]{:S(2)}) collective-permute-start(bf16[480,256]{1,0:T(8,128)(2,1)S(1)} %copy-done.2), channel_id=1, source_target_pairs={{0,32},{32,64},{64,96},{96,128},{128,160},{160,192},{192,224},{224... | collective-permute-start | bytes 737288 | tf_op jit(solution)/shard_map/ppermute | solution.py:29
  21.6 3.8 %collective-permute-start.1 = (bf16[352,256]{1,0:T(8,128)(2,1)}, bf16[352,256]{1,0:T(8,128)(2,1)S(1)}, u32[]{:S(2)}, u32[]{:S(2)}) collective-permute-start(bf16[352,256]{1,0:T(8,128)(2,1)} %get-tuple-element.24), channel_id=1, source_target_pairs={{0,448},{32,480},{64,0},{96,32},{128,64},{160,96},{192,128},{224,1... | collective-permute-start | bytes 540680 | tf_op jit(solution)/shard_map/ppermute | solution.py:29
  25.4 2.4 %collective-permute-start.3 = (bf16[352,256]{1,0:T(8,128)(2,1)}, bf16[352,256]{1,0:T(8,128)(2,1)S(1)}, u32[]{:S(2)}, u32[]{:S(2)}) collective-permute-start(bf16[352,256]{1,0:T(8,128)(2,1)} %get-tuple-element.26), channel_id=1, source_target_pairs={{0,64},{32,96},{64,128},{96,160},{128,192},{160,224},{192,256},{22... | collective-permute-start | bytes 540680 | tf_op jit(solution)/shard_map/ppermute | solution.py:29
  27.9 0.1 and_select_fusion
  27.9 0.1 add_select_fusion
  28.0 0.1 fusion.3
  28.1 0.0 copy-done.1
  28.1 0.1 copy.4
  28.2 0.6 gather_fusion
  28.8 0.3 compare_reduce_fusion
  29.1 1.8 %collective-permute-done.1.up2 = bf16[352,256]{1,0:T(8,128)(2,1)S(1)} collective-permute-done((bf16[352,256]{1,0:T(8,128)(2,1)}, bf16[352,256]{1,0:T(8,128)(2,1)S(1)}, u32[]{:S(2)}, u32[]{:S(2)}) %collective-permute-start.1) | collective-permute-done | bytes 180256 | tf_op jit(solution)/shard_map/ppermute | solution.py:29
  30.9 3.4 %collective-permute-done.3.down2 = bf16[352,256]{1,0:T(8,128)(2,1)S(1)} collective-permute-done((bf16[352,256]{1,0:T(8,128)(2,1)}, bf16[352,256]{1,0:T(8,128)(2,1)S(1)}, u32[]{:S(2)}, u32[]{:S(2)}) %collective-permute-start.3) | collective-permute-done | bytes 180256 | tf_op jit(solution)/shard_map/ppermute | solution.py:29
  34.4 0.0 collective-permute-done.up1
  34.4 0.0 collective-permute-done.2.down1
  34.4 0.0 all-to-all-done.left
  34.4 0.0 copy-done
  34.4 2.1 %square_terms.1 = bf16[4,512,256]{2,1,0:T(8,128)(2,1)S(1)} custom-call(s32[9,16]{1,0:T(8,128)S(1)} %convert_element_type.3.flags, bf16[512,256]{1,0:T(8,128)(2,1)S(1)} %copy-done, bf16[480,256]{1,0:T(8,128)(2,1)S(1)} %collective-permute-done.up1, bf16[352,256]{1,0:T(8,128)(2,1)S(1)} %collective-permute-done.1.up2, ...), custom_call_target="tpu_custom_call" | custom-call | flops 1073741824 | bytes 6291456 | tf_op jit(solution)/shard_map/square_terms/pallas_call | solution.py:85
  36.5 13.5 %all_to_all.15.parts = bf16[4,512,256]{2,1,0:T(8,128)(2,1)S(1)} all-to-all(bf16[4,512,256]{2,1,0:T(8,128)(2,1)S(1)} %square_terms.1), channel_id=1, replica_groups=mesh['z'=16,'x'=4,'y'=4,'core'=2] {'x'}, dimensions={0} | all-to-all | bytes 2097152 | tf_op jit(solution)/shard_map/all_to_all | solution.py:260
  50.0 0.8 gather_square.1
  50.8 12.9 %collective-permute-start.4 = (bf16[480,256]{1,0:T(8,128)(2,1)S(1)}, bf16[480,256]{1,0:T(8,128)(2,1)S(1)}, u32[]{:S(2)}, u32[]{:S(2)}) collective-permute-start(bf16[480,256]{1,0:T(8,128)(2,1)S(1)} %get-tuple-element.33), channel_id=1, source_target_pairs={{0,480},{32,0},{64,32},{96,64},{128,96},{160,128},{192,160},{224,1... | collective-permute-start | bytes 737288 | tf_op jit(solution)/shard_map/ppermute | solution.py:29
  63.7 1.9 %collective-permute-start.6 = (bf16[480,256]{1,0:T(8,128)(2,1)S(1)}, bf16[480,256]{1,0:T(8,128)(2,1)S(1)}, u32[]{:S(2)}, u32[]{:S(2)}) collective-permute-start(bf16[480,256]{1,0:T(8,128)(2,1)S(1)} %get-tuple-element.35), channel_id=1, source_target_pairs={{0,32},{32,64},{64,96},{96,128},{128,160},{160,192},{192,224},{224... | collective-permute-start | bytes 737288 | tf_op jit(solution)/shard_map/ppermute | solution.py:29
  65.6 3.8 %collective-permute-start.5 = (bf16[352,256]{1,0:T(8,128)(2,1)S(1)}, bf16[352,256]{1,0:T(8,128)(2,1)S(1)}, u32[]{:S(2)}, u32[]{:S(2)}) collective-permute-start(bf16[352,256]{1,0:T(8,128)(2,1)S(1)} %get-tuple-element.34), channel_id=1, source_target_pairs={{0,448},{32,480},{64,0},{96,32},{128,64},{160,96},{192,128},{224,1... | collective-permute-start | bytes 540680 | tf_op jit(solution)/shard_map/ppermute | solution.py:29
  69.4 2.4 %collective-permute-start.7 = (bf16[352,256]{1,0:T(8,128)(2,1)S(1)}, bf16[352,256]{1,0:T(8,128)(2,1)S(1)}, u32[]{:S(2)}, u32[]{:S(2)}) collective-permute-start(bf16[352,256]{1,0:T(8,128)(2,1)S(1)} %get-tuple-element.36), channel_id=1, source_target_pairs={{0,64},{32,96},{64,128},{96,160},{128,192},{160,224},{192,256},{22... | collective-permute-start | bytes 540680 | tf_op jit(solution)/shard_map/ppermute | solution.py:29
  71.8 2.3 %collective-permute-done.5.up2 = bf16[352,256]{1,0:T(8,128)(2,1)S(1)} collective-permute-done((bf16[352,256]{1,0:T(8,128)(2,1)S(1)}, bf16[352,256]{1,0:T(8,128)(2,1)S(1)}, u32[]{:S(2)}, u32[]{:S(2)}) %collective-permute-start.5) | collective-permute-done | bytes 180256 | tf_op jit(solution)/shard_map/ppermute | solution.py:29
  74.1 3.8 %collective-permute-done.7.down2 = bf16[352,256]{1,0:T(8,128)(2,1)S(1)} collective-permute-done((bf16[352,256]{1,0:T(8,128)(2,1)S(1)}, bf16[352,256]{1,0:T(8,128)(2,1)S(1)}, u32[]{:S(2)}, u32[]{:S(2)}) %collective-permute-start.7) | collective-permute-done | bytes 180256 | tf_op jit(solution)/shard_map/ppermute | solution.py:29
  77.9 0.0 collective-permute-done.4.up1
  77.9 0.0 collective-permute-done.6.down1
  77.9 2.5 %cube_terms.1 = bf16[32,128,128]{2,1,0:T(8,128)(2,1)S(1)} custom-call(s32[9,16]{1,0:T(8,128)S(1)} %convert_element_type.3.flags, bf16[512,256]{1,0:T(8,128)(2,1)S(1)} %get-tuple-element.32.own, bf16[480,256]{1,0:T(8,128)(2,1)S(1)} %collective-permute-done.4.up1, bf16[352,256]{1,0:T(8,128)(2,1)S(1)} %collective-permute-done.5.up2, ...), custom_call_target="tpu_custom_call" | custom-call | flops 1073741824 | bytes 6291456 | tf_op jit(solution)/shard_map/cube_terms/pallas_call | solution.py:85
  80.4 28.6 %all_to_all.16 = bf16[32,128,128]{2,1,0:T(8,128)(2,1)S(1)} all-to-all(bf16[32,128,128]{2,1,0:T(8,128)(2,1)S(1)} %cube_terms.1), channel_id=1, replica_groups=mesh['z'=16,'x'=4,'y'=4,'core'=2] {'x','y','core'}, dimensions={0} | all-to-all | bytes 2097152 | tf_op jit(solution)/shard_map/all_to_all | solution.py:263
  108.9 1.6 %finish.1 = f32[4,4,32,256]{3,2,1,0:T(8,128)} custom-call(s32[9,16]{1,0:T(8,128)S(1)} %convert_element_type.3.flags, bf16[4,8,128,128]{3,2,1,0:T(8,128)(2,1)S(1)} %bitcast.9), custom_call_target="tpu_custom_call" | custom-call | tf_op jit(solution)/shard_map/finish/pallas_call | solution.py:117
  (6 shorter events, 0.0 us)
Async XLA Ops:
  3.5 16.1 %copy-start.2 = (bf16[480,256]{1,0:T(8,128)(2,1)S(1)}, bf16[480,256]{1,0:T(8,128)(2,1)}, u32[]{:S(2)}) copy-start(bf16[480,256]{1,0:T(8,128)(2,1)} %get-tuple-element.25) | copy-start | bytes 737284
  3.5 24.6 %copy-start.1 = (s32[64,16]{0,1:T(8,128)S(1)}, s32[64,16]{0,1:T(8,128)}, u32[]{:S(2)}) copy-start(s32[64,16]{0,1:T(8,128)} %param.3) | copy-start | bytes 12292
  3.5 30.8 %copy-start = (bf16[512,256]{1,0:T(8,128)(2,1)S(1)}, bf16[512,256]{1,0:T(8,128)(2,1)}, u32[]{:S(2)}) copy-start(bf16[512,256]{1,0:T(8,128)(2,1)} %get-tuple-element.21.own) | copy-start | bytes 786436
  3.5 30.8 %all-to-all-start = ((bf16[4,4,256,256]{3,2,1,0:T(8,128)(2,1)}), bf16[4,4,256,256]{3,2,1,0:T(8,128)(2,1)S(1)}, u32[]{:S(2)}, u32[]{:S(2)}) async-start(bf16[4,4,256,256]{3,2,1,0:T(8,128)(2,1)} %get-tuple-element.22), calls=%async_computation | async-start | bytes 4194304 | tf_op jit(solution)/shard_map/all_to_all | solution.py:247
  8.5 25.8 %collective-permute-start = (bf16[480,256]{1,0:T(8,128)(2,1)}, bf16[480,256]{1,0:T(8,128)(2,1)S(1)}, u32[]{:S(2)}, u32[]{:S(2)}) collective-permute-start(bf16[480,256]{1,0:T(8,128)(2,1)} %get-tuple-element.23), channel_id=1, source_target_pairs={{0,480},{32,0},{64,32},{96,64},{128,96},{160,128},{192,160},{224,1... | collective-permute-start | bytes 737288 | tf_op jit(solution)/shard_map/ppermute | solution.py:29
  19.7 14.7 %collective-permute-start.2 = (bf16[480,256]{1,0:T(8,128)(2,1)S(1)}, bf16[480,256]{1,0:T(8,128)(2,1)S(1)}, u32[]{:S(2)}, u32[]{:S(2)}) collective-permute-start(bf16[480,256]{1,0:T(8,128)(2,1)S(1)} %copy-done.2), channel_id=1, source_target_pairs={{0,32},{32,64},{64,96},{96,128},{128,160},{160,192},{192,224},{224... | collective-permute-start | bytes 737288 | tf_op jit(solution)/shard_map/ppermute | solution.py:29
  21.6 9.3 %collective-permute-start.1 = (bf16[352,256]{1,0:T(8,128)(2,1)}, bf16[352,256]{1,0:T(8,128)(2,1)S(1)}, u32[]{:S(2)}, u32[]{:S(2)}) collective-permute-start(bf16[352,256]{1,0:T(8,128)(2,1)} %get-tuple-element.24), channel_id=1, source_target_pairs={{0,448},{32,480},{64,0},{96,32},{128,64},{160,96},{192,128},{224,1... | collective-permute-start | bytes 540680 | tf_op jit(solution)/shard_map/ppermute | solution.py:29
  25.4 9.0 %collective-permute-start.3 = (bf16[352,256]{1,0:T(8,128)(2,1)}, bf16[352,256]{1,0:T(8,128)(2,1)S(1)}, u32[]{:S(2)}, u32[]{:S(2)}) collective-permute-start(bf16[352,256]{1,0:T(8,128)(2,1)} %get-tuple-element.26), channel_id=1, source_target_pairs={{0,64},{32,96},{64,128},{96,160},{128,192},{160,224},{192,256},{22... | collective-permute-start | bytes 540680 | tf_op jit(solution)/shard_map/ppermute | solution.py:29
  50.8 27.1 %collective-permute-start.4 = (bf16[480,256]{1,0:T(8,128)(2,1)S(1)}, bf16[480,256]{1,0:T(8,128)(2,1)S(1)}, u32[]{:S(2)}, u32[]{:S(2)}) collective-permute-start(bf16[480,256]{1,0:T(8,128)(2,1)S(1)} %get-tuple-element.33), channel_id=1, source_target_pairs={{0,480},{32,0},{64,32},{96,64},{128,96},{160,128},{192,160},{224,1... | collective-permute-start | bytes 737288 | tf_op jit(solution)/shard_map/ppermute | solution.py:29
  63.7 14.2 %collective-permute-start.6 = (bf16[480,256]{1,0:T(8,128)(2,1)S(1)}, bf16[480,256]{1,0:T(8,128)(2,1)S(1)}, u32[]{:S(2)}, u32[]{:S(2)}) collective-permute-start(bf16[480,256]{1,0:T(8,128)(2,1)S(1)} %get-tuple-element.35), channel_id=1, source_target_pairs={{0,32},{32,64},{64,96},{96,128},{128,160},{160,192},{192,224},{224... | collective-permute-start | bytes 737288 | tf_op jit(solution)/shard_map/ppermute | solution.py:29
  65.6 8.5 %collective-permute-start.5 = (bf16[352,256]{1,0:T(8,128)(2,1)S(1)}, bf16[352,256]{1,0:T(8,128)(2,1)S(1)}, u32[]{:S(2)}, u32[]{:S(2)}) collective-permute-start(bf16[352,256]{1,0:T(8,128)(2,1)S(1)} %get-tuple-element.34), channel_id=1, source_target_pairs={{0,448},{32,480},{64,0},{96,32},{128,64},{160,96},{192,128},{224,1... | collective-permute-start | bytes 540680 | tf_op jit(solution)/shard_map/ppermute | solution.py:29
  69.4 8.5 %collective-permute-start.7 = (bf16[352,256]{1,0:T(8,128)(2,1)S(1)}, bf16[352,256]{1,0:T(8,128)(2,1)S(1)}, u32[]{:S(2)}, u32[]{:S(2)}) collective-permute-start(bf16[352,256]{1,0:T(8,128)(2,1)S(1)} %get-tuple-element.36), channel_id=1, source_target_pairs={{0,64},{32,96},{64,128},{96,160},{128,192},{160,224},{192,256},{22... | collective-permute-start | bytes 540680 | tf_op jit(solution)/shard_map/ppermute | solution.py:29

commit v6 on v5

--- a/solution.py
+++ b/solution.py
@@ -32,10 +32,12 @@
 def band_kernel(last, flags, own, up1, up2, down1, down2, left, out, padded):
     x = lax.axis_index("x")
     edge = 8 * SLAB
-    for dz in range(5):
-        padded[dz, :edge, :] = jnp.zeros((edge, BS), BF)
-        padded[dz, 3 * edge :, :] = jnp.zeros((edge, BS), BF)
-    padded[5] = jnp.zeros((4 * edge, BS), BF)
+    for dz, (below, above) in enumerate(((8, 32), (8, 32), (5, 28), (1, 24), (1, 24))):
+        if below < 8:
+            padded[dz, below * SLAB : edge, :] = jnp.zeros((edge - below * SLAB, BS), BF)
+        if above > 24:
+            padded[dz, 3 * edge : above * SLAB, :] = jnp.zeros((above * SLAB - 3 * edge, BS), BF)
+    padded[5, :ROWS, :] = jnp.zeros((ROWS, BS), BF)
     for dz, part, (lo, hi) in zip(
         (2, 3, 4, 1, 0), (own, up1, up2, down1, down2), ((0, BAND), *READ)
     ):
@@ -53,8 +55,10 @@
         rows, blocks = [], []
         for q in range(4):
             start = (16 - e - 4 * q) * SLAB
-            plane = jnp.where(flags[target, 4 * q + e] > 0, q + wrapped, 5)
-            rows.append(padded[plane, start : start + ROWS, :])
+            present = flags[target, 4 * q + e] > 0
+            plane = jnp.where(present, q + wrapped, 5)
+            begin = pl.multiple_of(jnp.where(present, start, 0), SLAB)
+            rows.append(padded[plane, pl.ds(begin, ROWS), :])
             blocks.append(left[target, q])
         total = lax.dot_general(
             jnp.concatenate(rows, axis=1),
@@ -246,8 +250,6 @@
     own, *outgoing, sent = prepare(blocks[0])
     left = lax.all_to_all(sent, "x", 0, 0, tiled=True)
     own, *around = band_window(own, outgoing)
-    left, around = lax.optimization_barrier((left, around))
-
     z, x = lax.axis_index("z"), lax.axis_index("x")
     rows = jnp.concatenate(
         [NX * z + jnp.arange(NX), NX * (z + jnp.arange(-2, 3)) + x]

time: 111 us -> 111 us (level)
  starting transfers between devices: 45.2 us -> 38.6 us
  blocking collectives: 42.1 us -> 45.6 us
  waiting for transfers between devices: 11.4 us -> 14.5 us
    ppermute x8, starting transfers between devices: 40.2 us -> 33.6 us  [shift(): lax.ppermute(value, axis, [(s, (s + steps) % count) for s in range(count)])]
    all_to_all x1, blocking collectives: 13.5 us -> 17 us  [per_device(): parts = lax.all_to_all(terms, 'x', 0, 0, tiled=True)]
    ppermute x8, waiting for transfers between devices: 11.4 us -> 14.4 us  [shift(): lax.ppermute(value, axis, [(s, (s + steps) % count) for s in range(count)])]
where the time goes in v6:
time: 111 us; the launch traced here: 110 us
  blocking collectives  45.6 us (41%)
  starting transfers between devices  38.6 us (35%)
  waiting for transfers between devices  14.5 us (13%)
  Pallas kernels  10.3 us (9%)
    ppermute x8, starting transfers between devices, shift(): lax.ppermute(value, axis, [(s, (s + steps) % count) for s in range(count)])  33.6 us
    all_to_all x1, blocking collectives, per_device(): parts = lax.all_to_all(terms, ('x', 'y', 'core'), 0, 0, tiled=True)  28.6 us
    all_to_all x1, blocking collectives, per_device(): parts = lax.all_to_all(terms, 'x', 0, 0, tiled=True)  17 us
    ppermute x8, waiting for transfers between devices, shift(): lax.ppermute(value, axis, [(s, (s + steps) % count) for s in range(count)])  14.4 us
    all_to_all x1, starting transfers between devices, per_device(): left = lax.all_to_all(sent, 'x', 0, 0, tiled=True)  4.99 us
    pallas_call x2, Pallas kernels, band_terms(): pl.pallas_call(functools.partial(band_kernel, last), out_shape=jax.ShapeD...  4.4 us
    pallas_call x1, Pallas kernels, prepare(): pl.pallas_call(prepare_kernel, out_shape=(jax.ShapeDtypeStruct((ROWS, BS)...  3.51 us
  transfers between devices with their start and end apart: 9, of which 4 were waited for; matrix products, arithmetic and copies ran while one was open for 1% of the time, Pallas kernels for 0%

profile of v6, /device:TPU:1, one launch (start us, length us, event | category | flops | bytes accessed | tf_op | source)
XLA Modules:
  0.0 110.4 jit_solution(5758357590088119044)
XLA Ops:
  0.0 3.5 %prepare.1 = (bf16[512,256]{1,0:T(8,128)(2,1)}, bf16[480,256]{1,0:T(8,128)(2,1)}, bf16[352,256]{1,0:T(8,128)(2,1)}, bf16[480,256]{1,0:T(8,128)(2,1)}, bf16[352,2...) custom-call(bf16[16,256,256]{2,1,0:T(8,128)(2,1)} %bitcast.10), custom_call_target="tpu_custom_call" | custom-call | tf_op jit(solution)/shard_map/prepare/pallas_call | solution.py:207
  3.5 0.0 copy-start.2
  3.5 0.0 copy-start.1
  3.5 0.0 copy-start
  3.5 5.0 %all-to-all-start = ((bf16[4,4,256,256]{3,2,1,0:T(8,128)(2,1)}), bf16[4,4,256,256]{3,2,1,0:T(8,128)(2,1)S(1)}, u32[]{:S(2)}, u32[]{:S(2)}) async-start(bf16[4,4,256,256]{3,2,1,0:T(8,128)(2,1)} %get-tuple-element.21), calls=%async_computation | async-start | bytes 4194304 | tf_op jit(solution)/shard_map/all_to_all | solution.py:251
  8.5 11.6 %collective-permute-start.1 = (bf16[352,256]{1,0:T(8,128)(2,1)}, bf16[352,256]{1,0:T(8,128)(2,1)S(1)}, u32[]{:S(2)}, u32[]{:S(2)}) collective-permute-start(bf16[352,256]{1,0:T(8,128)(2,1)} %get-tuple-element.18), channel_id=1, source_target_pairs={{0,448},{32,480},{64,0},{96,32},{128,64},{160,96},{192,128},{224,1... | collective-permute-start | bytes 540680 | tf_op jit(solution)/shard_map/ppermute | solution.py:29
  20.1 1.9 %collective-permute-start.3 = (bf16[352,256]{1,0:T(8,128)(2,1)}, bf16[352,256]{1,0:T(8,128)(2,1)S(1)}, u32[]{:S(2)}, u32[]{:S(2)}) collective-permute-start(bf16[352,256]{1,0:T(8,128)(2,1)} %get-tuple-element.20), channel_id=1, source_target_pairs={{0,64},{32,96},{64,128},{96,160},{128,192},{160,224},{192,256},{22... | collective-permute-start | bytes 540680 | tf_op jit(solution)/shard_map/ppermute | solution.py:29
  22.0 5.0 %collective-permute-start = (bf16[480,256]{1,0:T(8,128)(2,1)}, bf16[480,256]{1,0:T(8,128)(2,1)S(1)}, u32[]{:S(2)}, u32[]{:S(2)}) collective-permute-start(bf16[480,256]{1,0:T(8,128)(2,1)} %get-tuple-element.17), channel_id=1, source_target_pairs={{0,480},{32,0},{64,32},{96,64},{128,96},{160,128},{192,160},{224,1... | collective-permute-start | bytes 737288 | tf_op jit(solution)/shard_map/ppermute | solution.py:29
  27.1 0.0 copy-done.2
  27.1 1.9 %collective-permute-start.2 = (bf16[480,256]{1,0:T(8,128)(2,1)S(1)}, bf16[480,256]{1,0:T(8,128)(2,1)S(1)}, u32[]{:S(2)}, u32[]{:S(2)}) collective-permute-start(bf16[480,256]{1,0:T(8,128)(2,1)S(1)} %copy-done.2), channel_id=1, source_target_pairs={{0,32},{32,64},{64,96},{96,128},{128,160},{160,192},{192,224},{224... | collective-permute-start | bytes 737288 | tf_op jit(solution)/shard_map/ppermute | solution.py:29
  29.1 0.1 and_select_fusion
  29.1 0.1 add_select_fusion
  29.2 0.1 fusion.3
  29.3 0.0 copy-done.1
  29.3 0.1 copy.4
  29.4 0.6 gather_fusion
  30.0 0.3 compare_reduce_fusion
  30.3 0.0 collective-permute-done.1.up2
  30.3 0.0 collective-permute-done.3.down2
  30.3 2.3 %collective-permute-done.up1 = bf16[480,256]{1,0:T(8,128)(2,1)S(1)} collective-permute-done((bf16[480,256]{1,0:T(8,128)(2,1)}, bf16[480,256]{1,0:T(8,128)(2,1)S(1)}, u32[]{:S(2)}, u32[]{:S(2)}) %collective-permute-start) | collective-permute-done | bytes 245792 | tf_op jit(solution)/shard_map/ppermute | solution.py:29
  32.6 6.0 %collective-permute-done.2.down1 = bf16[480,256]{1,0:T(8,128)(2,1)S(1)} collective-permute-done((bf16[480,256]{1,0:T(8,128)(2,1)S(1)}, bf16[480,256]{1,0:T(8,128)(2,1)S(1)}, u32[]{:S(2)}, u32[]{:S(2)}) %collective-permute-start.2) | collective-permute-done | bytes 245792 | tf_op jit(solution)/shard_map/ppermute | solution.py:29
  38.7 0.0 all-to-all-done.left
  38.7 0.0 copy-done
  38.7 2.0 %square_terms.1 = bf16[4,512,256]{2,1,0:T(8,128)(2,1)S(1)} custom-call(s32[9,16]{1,0:T(8,128)S(1)} %convert_element_type.3.flags, bf16[512,256]{1,0:T(8,128)(2,1)S(1)} %copy-done, bf16[480,256]{1,0:T(8,128)(2,1)S(1)} %collective-permute-done.up1, bf16[352,256]{1,0:T(8,128)(2,1)S(1)} %collective-permute-done.1.up2, ...), custom_call_target="tpu_custom_call" | custom-call | flops 1073741824 | bytes 6291456 | tf_op jit(solution)/shard_map/square_terms/pallas_call | solution.py:89
  40.7 17.0 %all_to_all.15.parts = bf16[4,512,256]{2,1,0:T(8,128)(2,1)S(1)} all-to-all(bf16[4,512,256]{2,1,0:T(8,128)(2,1)S(1)} %square_terms.1), channel_id=1, replica_groups=mesh['z'=16,'x'=4,'y'=4,'core'=2] {'x'}, dimensions={0} | all-to-all | bytes 2097152 | tf_op jit(solution)/shard_map/all_to_all | solution.py:262
  57.7 0.8 gather_square.1
  58.5 5.1 %collective-permute-start.4 = (bf16[480,256]{1,0:T(8,128)(2,1)S(1)}, bf16[480,256]{1,0:T(8,128)(2,1)S(1)}, u32[]{:S(2)}, u32[]{:S(2)}) collective-permute-start(bf16[480,256]{1,0:T(8,128)(2,1)S(1)} %get-tuple-element.23), channel_id=1, source_target_pairs={{0,480},{32,0},{64,32},{96,64},{128,96},{160,128},{192,160},{224,1... | collective-permute-start | bytes 737288 | tf_op jit(solution)/shard_map/ppermute | solution.py:29
  63.6 1.9 %collective-permute-start.6 = (bf16[480,256]{1,0:T(8,128)(2,1)S(1)}, bf16[480,256]{1,0:T(8,128)(2,1)S(1)}, u32[]{:S(2)}, u32[]{:S(2)}) collective-permute-start(bf16[480,256]{1,0:T(8,128)(2,1)S(1)} %get-tuple-element.25), channel_id=1, source_target_pairs={{0,32},{32,64},{64,96},{96,128},{128,160},{160,192},{192,224},{224... | collective-permute-start | bytes 737288 | tf_op jit(solution)/shard_map/ppermute | solution.py:29
  65.5 3.8 %collective-permute-start.5 = (bf16[352,256]{1,0:T(8,128)(2,1)S(1)}, bf16[352,256]{1,0:T(8,128)(2,1)S(1)}, u32[]{:S(2)}, u32[]{:S(2)}) collective-permute-start(bf16[352,256]{1,0:T(8,128)(2,1)S(1)} %get-tuple-element.24), channel_id=1, source_target_pairs={{0,448},{32,480},{64,0},{96,32},{128,64},{160,96},{192,128},{224,1... | collective-permute-start | bytes 540680 | tf_op jit(solution)/shard_map/ppermute | solution.py:29
  69.4 2.4 %collective-permute-start.7 = (bf16[352,256]{1,0:T(8,128)(2,1)S(1)}, bf16[352,256]{1,0:T(8,128)(2,1)S(1)}, u32[]{:S(2)}, u32[]{:S(2)}) collective-permute-start(bf16[352,256]{1,0:T(8,128)(2,1)S(1)} %get-tuple-element.26), channel_id=1, source_target_pairs={{0,64},{32,96},{64,128},{96,160},{128,192},{160,224},{192,256},{22... | collective-permute-start | bytes 540680 | tf_op jit(solution)/shard_map/ppermute | solution.py:29
  71.7 2.9 %collective-permute-done.5.up2 = bf16[352,256]{1,0:T(8,128)(2,1)S(1)} collective-permute-done((bf16[352,256]{1,0:T(8,128)(2,1)S(1)}, bf16[352,256]{1,0:T(8,128)(2,1)S(1)}, u32[]{:S(2)}, u32[]{:S(2)}) %collective-permute-start.5) | collective-permute-done | bytes 180256 | tf_op jit(solution)/shard_map/ppermute | solution.py:29
  74.7 3.2 %collective-permute-done.7.down2 = bf16[352,256]{1,0:T(8,128)(2,1)S(1)} collective-permute-done((bf16[352,256]{1,0:T(8,128)(2,1)S(1)}, bf16[352,256]{1,0:T(8,128)(2,1)S(1)}, u32[]{:S(2)}, u32[]{:S(2)}) %collective-permute-start.7) | collective-permute-done | bytes 180256 | tf_op jit(solution)/shard_map/ppermute | solution.py:29
  77.8 0.0 collective-permute-done.4.up1
  77.8 0.0 collective-permute-done.6.down1
  77.9 2.4 %cube_terms.1 = bf16[32,128,128]{2,1,0:T(8,128)(2,1)S(1)} custom-call(s32[9,16]{1,0:T(8,128)S(1)} %convert_element_type.3.flags, bf16[512,256]{1,0:T(8,128)(2,1)S(1)} %get-tuple-element.22.own, bf16[480,256]{1,0:T(8,128)(2,1)S(1)} %collective-permute-done.4.up1, bf16[352,256]{1,0:T(8,128)(2,1)S(1)} %collective-permute-done.5.up2, ...), custom_call_target="tpu_custom_call" | custom-call | flops 1073741824 | bytes 6291456 | tf_op jit(solution)/shard_map/cube_terms/pallas_call | solution.py:89
  80.2 28.6 %all_to_all.16 = bf16[32,128,128]{2,1,0:T(8,128)(2,1)S(1)} all-to-all(bf16[32,128,128]{2,1,0:T(8,128)(2,1)S(1)} %cube_terms.1), channel_id=1, replica_groups=mesh['z'=16,'x'=4,'y'=4,'core'=2] {'x','y','core'}, dimensions={0} | all-to-all | bytes 2097152 | tf_op jit(solution)/shard_map/all_to_all | solution.py:265
  108.8 1.6 %finish.1 = f32[4,4,32,256]{3,2,1,0:T(8,128)} custom-call(s32[9,16]{1,0:T(8,128)S(1)} %convert_element_type.3.flags, bf16[4,8,128,128]{3,2,1,0:T(8,128)(2,1)S(1)} %bitcast.9), custom_call_target="tpu_custom_call" | custom-call | tf_op jit(solution)/shard_map/finish/pallas_call | solution.py:121
  (6 shorter events, 0.0 us)
Async XLA Ops:
  3.5 23.6 %copy-start.2 = (bf16[480,256]{1,0:T(8,128)(2,1)S(1)}, bf16[480,256]{1,0:T(8,128)(2,1)}, u32[]{:S(2)}) copy-start(bf16[480,256]{1,0:T(8,128)(2,1)} %get-tuple-element.19) | copy-start | bytes 737284
  3.5 25.8 %copy-start.1 = (s32[64,16]{0,1:T(8,128)S(1)}, s32[64,16]{0,1:T(8,128)}, u32[]{:S(2)}) copy-start(s32[64,16]{0,1:T(8,128)} %param.3) | copy-start | bytes 12292
  3.5 35.1 %copy-start = (bf16[512,256]{1,0:T(8,128)(2,1)S(1)}, bf16[512,256]{1,0:T(8,128)(2,1)}, u32[]{:S(2)}) copy-start(bf16[512,256]{1,0:T(8,128)(2,1)} %get-tuple-element.16.own) | copy-start | bytes 786436
  3.5 35.1 %all-to-all-start = ((bf16[4,4,256,256]{3,2,1,0:T(8,128)(2,1)}), bf16[4,4,256,256]{3,2,1,0:T(8,128)(2,1)S(1)}, u32[]{:S(2)}, u32[]{:S(2)}) async-start(bf16[4,4,256,256]{3,2,1,0:T(8,128)(2,1)} %get-tuple-element.21), calls=%async_computation | async-start | bytes 4194304 | tf_op jit(solution)/shard_map/all_to_all | solution.py:251
  8.5 21.8 %collective-permute-start.1 = (bf16[352,256]{1,0:T(8,128)(2,1)}, bf16[352,256]{1,0:T(8,128)(2,1)S(1)}, u32[]{:S(2)}, u32[]{:S(2)}) collective-permute-start(bf16[352,256]{1,0:T(8,128)(2,1)} %get-tuple-element.18), channel_id=1, source_target_pairs={{0,448},{32,480},{64,0},{96,32},{128,64},{160,96},{192,128},{224,1... | collective-permute-start | bytes 540680 | tf_op jit(solution)/shard_map/ppermute | solution.py:29
  20.1 10.2 %collective-permute-start.3 = (bf16[352,256]{1,0:T(8,128)(2,1)}, bf16[352,256]{1,0:T(8,128)(2,1)S(1)}, u32[]{:S(2)}, u32[]{:S(2)}) collective-permute-start(bf16[352,256]{1,0:T(8,128)(2,1)} %get-tuple-element.20), channel_id=1, source_target_pairs={{0,64},{32,96},{64,128},{96,160},{128,192},{160,224},{192,256},{22... | collective-permute-start | bytes 540680 | tf_op jit(solution)/shard_map/ppermute | solution.py:29
  22.0 10.6 %collective-permute-start = (bf16[480,256]{1,0:T(8,128)(2,1)}, bf16[480,256]{1,0:T(8,128)(2,1)S(1)}, u32[]{:S(2)}, u32[]{:S(2)}) collective-permute-start(bf16[480,256]{1,0:T(8,128)(2,1)} %get-tuple-element.17), channel_id=1, source_target_pairs={{0,480},{32,0},{64,32},{96,64},{128,96},{160,128},{192,160},{224,1... | collective-permute-start | bytes 737288 | tf_op jit(solution)/shard_map/ppermute | solution.py:29
  27.1 11.6 %collective-permute-start.2 = (bf16[480,256]{1,0:T(8,128)(2,1)S(1)}, bf16[480,256]{1,0:T(8,128)(2,1)S(1)}, u32[]{:S(2)}, u32[]{:S(2)}) collective-permute-start(bf16[480,256]{1,0:T(8,128)(2,1)S(1)} %copy-done.2), channel_id=1, source_target_pairs={{0,32},{32,64},{64,96},{96,128},{128,160},{160,192},{192,224},{224... | collective-permute-start | bytes 737288 | tf_op jit(solution)/shard_map/ppermute | solution.py:29
  58.5 19.3 %collective-permute-start.4 = (bf16[480,256]{1,0:T(8,128)(2,1)S(1)}, bf16[480,256]{1,0:T(8,128)(2,1)S(1)}, u32[]{:S(2)}, u32[]{:S(2)}) collective-permute-start(bf16[480,256]{1,0:T(8,128)(2,1)S(1)} %get-tuple-element.23), channel_id=1, source_target_pairs={{0,480},{32,0},{64,32},{96,64},{128,96},{160,128},{192,160},{224,1... | collective-permute-start | bytes 737288 | tf_op jit(solution)/shard_map/ppermute | solution.py:29
  63.6 14.2 %collective-permute-start.6 = (bf16[480,256]{1,0:T(8,128)(2,1)S(1)}, bf16[480,256]{1,0:T(8,128)(2,1)S(1)}, u32[]{:S(2)}, u32[]{:S(2)}) collective-permute-start(bf16[480,256]{1,0:T(8,128)(2,1)S(1)} %get-tuple-element.25), channel_id=1, source_target_pairs={{0,32},{32,64},{64,96},{96,128},{128,160},{160,192},{192,224},{224... | collective-permute-start | bytes 737288 | tf_op jit(solution)/shard_map/ppermute | solution.py:29
  65.5 9.1 %collective-permute-start.5 = (bf16[352,256]{1,0:T(8,128)(2,1)S(1)}, bf16[352,256]{1,0:T(8,128)(2,1)S(1)}, u32[]{:S(2)}, u32[]{:S(2)}) collective-permute-start(bf16[352,256]{1,0:T(8,128)(2,1)S(1)} %get-tuple-element.24), channel_id=1, source_target_pairs={{0,448},{32,480},{64,0},{96,32},{128,64},{160,96},{192,128},{224,1... | collective-permute-start | bytes 540680 | tf_op jit(solution)/shard_map/ppermute | solution.py:29
  69.4 8.5 %collective-permute-start.7 = (bf16[352,256]{1,0:T(8,128)(2,1)S(1)}, bf16[352,256]{1,0:T(8,128)(2,1)S(1)}, u32[]{:S(2)}, u32[]{:S(2)}) collective-permute-start(bf16[352,256]{1,0:T(8,128)(2,1)S(1)} %get-tuple-element.26), channel_id=1, source_target_pairs={{0,64},{32,96},{64,128},{96,160},{128,192},{160,224},{192,256},{22... | collective-permute-start | bytes 540680 | tf_op jit(solution)/shard_map/ppermute | solution.py:29
